TPU v7x, 32 devices: a whole 2x2x4 slice. The times are simulated.
32 devices in a mesh: row: 4 (over z), col: 8 (over y, x, core).
Axes of the slice: x: 2, y: 2, z: 4, core: 2. Of those that a mesh axis runs over, the one named last changes fastest.
Arguments:
- a_panels: float32 [4096, 2048], P('row', 'col'), may hold values from -6 to 6
- b_panels: float32 [2048, 16384], P('row', 'col'), may hold values from -0.1875 to 0.1875
- a_occupancy: int32 [32, 16], P('row', 'col'), may hold values 0 or 1
- b_occupancy: int32 [16, 128], P('row', 'col'), may hold values 0 or 1
- owner_device: int32 [4, 8, 128, 1], P('row', 'col'), may hold values from 0 to 31; in each aligned block of 128 rows (0 to 127, 128 to 255, ..., all dimensions but the last counted through in order) at most 8 rows name the same one
- owner_block: int32 [4, 8, 128], P('row', 'col'), may hold values from 0 to 127
- c_previous: float32 [4, 8, 128, 128, 128], P('row', 'col'), may hold values from -6 to 6
Outputs:
- c_owned: float32 [4, 8, 128, 128, 128], P('row', 'col')
Inputs may be any that keep to these rules, and one draw needn't show every extreme that they name: `owner_device`: among the 128 product blocks of one device, at most 8 name the same owner; some owner is named exactly 8 times by one device.
All inputs are finite; a program needn't handle non-finite values. No bound on the sum of `a_occupancy` or of `b_occupancy` on one device may be relied on, other than what follows from the above.
Results may differ from a plain program's by a relative error of at most 0.0003.
Values sent between devices are 32-bit elements; how exact they have to be, the bound alone decides.
No kernel may reach another device: no remote copies, remote signals or barrier semaphores. Data moves between devices by JAX's collectives and lax.ppermute only.
A program may use at most 192 MiB of HBM per device.

v0:
```python
import jax
import jax.numpy as jnp
from jax import lax
from jax.sharding import PartitionSpec as P

BLK = 128
TICKS = 4


def shifted(value, axis, steps):
    count = lax.axis_size(axis)
    pairs = [(source, (source + steps) % count) for source in range(count)]
    return lax.ppermute(value, axis, pairs)


def widen(occupancy, panel):
    return panel * jnp.repeat(jnp.repeat(occupancy.astype(jnp.float32), BLK, axis=0), BLK, axis=1)


def multiply(left, right):
    return jnp.dot(left, right, preferred_element_type=jnp.float32, precision=lax.Precision.HIGHEST)


def pick_image(held, tick, n_row, n_col):
    images = n_col // n_row
    inner = held.shape[0] // images
    slot = (lax.axis_index("row") + lax.axis_index("col") + tick) % n_col // n_row
    return lax.dynamic_slice_in_dim(held, slot * inner, inner, 0)


def per_device(a_panels, b_panels, a_occupancy, b_occupancy, owner_device, owner_block, c_previous):
    n_row = lax.axis_size("row")
    n_col = lax.axis_size("col")
    left = widen(a_occupancy, a_panels)
    right = widen(b_occupancy, b_panels)
    acc = jnp.zeros((left.shape[0], right.shape[1]), jnp.float32)
    for tick in range(TICKS):
        acc = acc + multiply(left, pick_image(right, tick, n_row, n_col))
        if tick + 1 < TICKS:
            left = shifted(left, "col", -1)
            right = shifted(right, "row", -1)
    rows_blocks = left.shape[0] // BLK
    cols_blocks = right.shape[1] // BLK
    count_blocks = rows_blocks * cols_blocks
    pieces = (
        acc.reshape(rows_blocks, BLK, cols_blocks, BLK)
        .transpose(0, 2, 1, 3)
        .reshape(count_blocks, BLK, BLK)
    )
    devices_all = n_row * n_col
    capacity = max(2, (2 * count_blocks + devices_all - 1) // devices_all)
    owners = owner_device.reshape(count_blocks)
    targets = owner_block.reshape(count_blocks)
    onehot = (owners[:, None] == jnp.arange(devices_all, dtype=jnp.int32)[None, :]).astype(
        jnp.int32
    )
    earlier = jnp.cumsum(onehot, axis=0) - onehot
    ranks = jnp.sum(earlier * onehot, axis=1)
    places = owners * capacity + ranks
    send_blocks = jnp.zeros((devices_all * capacity, BLK, BLK), jnp.float32).at[places].set(pieces)
    send_targets = (
        jnp.full((devices_all * capacity,), -1.0, jnp.float32)
        .at[places]
        .set(targets.astype(jnp.float32))
    )
    got_blocks, got_targets = (
        lax.all_to_all(
            send_blocks.reshape(devices_all, capacity, BLK, BLK),
            ("row", "col"),
            split_axis=0,
            concat_axis=0,
            tiled=True,
        ),
        lax.all_to_all(
            send_targets.reshape(devices_all, capacity),
            ("row", "col"),
            split_axis=0,
            concat_axis=0,
            tiled=True,
        ),
    )
    flat_blocks = got_blocks.reshape(devices_all * capacity, BLK * BLK)
    flat_targets = got_targets.reshape(devices_all * capacity)
    owned = c_previous.shape[2]
    select = (jnp.arange(owned, dtype=jnp.float32)[:, None] == flat_targets[None, :]).astype(
        jnp.float32
    )
    added = jnp.dot(
        select, flat_blocks, preferred_element_type=jnp.float32, precision=lax.Precision.HIGHEST
    )
    result = c_previous.reshape(owned, BLK * BLK) + added
    return result.reshape(c_previous.shape)


def solution(mesh):
    in_specs = (
        P("row", "col"),
        P("row", "col"),
        P("row", "col"),
        P("row", "col"),
        P("row", "col", None, None),
        P("row", "col", None),
        P("row", "col", None, None, None),
    )
    out_specs = P("row", "col", None, None, None)
    return jax.shard_map(
        per_device, mesh=mesh, in_specs=in_specs, out_specs=out_specs, check_vma=False
    )
```

profile of v0, /device:TPU:0, one launch (start us, length us, event | category | flops | bytes accessed | tf_op | source)
XLA Modules:
  0.0 763.3 jit_solution(1701607022832837629)
XLA Ops:
  0.0 0.7 convert_element_type.20
  0.7 0.0 copy-start.4
  0.7 1.1 broadcast_in_dim.27
  1.9 0.0 copy-start.1
  1.9 0.0 copy-start.3
  1.9 0.0 copy-start.5
  1.9 4.5 bitcast_multiply_fusion
  6.4 0.0 copy-start
  6.5 2.0 copy-done
  8.5 5.0 collective-permute-start.1
  13.5 89.8 %collective-permute-done.1 = f32[512,2048]{1,0:T(8,128)S(1)} collective-permute-done((f32[512,2048]{1,0:T(8,128)S(1)}, f32[512,2048]{1,0:T(8,128)S(1)}, u32[]{:S(2)}, u32[]{:S(2)}) %collective-permute-start.1) | collective-permute-done | bytes 4194336 | tf_op jit(solution)/shard_map/ppermute | solution.py:13
  103.3 1.9 copy-done.2
  105.3 4.3 collective-permute-start.3
  109.6 89.0 %collective-permute-done.3 = f32[512,2048]{1,0:T(8,128)} collective-permute-done((f32[512,2048]{1,0:T(8,128)S(1)}, f32[512,2048]{1,0:T(8,128)}, u32[]{:S(2)}, u32[]{:S(2)}) %collective-permute-start.3) | collective-permute-done | bytes 4194336 | tf_op jit(solution)/shard_map/ppermute | solution.py:13
  198.5 4.4 collective-permute-start.5
  202.9 0.1 copy.12
  203.0 1.2 broadcast_in_dim.25
  204.3 0.1 bitcast_multiply_fusion.1
  204.4 0.1 collective-permute-start
  204.5 12.3 %collective-permute-done = f32[1024,256]{1,0:T(8,128)S(1)} collective-permute-done((f32[1024,256]{1,0:T(8,128)S(1)}, f32[1024,256]{1,0:T(8,128)S(1)}, u32[]{:S(2)}, u32[]{:S(2)}) %collective-permute-start) | collective-permute-done | bytes 1048608 | tf_op jit(solution)/shard_map/ppermute | solution.py:13
  216.8 2.8 collective-permute-start.2
  219.6 0.1 fusion.13
  219.7 0.2 reduce_window_sum.11
  219.9 0.2 select_reduce_fusion
  220.1 1.0 scatter_custom_fusion
  221.1 0.7 all_to_all.9
  221.8 3.1 all-to-all-start
  224.9 7.0 collective-permute-done.2
  231.9 3.4 collective-permute-start.4
  235.4 10.2 %fusion.10 = f32[1024,2048]{1,0:T(8,128)} fusion(f32[1024,256]{1,0:T(8,128)S(1)} %bitcast_multiply_fusion.1, f32[512,2048]{1,0:T(8,128)} %copy-done, s32[]{:T(128)S(6)} %select_n.58), kind=kOutput, calls=%fused_computation.13 | convolution fusion | flops 6442450944 | bytes 11534340 | tf_op jit(solution)/shard_map/dot_general | solution.py:21
  245.6 9.2 %fusion.8 = f32[1024,2048]{1,0:T(8,128)S(1)} fusion(f32[1024,256]{1,0:T(8,128)S(1)} %collective-permute-done, f32[512,2048]{1,0:T(8,128)} %copy-done.2, s32[]{:T(128)S(6)} %select_n.61), kind=kOutput, calls=%fused_computation.11 | convolution fusion | flops 6442450944 | bytes 11534340 | tf_op jit(solution)/shard_map/dot_general | solution.py:21
  254.8 0.0 slice-start.1
  254.8 10.9 %fusion.6 = f32[1024,2048]{1,0:T(8,128)} fusion(f32[1024,256]{1,0:T(8,128)} %collective-permute-done.2, f32[512,2048]{1,0:T(8,128)} %collective-permute-done.3, s32[]{:T(128)S(6)} %select_n.64), kind=kOutput, calls=%fused_computation.9 | convolution fusion | flops 6442450944 | bytes 11534340 | tf_op jit(solution)/shard_map/dot_general | solution.py:21
  265.7 0.0 collective-permute-done.4
  265.7 25.7 %collective-permute-done.5 = f32[512,2048]{1,0:T(8,128)} collective-permute-done((f32[512,2048]{1,0:T(8,128)}, f32[512,2048]{1,0:T(8,128)}, u32[]{:S(2)}, u32[]{:S(2)}) %collective-permute-start.5) | collective-permute-done | bytes 4194336 | tf_op jit(solution)/shard_map/ppermute | solution.py:13
  291.4 13.8 %add_bitcast_fusion = f32[128,8,16,128]{3,1,2,0:T(8,128)} fusion(f32[1024,2048]{1,0:T(8,128)} %fusion.6, f32[1024,2048]{1,0:T(8,128)S(1)} %bitcast.51, f32[1024,2048]{1,0:T(8,128)S(1)} %fusion.8, f32[1024,256]{1,0:T(8,128)} %collective-permute-done.4, f32[512,2048]{1,0:T(8,128)} %collective-permute-done.5, s32[]{:T(128)S(6)} %select_n.67), kind=kOutput, calls=%fused_computation.5 | convolution fusion | flops 6448742400 | bytes 36700164 | tf_op jit(solution)/shard_map/dot_general | solution.py:21
  305.2 5.4 copy.17
  310.6 5.9 copy.13
  316.5 7.9 %broadcast_in_dim.23 = f32[256,128,128]{2,1,0:T(8,128)} broadcast(f32[]{:T(128)} %constant.79.clone.1), dimensions={} | broadcast | bytes 16777220 | tf_op jit(solution)/shard_map/broadcast_in_dim | solution.py:60
  324.4 23.4 %scatter_fusion = f32[256,128,128]{2,1,0:T(8,128)} fusion(f32[256,128,128]{2,1,0:T(8,128)} %broadcast_in_dim.23, s32[128]{0:T(128)S(1)} %fusion.18, f32[128,128,128]{2,1,0:T(8,128)} %bitcast.52), kind=kCustom, calls=%fused_computation.1 | custom fusion | bytes 25166336 | tf_op jit(solution)/shard_map/scatter | solution.py:60
  347.8 0.0 all-to-all-done
  347.8 6.9 all-to-all-start.1
  354.7 0.5 broadcast.49
  355.2 1.4 reduce.3
  356.6 0.1 eq.40
  356.7 370.6 %all-to-all-done.1 = f32[32,8,128,128]{3,2,1,0:T(8,128)} async-done(((f32[32,8,128,128]{3,2,1,0:T(8,128)}), f32[32,8,128,128]{3,2,1,0:T(8,128)}, u32[]{:S(2)}, u32[]{:S(2)}) %all-to-all-start.1) | async-done | bytes 16777248 | tf_op jit(solution)/shard_map/all_to_all | solution.py:67
  727.3 27.5 %fusion.2 = f32[16,8,128,128]{3,1,2,0:T(8,128)} fusion(f32[32,8,128,128]{3,2,1,0:T(8,128)} %all-to-all-done.1, f32[16,8,128,128]{3,2,1,0:T(8,128)} %bitcast.55, f32[256]{0:T(256)S(1)} %eq.40), kind=kOutput, calls=%fused_computation.7 | convolution fusion | flops 6444580864 | bytes 33555456 | tf_op jit(solution)/shard_map/dot_general | solution.py:88
  754.8 8.2 %copy.19 = f32[16,8,128,128]{3,2,1,0:T(8,128)} copy(f32[16,8,128,128]{3,1,2,0:T(8,128)} %fusion.2) | data formatting | bytes 16777216
  (14 shorter events, 0.1 us)
Async XLA Ops:
  0.7 202.2 %copy-start.4 = (s32[8,2]{0,1:T(2,128)S(1)}, s32[8,2]{0,1:T(2,128)}, u32[]{:S(2)}) copy-start(s32[8,2]{0,1:T(2,128)} %param.9) | copy-start | bytes 196
  1.9 202.4 %copy-start.1 = (f32[1024,256]{1,0:T(8,128)S(1)}, f32[1024,256]{1,0:T(8,128)}, u32[]{:S(2)}) copy-start(f32[1024,256]{1,0:T(8,128)} %param.7) | copy-start | bytes 3145732
  1.9 217.7 %copy-start.3 = (s32[1,1,128,1]{2,3,1,0:T(1,128)S(1)}, s32[1,1,128,1]{2,3,1,0:T(1,128)}, u32[]{:S(2)}) copy-start(s32[1,1,128,1]{2,3,1,0:T(1,128)} %param.11) | copy-start | bytes 1540
  1.9 218.2 %copy-start.5 = (s32[1,1,128]{2,1,0:T(1,128)S(1)}, s32[1,1,128]{2,1,0:T(1,128)}, u32[]{:S(2)}) copy-start(s32[1,1,128]{2,1,0:T(1,128)} %param.12) | copy-start | bytes 1540
  6.4 2.0 copy-start
  8.5 94.9 %collective-permute-start.1 = (f32[512,2048]{1,0:T(8,128)S(1)}, f32[512,2048]{1,0:T(8,128)S(1)}, u32[]{:S(2)}, u32[]{:S(2)}) collective-permute-start(f32[512,2048]{1,0:T(8,128)S(1)} %bitcast_multiply_fusion), channel_id=1, source_target_pairs={{0,24},{8,0},{16,8},{24,16},{1,25},{9,1},{17,9},{25,17},{2,26},{10... | collective-permute-start | bytes 12582920 | tf_op jit(solution)/shard_map/ppermute | solution.py:13
  103.3 1.9 copy-start.2
  105.3 93.2 %collective-permute-start.3 = (f32[512,2048]{1,0:T(8,128)S(1)}, f32[512,2048]{1,0:T(8,128)}, u32[]{:S(2)}, u32[]{:S(2)}) collective-permute-start(f32[512,2048]{1,0:T(8,128)S(1)} %collective-permute-done.1), channel_id=1, source_target_pairs={{0,24},{8,0},{16,8},{24,16},{1,25},{9,1},{17,9},{25,17},{2,26},{10... | collective-permute-start | bytes 12582920 | tf_op jit(solution)/shard_map/ppermute | solution.py:13
  198.5 92.9 %collective-permute-start.5 = (f32[512,2048]{1,0:T(8,128)}, f32[512,2048]{1,0:T(8,128)}, u32[]{:S(2)}, u32[]{:S(2)}) collective-permute-start(f32[512,2048]{1,0:T(8,128)} %collective-permute-done.3), channel_id=1, source_target_pairs={{0,24},{8,0},{16,8},{24,16},{1,25},{9,1},{17,9},{25,17},{2,26},{10... | collective-permute-start | bytes 12582920 | tf_op jit(solution)/shard_map/ppermute | solution.py:13
  204.4 12.4 %collective-permute-start = (f32[1024,256]{1,0:T(8,128)S(1)}, f32[1024,256]{1,0:T(8,128)S(1)}, u32[]{:S(2)}, u32[]{:S(2)}) collective-permute-start(f32[1024,256]{1,0:T(8,128)S(1)} %bitcast_multiply_fusion.1), channel_id=1, source_target_pairs={{0,7},{1,0},{2,1},{3,2},{4,3},{5,4},{6,5},{7,6},{8,15},{9,8},{10,9... | collective-permute-start | bytes 3145736 | tf_op jit(solution)/shard_map/ppermute | solution.py:13
  216.8 15.1 %collective-permute-start.2 = (f32[1024,256]{1,0:T(8,128)S(1)}, f32[1024,256]{1,0:T(8,128)}, u32[]{:S(2)}, u32[]{:S(2)}) collective-permute-start(f32[1024,256]{1,0:T(8,128)S(1)} %collective-permute-done), channel_id=1, source_target_pairs={{0,7},{1,0},{2,1},{3,2},{4,3},{5,4},{6,5},{7,6},{8,15},{9,8},{10,9... | collective-permute-start | bytes 3145736 | tf_op jit(solution)/shard_map/ppermute | solution.py:13
  221.8 126.0 %all-to-all-start = ((f32[32,1,8]{2,1,0:T(1,128)}), f32[32,1,8]{2,1,0:T(1,128)}, u32[]{:S(2)}, u32[]{:S(2)}) async-start(f32[32,1,8]{2,1,0:T(1,128)} %bitcast.5), calls=%async_computation | async-start | bytes 32768 | tf_op jit(solution)/shard_map/all_to_all | solution.py:74
  231.9 33.8 %collective-permute-start.4 = (f32[1024,256]{1,0:T(8,128)}, f32[1024,256]{1,0:T(8,128)}, u32[]{:S(2)}, u32[]{:S(2)}) collective-permute-start(f32[1024,256]{1,0:T(8,128)} %collective-permute-done.2), channel_id=1, source_target_pairs={{0,7},{1,0},{2,1},{3,2},{4,3},{5,4},{6,5},{7,6},{8,15},{9,8},{10,9... | collective-permute-start | bytes 3145736 | tf_op jit(solution)/shard_map/ppermute | solution.py:13
  245.6 45.9 %slice-start = ((s8[8388608]{0:T(1024)(128)(4,1)}), s8[4194304]{0:T(1024)(128)(4,1)S(1)}, s32[]{:S(2)}) async-start(s8[8388608]{0:T(1024)(128)(4,1)} %bitcast.50), calls=%async_computation.2 | async-start | bytes 8388608
  254.8 36.6 %slice-start.1 = ((s8[8388608]{0:T(1024)(128)(4,1)}), s8[4194304]{0:T(1024)(128)(4,1)S(1)}, s32[]{:S(2)}) async-start(s8[8388608]{0:T(1024)(128)(4,1)} %bitcast.50), calls=%async_computation.3 | async-start | bytes 8388608
  347.8 379.5 %all-to-all-start.1 = ((f32[32,8,128,128]{3,2,1,0:T(8,128)}), f32[32,8,128,128]{3,2,1,0:T(8,128)}, u32[]{:S(2)}, u32[]{:S(2)}) async-start(f32[32,8,128,128]{3,2,1,0:T(8,128)} %bitcast.49), calls=%async_computation.1 | async-start | bytes 33554432 | tf_op jit(solution)/shard_map/all_to_all | solution.py:67
where the time goes:
time: 768 us; the launch traced here: 763 us
  waiting for transfers between devices  594 us (77%)
  matrix products  71.6 us (9%)
  local copies, waits for them, and re-layouts  59.5 us (8%)
  starting transfers between devices  30 us (4%)
    all_to_all x1, waiting for transfers between devices, per_device(): lax.all_to_all(send_blocks.reshape(devices_all, capacity, BLK, BLK), ('ro...  371 us
    ppermute x6, waiting for transfers between devices, shifted(): return lax.ppermute(value, axis, pairs)  224 us
    dot_general x4, matrix products, multiply(): jnp.dot(left, right, preferred_element_type=jnp.float32, precision=lax.Pr...  44.1 us
    dot_general x1, matrix products, per_device(): jnp.dot(select, flat_blocks, preferred_element_type=jnp.float32, precisio...  27.5 us
    scatter x1, local copies, waits for them, and re-layouts, per_device(): jnp.zeros((devices_all * capacity, BLK, BLK), jnp.float32).at[places]  23.4 us
    ppermute x6, starting transfers between devices, shifted(): return lax.ppermute(value, axis, pairs)  20 us
    unnamed x18, local copies, waits for them, and re-layouts  17.6 us
  transfers between devices with their start and end apart: 8, of which 6 were waited for; matrix products, arithmetic and copies ran while one was open for 12% of the time, Pallas kernels for 0%

commit v1 on v0

v1 whole, which is shorter than its diff:
```python
import functools

import jax
import jax.numpy as jnp
import numpy as np
from jax import lax
from jax.experimental import pallas as pl
from jax.experimental.pallas import tpu as pltpu
from jax.sharding import PartitionSpec as P

BLK = 128
TICKS = 4
VMEM_LIMIT = 48 * 1024 * 1024


def widen(occupancy, panel):
    return panel * jnp.repeat(jnp.repeat(occupancy.astype(jnp.float32), BLK, axis=0), BLK, axis=1)


def after(value, *others):
    return lax.optimization_barrier((value,) + others)[0]


def up_step(value, sources, step, n_row):
    pairs = [(b + step - 1, b + step) for b in sources if b + step < n_row]
    return lax.ppermute(value, "row", pairs) if pairs else None


def down_step(value, sources, step):
    pairs = [(b - step + 1, b - step) for b in sources if b - step >= 0]
    return lax.ppermute(value, "row", pairs) if pairs else None


def visit_order(n_row):
    return [sorted(range(n_row), key=lambda i: (abs(i - r), i < r)) for r in range(n_row)]


def image_key(row, inner, n_row):
    source, kind = inner % n_row, "XY"[inner // n_row]
    return (kind, source - row)


def split(value):
    high = value.astype(jnp.bfloat16)
    low = (value - high.astype(jnp.float32)).astype(jnp.bfloat16)
    return high, low


def product_kernel(place, choices, table, which, *refs):
    count = len(choices)
    lefts = refs[:TICKS]
    rights = refs[TICKS : TICKS + count]
    out = refs[TICKS + count]
    left_in, right_in, left_hi, left_lo, right_hi, right_lo, left_sem, right_sem = refs[TICKS + count + 1 :]
    inner = right_in.shape[1]
    q_blocks = right_in.shape[2] // BLK

    def left_copy(t):
        return pltpu.make_async_copy(lefts[t].at[place], left_in.at[t], left_sem.at[t])

    for t in range(TICKS):
        left_copy(t).start()
        for position, (ref, ticks) in enumerate(zip(rights, choices)):
            if t in ticks:

                @pl.when(which[t] == position)
                def _():
                    pltpu.make_async_copy(ref, right_in.at[t], right_sem.at[t]).start()

    for t in range(TICKS):
        left_copy(t).wait()
        pltpu.make_async_copy(rights[0], right_in.at[t], right_sem.at[t]).wait()
        cols = pl.ds(t * inner, inner)

        @pl.loop(0, left_in.shape[1] // BLK)
        def _(p):
            rows = pl.ds(pl.multiple_of(p * BLK, BLK), BLK)
            left_hi[rows, cols], left_lo[rows, cols] = split(left_in[t, rows, :])

        @pl.loop(0, inner // 32)
        def _(p):
            rows = pl.ds(pl.multiple_of(p * 32, 32), 32)
            to = pl.ds(pl.multiple_of(t * inner + p * 32, 32), 32)
            right_hi[to, :], right_lo[to, :] = split(right_in[t, rows, :])

    @pl.loop(0, out.shape[0])
    def _(slot):
        block = table[slot]

        @pl.when(block >= 0)
        def _():
            rows = pl.ds(pl.multiple_of((block // q_blocks) * BLK, BLK), BLK)
            cols = pl.ds(pl.multiple_of((block % q_blocks) * BLK, BLK), BLK)
            dot = functools.partial(jnp.dot, preferred_element_type=jnp.float32)
            high, low = left_hi[rows, :], right_lo[:, cols]
            small = dot(high, low)
            other = right_hi[:, cols]
            small = small + dot(left_lo[rows, :], other)
            out[slot] = small + dot(high, other)

        @pl.when(block < 0)
        def _():
            out[slot] = jnp.zeros((BLK, BLK), jnp.float32)


def products(table, which, lefts, rights, choices, place, slots):
    rows, inner = lefts[0].shape[1:]
    cols = rights[0].shape[1]
    smem = pl.BlockSpec(memory_space=pltpu.SMEM)
    hbm = pl.BlockSpec(memory_space=pl.ANY)
    deep = TICKS * inner
    return pl.pallas_call(
        functools.partial(product_kernel, place, choices),
        out_shape=jax.ShapeDtypeStruct((slots, BLK, BLK), jnp.float32),
        in_specs=[smem, smem] + [hbm] * (TICKS + len(rights)),
        out_specs=pl.BlockSpec(memory_space=pltpu.VMEM),
        scratch_shapes=[
            pltpu.VMEM((TICKS, rows, inner), jnp.float32),
            pltpu.VMEM((TICKS, inner, cols), jnp.float32),
            pltpu.VMEM((rows, deep), jnp.bfloat16),
            pltpu.VMEM((rows, deep), jnp.bfloat16),
            pltpu.VMEM((deep, cols), jnp.bfloat16),
            pltpu.VMEM((deep, cols), jnp.bfloat16),
            pltpu.SemaphoreType.DMA((TICKS,)),
            pltpu.SemaphoreType.DMA((TICKS,)),
        ],
        compiler_params=pltpu.CompilerParams(vmem_limit_bytes=VMEM_LIMIT),
        cost_estimate=pl.CostEstimate(
            flops=2 * 6 * slots * BLK * BLK * deep,
            bytes_accessed=4 * (deep * (rows + cols) + slots * BLK * BLK),
            transcendentals=0,
        ),
        name="products",
    )(table, which, *lefts, *rights)


def add_kernel(targets, got, start, out):
    out[...] = start[...]

    @pl.loop(0, got.shape[0])
    def _(slot):
        target = targets[slot]

        @pl.when(target >= 0)
        def _():
            out[target] = out[target] + got[slot]


def add_blocks(targets, got, start):
    vmem = pl.BlockSpec(memory_space=pltpu.VMEM)
    return pl.pallas_call(
        add_kernel,
        out_shape=jax.ShapeDtypeStruct(start.shape, jnp.float32),
        in_specs=[pl.BlockSpec(memory_space=pltpu.SMEM), vmem, vmem],
        out_specs=vmem,
        compiler_params=pltpu.CompilerParams(vmem_limit_bytes=VMEM_LIMIT),
        cost_estimate=pl.CostEstimate(
            flops=got.size, bytes_accessed=4 * (got.size + 2 * start.size), transcendentals=0
        ),
        name="add_blocks",
    )(targets, got, start)


def tables(owner_device, owner_block, n_row, n_col, capacity):
    row, col = lax.axis_index("row"), lax.axis_index("col")
    mine = jnp.stack([owner_device.reshape(-1), owner_block.reshape(-1)])
    every = lax.all_gather(mine, ("row", "col"))
    count = mine.shape[1]
    every = every.reshape(n_row, n_col, 2, count)
    places = jnp.arange(capacity, dtype=jnp.int32)

    def spread(match, values):
        rank = jnp.cumsum(match.astype(jnp.int32), axis=-1) - 1
        hit = match[..., None, :] & (rank[..., None, :] == places[:, None])
        return jnp.max(jnp.where(hit, values[..., None, :], -1), axis=-1)

    column = lax.dynamic_index_in_dim(every[:, :, 0], col, axis=1, keepdims=False)
    owners = row * n_col + jnp.arange(n_col, dtype=jnp.int32)
    numbers = jnp.arange(count, dtype=jnp.int32)
    sent = spread(
        column[:, None, :] == owners[None, :, None],
        jnp.broadcast_to(numbers, (n_row, n_col, count)),
    )
    got = spread(every[:, :, 0] == row * n_col + col, every[:, :, 1])
    return sent.reshape(n_row, n_col * capacity), got.reshape(n_row, n_col * capacity)


def per_device(a_panels, b_panels, a_occupancy, b_occupancy, owner_device, owner_block, c_previous):
    n_row = lax.axis_size("row")
    n_col = lax.axis_size("col")
    row, col = lax.axis_index("row"), lax.axis_index("col")
    images = n_col // n_row
    inner = b_panels.shape[0] // images
    count_blocks = owner_block.size
    capacity = max(2, (2 * count_blocks + n_row * n_col - 1) // (n_row * n_col))
    order = visit_order(n_row)

    left = widen(a_occupancy, a_panels)
    right = widen(b_occupancy, b_panels)

    def image(number):
        slot = (row + col + number * n_row) % n_col // n_row
        return lax.dynamic_slice_in_dim(right, slot * inner, inner, 0)

    held = {("X", 0): image(0), ("Y", 0): image(1)}
    panels = {0: left}
    every_row = list(range(n_row))
    early = list(range(TICKS - 1))

    sent, got = tables(owner_device, owner_block, n_row, n_col, capacity)
    for d in range(1, n_row):
        panels[-d] = up_step(panels[1 - d], every_row, d, n_row)
        panels[d] = down_step(panels[d - 1], every_row, d)
        held["Y", -d] = up_step(held["Y", 1 - d], early, d, n_row)
        held["X", d] = down_step(held["X", d - 1], every_row, d)
    gate = (held["Y", 2 - n_row], held["X", n_row - 2])
    later = {("X", 0): after(held["X", 0], *gate), ("Y", 0): after(held["Y", 0], *gate)}
    for d in range(1, n_row):
        held["X", -d] = later["X", -d] = up_step(later["X", 1 - d], every_row, d, n_row)
        if d < TICKS - 1:
            held["Y", d] = later["Y", d] = down_step(later["Y", d - 1], early, d)

    backward = [((c + 1) % n_col, c) for c in range(n_col)]

    def chosen(step):
        offsets = [order[r][step] - r for r in range(n_row)]
        kinds = sorted(set(offsets))
        index = jnp.asarray([kinds.index(o) for o in offsets], jnp.int32)[row]
        return lax.select_n(index, *[panels[k] for k in kinds]) if len(kinds) > 2 else lax.select_n(
            index == len(kinds) - 1, *[panels[k] for k in kinds]
        )

    first = [left[None]]
    rest = [jnp.stack([chosen(step) for step in range(1, n_row)])]
    for t in range(1, TICKS):
        first.append(lax.ppermute(first[-1], "col", backward))
    for t in range(1, TICKS):
        rest.append(lax.ppermute(rest[-1], "col", backward))

    total = c_previous.reshape(c_previous.shape[2:])
    for step in range(n_row):
        keys = [[image_key(r, order[r][step] + t, n_row) for t in range(TICKS)] for r in range(n_row)]
        names = sorted({key for of_row in keys for key in of_row})
        choices = [{t for r in range(n_row) for t in range(TICKS) if keys[r][t] == name} for name in names]
        which = jnp.asarray([[names.index(key) for key in of_row] for of_row in keys], jnp.int32)[row]
        visit = jnp.asarray([order[r][step] for r in range(n_row)], jnp.int32)[row]
        blocks = products(
            sent[visit],
            which,
            first if step == 0 else rest,
            [held[name] for name in names],
            choices,
            0 if step == 0 else step - 1,
            n_col * capacity,
        )
        arrived = lax.all_to_all(blocks, "col", split_axis=0, concat_axis=0, tiled=True)
        total = add_blocks(got[visit], arrived, total)
    return total.reshape(c_previous.shape)


def solution(mesh):
    in_specs = (
        P("row", "col"),
        P("row", "col"),
        P("row", "col"),
        P("row", "col"),
        P("row", "col", None, None),
        P("row", "col", None),
        P("row", "col", None, None, None),
    )
    out_specs = P("row", "col", None, None, None)
    return jax.shard_map(
        per_device, mesh=mesh, in_specs=in_specs, out_specs=out_specs, check_vma=False
    )
```

time: 768 us -> 586 us (0.76)
  waiting for transfers between devices: 594 us -> 296 us
  Pallas kernels: 0 us -> 122 us
  blocking collectives: 0 us -> 73.9 us
  matrix products: 71.6 us -> 0 us
  local copies, waits for them, and re-layouts: 59.5 us -> 15.8 us
  starting transfers between devices: 30 us -> 58.3 us
  between operations: 0.49 us -> 9.85 us
    all_to_all x2 -> x4, waiting for transfers between devices: 371 us -> 45.9 us  [per_device(): lax.all_to_all(blocks, 'col', split_axis=0, concat_axis=0, tiled=True)]
    pallas_call x0 -> x8, Pallas kernels: none -> 122 us  [the longest x4 83.8 us: products(): pl.pallas_call(functools.partial(product_kernel, place, choices), out_sha...]
    all_gather x0 -> x1, blocking collectives: none -> 73.9 us  [tables(): every = lax.all_gather(mine, ('row', 'col'))]
    dot_general x5 -> x0, matrix products: 71.6 us -> none  [the longest x4 44.1 us: multiply(): jnp.dot(left, right, preferred_element_type=jnp.float32, precision=lax.Pr...]
    ppermute x6 -> x23, waiting for transfers between devices: 224 us -> 250 us  [the longest x8 228 us: down_step(): return lax.ppermute(value, 'row', pairs) if pairs else None]
    scatter x2 -> x0, local copies, waits for them, and re-layouts: 24.4 us -> none  [the longest x1 23.4 us: per_device(): jnp.zeros((devices_all * capacity, BLK, BLK), jnp.float32).at[places]]
    ppermute x6 -> x23, starting transfers between devices: 20 us -> 37.2 us  [the longest x9 21.9 us: up_step(): return lax.ppermute(value, 'row', pairs) if pairs else None]
    unnamed x18 -> x52, local copies, waits for them, and re-layouts: 17.6 us -> 6.28 us
  transfers between devices with their start and end apart: 8 -> 27, of which waited for: 6 -> 11; matrix products, arithmetic and copies ran while one was open for 12% -> 2% of each run, Pallas kernels for 0% -> 19%
where the time goes in v1:
time: 586 us
  waiting for transfers between devices  296 us (51%)
  Pallas kernels  122 us (21%)
  blocking collectives  73.9 us (13%)
  starting transfers between devices  58.3 us (10%)
  local copies, waits for them, and re-layouts  15.8 us (3%)
  other arithmetic  10.3 us (2%)
  between operations  9.85 us (2%)
    ppermute x8, waiting for transfers between devices, down_step(): return lax.ppermute(value, 'row', pairs) if pairs else None  228 us
    pallas_call x4, Pallas kernels, products(): pl.pallas_call(functools.partial(product_kernel, place, choices), out_sha...  83.8 us
    all_gather x1, blocking collectives, tables(): every = lax.all_gather(mine, ('row', 'col'))  73.9 us
    all_to_all x4, waiting for transfers between devices, per_device(): lax.all_to_all(blocks, 'col', split_axis=0, concat_axis=0, tiled=True)  45.9 us
    pallas_call x4, Pallas kernels, add_blocks(): pl.pallas_call(add_kernel, out_shape=jax.ShapeDtypeStruct(start.shape, jn...  38.3 us
    ppermute x9, starting transfers between devices, up_step(): return lax.ppermute(value, 'row', pairs) if pairs else None  21.9 us
    all_to_all x4, starting transfers between devices, per_device(): lax.all_to_all(blocks, 'col', split_axis=0, concat_axis=0, tiled=True)  21.1 us
  transfers between devices with their start and end apart: 27, of which 11 were waited for; matrix products, arithmetic and copies ran while one was open for 2% of the time, Pallas kernels for 19%

profile of v1, /device:TPU:0, one launch (start us, length us, event | category | flops | bytes accessed | tf_op | source)
XLA Modules:
  0.0 586.5 jit_solution(9454808768107801910)
XLA Ops:
  0.9 1.2 broadcast_in_dim.46
  2.1 1.4 bitcast_multiply_fusion.1
  3.5 1.3 collective-permute-start
  4.8 5.6 collective-permute-start.1
  10.4 21.2 %collective-permute-done = f32[1024,256]{1,0:T(8,128)S(1)} collective-permute-done((f32[1024,256]{1,0:T(8,128)S(1)}, f32[1024,256]{1,0:T(8,128)S(1)}, u32[]{:S(2)}, u32[]{:S(2)}) %collective-permute-start) | collective-permute-done | bytes 1048608 | tf_op jit(solution)/shard_map/ppermute | solution.py:31
  31.6 1.3 collective-permute-start.3
  32.9 1.7 collective-permute-start.2
  40.4 17.5 %collective-permute-done.3 = f32[1024,256]{1,0:T(8,128)} collective-permute-done((f32[1024,256]{1,0:T(8,128)S(1)}, f32[1024,256]{1,0:T(8,128)}, u32[]{:S(2)}, u32[]{:S(2)}) %collective-permute-start.3) | collective-permute-done | bytes 1048608 | tf_op jit(solution)/shard_map/ppermute | solution.py:31
  57.9 1.3 collective-permute-start.5
  61.1 2.3 bitcast_multiply_fusion
  63.7 19.7 %collective-permute-done.5 = f32[1024,256]{1,0:T(8,128)S(1)} collective-permute-done((f32[1024,256]{1,0:T(8,128)}, f32[1024,256]{1,0:T(8,128)S(1)}, u32[]{:S(2)}, u32[]{:S(2)}) %collective-permute-start.5) | collective-permute-done | bytes 1048608 | tf_op jit(solution)/shard_map/ppermute | solution.py:31
  83.4 2.1 select_bitcast_fusion.1
  85.9 1.3 collective-permute-start.11
  87.2 4.7 collective-permute-start.9
  91.9 43.9 %collective-permute-done.11.refs_8_.refs_7_.refs_6_.refs_5_ = f32[256,2048]{1,0:T(8,128)S(1)} collective-permute-done((f32[256,2048]{1,0:T(8,128)S(1)}, f32[256,2048]{1,0:T(8,128)S(1)}, u32[]{:S(2)}, u32[]{:S(2)}) %collective-permute-start.11) | collective-permute-done | bytes 2097184 | tf_op jit(solution)/shard_map/ppermute | solution.py:31
  135.8 1.3 collective-permute-start.12
  137.1 2.1 collective-permute-start.10
  139.1 1.3 collective-permute-start.20
  141.2 11.5 %collective-permute-done.20.refs_1_ = f32[1,1024,256]{2,1,0:T(8,128)S(1)} collective-permute-done((f32[1,1024,256]{2,1,0:T(8,128)S(1)}, f32[1,1024,256]{2,1,0:T(8,128)S(1)}, u32[]{:S(2)}, u32[]{:S(2)}) %collective-permute-start.20) | collective-permute-done | bytes 1048608 | tf_op jit(solution)/shard_map/ppermute | solution.py:236
  152.7 2.8 collective-permute-start.21
  156.5 28.6 %collective-permute-done.12.refs_9_.refs_8_.refs_7_.refs_6_ = f32[256,2048]{1,0:T(8,128)} collective-permute-done((f32[256,2048]{1,0:T(8,128)S(1)}, f32[256,2048]{1,0:T(8,128)}, u32[]{:S(2)}, u32[]{:S(2)}) %collective-permute-start.12) | collective-permute-done | bytes 2097184 | tf_op jit(solution)/shard_map/ppermute | solution.py:31
  185.1 1.3 collective-permute-start.16
  186.4 2.0 collective-permute-start.19
  188.4 73.9 %all-gather.1 = s32[32,2,128]{2,1,0:T(2,128)S(1)} all-gather(s32[1,2,128]{2,1,0:T(2,128)S(1)} %add_bitcast_fusion), channel_id=2, replica_groups=mesh['row'=4,'col'=8] {'row','col'}, dimensions={0}, use_global_device_ids=true | all-gather | bytes 33792 | tf_op jit(solution)/shard_map/all_gather | solution.py:167
  269.0 3.6 collective-permute-start.13
  275.9 1.2 copy-done.5
  277.2 19.3 %products.7 = f32[64,128,128]{2,1,0:T(8,128)} custom-call(s32[64]{0:T(128)S(1)} %get-tuple-element.20.table, s32[4]{0:T(128)S(1)} %fusion.13.which, f32[1,1024,256]{2,1,0:T(8,128)S(1)} %bitcast.62, f32[1,1024,256]{2,1,0:T(8,128)S(1)} %copy-done.5, f32[1,1024,256]{2,1,0:T(8,128)} %collective-permute-done.21.refs_2_, ...), custom_call_target="tpu_custom_call" | custom-call | flops 12884901888 | bytes 16777216 | tf_op jit(solution)/shard_map/products/pallas_call | solution.py:112
  296.5 7.2 %all-to-all-start.3 = ((f32[64,128,128]{2,1,0:T(8,128)}), f32[64,128,128]{2,1,0:T(8,128)}, u32[]{:S(2)}, u32[]{:S(2)}) async-start(f32[64,128,128]{2,1,0:T(8,128)} %products.7), calls=%async_computation.3 | async-start | bytes 8388608 | tf_op jit(solution)/shard_map/all_to_all | solution.py:256
  303.7 1.3 collective-permute-start.17
  305.0 11.1 %collective-permute-done.13.refs_6_.refs_5_.refs_4_ = f32[256,2048]{1,0:T(8,128)} collective-permute-done((f32[256,2048]{1,0:T(8,128)S(1)}, f32[256,2048]{1,0:T(8,128)}, u32[]{:S(2)}, u32[]{:S(2)}) %collective-permute-start.13) | collective-permute-done | bytes 2097184 | tf_op jit(solution)/shard_map/ppermute | solution.py:26
  317.6 37.7 %collective-permute-done.17.refs_13_ = f32[256,2048]{1,0:T(8,128)S(1)} collective-permute-done((f32[256,2048]{1,0:T(8,128)}, f32[256,2048]{1,0:T(8,128)S(1)}, u32[]{:S(2)}, u32[]{:S(2)}) %collective-permute-start.17) | collective-permute-done | bytes 2097184 | tf_op jit(solution)/shard_map/ppermute | solution.py:31
  355.3 1.4 copy-done.18
  356.6 20.7 %products.5 = f32[64,128,128]{2,1,0:T(8,128)} custom-call(s32[64]{0:T(128)S(1)} %get-tuple-element.22.table, s32[4]{0:T(128)S(1)} %fusion.7.which, f32[3,1024,256]{2,1,0:T(8,128)} %copy-done.7, f32[3,1024,256]{2,1,0:T(8,128)} %collective-permute-done.6.refs_1_, f32[3,1024,256]{2,1,0:T(8,128)} %collective-permute-done.7.refs_2_, ...), custom_call_target="tpu_custom_call" | custom-call | flops 12884901888 | bytes 16777216 | tf_op jit(solution)/shard_map/products/pallas_call | solution.py:112
  377.3 1.3 copy-done.2
  378.6 4.7 all-to-all-start.1
  384.0 21.1 %products.6 = f32[64,128,128]{2,1,0:T(8,128)} custom-call(s32[64]{0:T(128)S(1)} %get-tuple-element.21.table, s32[4]{0:T(128)S(1)} %fusion.10.which, f32[3,1024,256]{2,1,0:T(8,128)} %copy-done.7, f32[3,1024,256]{2,1,0:T(8,128)} %collective-permute-done.6.refs_1_, f32[3,1024,256]{2,1,0:T(8,128)} %collective-permute-done.7.refs_2_, ...), custom_call_target="tpu_custom_call" | custom-call | flops 12884901888 | bytes 16777216 | tf_op jit(solution)/shard_map/products/pallas_call | solution.py:112
  405.1 27.3 %all-to-all-done.1.got = f32[64,128,128]{2,1,0:T(8,128)} async-done(((f32[64,128,128]{2,1,0:T(8,128)}), f32[64,128,128]{2,1,0:T(8,128)}, u32[]{:S(2)}, u32[]{:S(2)}) %all-to-all-start.1) | async-done | bytes 4194336 | tf_op jit(solution)/shard_map/all_to_all | solution.py:256
  432.5 4.6 all-to-all-start.2
  437.0 1.3 collective-permute-start.18
  439.8 59.2 %collective-permute-done.18.refs_14_ = f32[256,2048]{1,0:T(8,128)S(1)} collective-permute-done((f32[256,2048]{1,0:T(8,128)}, f32[256,2048]{1,0:T(8,128)S(1)}, u32[]{:S(2)}, u32[]{:S(2)}) %collective-permute-start.18) | collective-permute-done | bytes 2097184 | tf_op jit(solution)/shard_map/ppermute | solution.py:31
  499.1 1.3 copy-done.19
  500.4 22.8 %products.4 = f32[64,128,128]{2,1,0:T(8,128)} custom-call(s32[64]{0:T(128)S(1)} %get-tuple-element.23.table, s32[4]{0:T(128)S(1)} %fusion.4.which, f32[3,1024,256]{2,1,0:T(8,128)} %copy-done.7, f32[3,1024,256]{2,1,0:T(8,128)} %collective-permute-done.6.refs_1_, f32[3,1024,256]{2,1,0:T(8,128)} %collective-permute-done.7.refs_2_, ...), custom_call_target="tpu_custom_call" | custom-call | flops 12884901888 | bytes 16777216 | tf_op jit(solution)/shard_map/products/pallas_call | solution.py:112
  523.1 4.6 all-to-all-start
  529.6 9.7 %add_blocks.4.start = f32[128,128,128]{2,1,0:T(8,128)} custom-call(s32[64]{0:T(128)S(1)} %get-tuple-element.24.targets, f32[64,128,128]{2,1,0:T(8,128)} %all-to-all-done.3.got, f32[128,128,128]{2,1,0:T(8,128)} %bitcast.64), custom_call_target="tpu_custom_call" | custom-call | flops 1048576 | bytes 20971520 | tf_op jit(solution)/shard_map/add_blocks/pallas_call | solution.py:151
  539.3 9.5 %add_blocks.5.start = f32[128,128,128]{2,1,0:T(8,128)} custom-call(s32[64]{0:T(128)S(1)} %get-tuple-element.25.targets, f32[64,128,128]{2,1,0:T(8,128)} %all-to-all-done.2.got, f32[128,128,128]{2,1,0:T(8,128)} %add_blocks.4.start), custom_call_target="tpu_custom_call" | custom-call | flops 1048576 | bytes 20971520 | tf_op jit(solution)/shard_map/add_blocks/pallas_call | solution.py:151
  548.7 9.6 %add_blocks.6.start = f32[128,128,128]{2,1,0:T(8,128)} custom-call(s32[64]{0:T(128)S(1)} %get-tuple-element.26.targets, f32[64,128,128]{2,1,0:T(8,128)} %all-to-all-done.1.got, f32[128,128,128]{2,1,0:T(8,128)} %add_blocks.5.start), custom_call_target="tpu_custom_call" | custom-call | flops 1048576 | bytes 20971520 | tf_op jit(solution)/shard_map/add_blocks/pallas_call | solution.py:151
  558.3 18.6 %all-to-all-done.got = f32[64,128,128]{2,1,0:T(8,128)} async-done(((f32[64,128,128]{2,1,0:T(8,128)}), f32[64,128,128]{2,1,0:T(8,128)}, u32[]{:S(2)}, u32[]{:S(2)}) %all-to-all-start) | async-done | bytes 4194336 | tf_op jit(solution)/shard_map/all_to_all | solution.py:256
  576.8 9.6 %add_blocks.7 = f32[128,128,128]{2,1,0:T(8,128)} custom-call(s32[64]{0:T(128)S(1)} %get-tuple-element.27.targets, f32[64,128,128]{2,1,0:T(8,128)} %all-to-all-done.got, f32[128,128,128]{2,1,0:T(8,128)} %add_blocks.6.start), custom_call_target="tpu_custom_call" | custom-call | flops 1048576 | bytes 20971520 | tf_op jit(solution)/shard_map/add_blocks/pallas_call | solution.py:151
  (105 shorter events, 17.2 us)
Async XLA Ops:
  0.0 34.5 %copy-start.25 = (s32[4]{0:T(128)S(1)}, s32[4]{0:T(128)}, u32[]{:S(2)}) copy-start(s32[4]{0:T(128)} %constant.103.clone) | copy-start | bytes 52
  0.0 36.4 %copy-start.24 = (s32[4]{0:T(128)S(1)}, s32[4]{0:T(128)}, u32[]{:S(2)}) copy-start(s32[4]{0:T(128)} %constant.104.clone) | copy-start | bytes 52
  0.0 39.0 %copy-start.23 = (s32[4]{0:T(128)S(1)}, s32[4]{0:T(128)}, u32[]{:S(2)}) copy-start(s32[4]{0:T(128)} %constant.102.clone) | copy-start | bytes 52
  0.0 40.3 %copy-start.13 = (s32[4,16]{1,0:T(4,128)S(1)}, s32[4,16]{1,0:T(4,128)}, u32[]{:S(2)}) copy-start(s32[4,16]{1,0:T(4,128)} %param.21) | copy-start | bytes 772
  3.5 28.1 %collective-permute-start = (f32[1024,256]{1,0:T(8,128)S(1)}, f32[1024,256]{1,0:T(8,128)S(1)}, u32[]{:S(2)}, u32[]{:S(2)}) collective-permute-start(f32[1024,256]{1,0:T(8,128)S(1)} %bitcast_multiply_fusion.1), channel_id=1, source_target_pairs={{8,0},{16,8},{24,16},{9,1},{17,9},{25,17},{10,2},{18,10},{26,18},{... | collective-permute-start | bytes 3145736 | tf_op jit(solution)/shard_map/ppermute | solution.py:31
  4.8 28.1 %collective-permute-start.1 = (f32[1024,256]{1,0:T(8,128)S(1)}, f32[1024,256]{1,0:T(8,128)S(1)}, u32[]{:S(2)}, u32[]{:S(2)}) collective-permute-start(f32[1024,256]{1,0:T(8,128)S(1)} %bitcast_multiply_fusion.1), channel_id=1, source_target_pairs={{0,8},{8,16},{16,24},{1,9},{9,17},{17,25},{2,10},{10,18},{18,26},{... | collective-permute-start | bytes 3145736 | tf_op jit(solution)/shard_map/ppermute | solution.py:26
  31.6 29.5 %copy-start.9 = (f32[1024,256]{1,0:T(8,128)}, f32[1024,256]{1,0:T(8,128)S(1)}, u32[]{:S(2)}) copy-start(f32[1024,256]{1,0:T(8,128)S(1)} %collective-permute-done) | copy-start | bytes 3145732
  31.6 26.3 %collective-permute-start.3 = (f32[1024,256]{1,0:T(8,128)S(1)}, f32[1024,256]{1,0:T(8,128)}, u32[]{:S(2)}, u32[]{:S(2)}) collective-permute-start(f32[1024,256]{1,0:T(8,128)S(1)} %collective-permute-done), channel_id=1, source_target_pairs={{8,0},{16,8},{9,1},{17,9},{10,2},{18,10},{11,3},{19,11},{12,4},{20... | collective-permute-start | bytes 3145736 | tf_op jit(solution)/shard_map/ppermute | solution.py:31
  32.9 28.2 %copy-start.11 = (f32[1024,256]{1,0:T(8,128)}, f32[1024,256]{1,0:T(8,128)S(1)}, u32[]{:S(2)}) copy-start(f32[1024,256]{1,0:T(8,128)S(1)} %collective-permute-done.1) | copy-start | bytes 3145732
  32.9 26.3 %collective-permute-start.2 = (f32[1024,256]{1,0:T(8,128)S(1)}, f32[1024,256]{1,0:T(8,128)}, u32[]{:S(2)}, u32[]{:S(2)}) collective-permute-start(f32[1024,256]{1,0:T(8,128)S(1)} %collective-permute-done.1), channel_id=1, source_target_pairs={{8,16},{16,24},{9,17},{17,25},{10,18},{18,26},{11,19},{19,27},{12,... | collective-permute-start | bytes 3145736 | tf_op jit(solution)/shard_map/ppermute | solution.py:26
  40.3 20.8 %copy-start.6 = (f32[512,2048]{1,0:T(8,128)S(1)}, f32[512,2048]{1,0:T(8,128)}, u32[]{:S(2)}) copy-start(f32[512,2048]{1,0:T(8,128)} %param.19) | copy-start | bytes 12582916
  57.9 25.5 %collective-permute-start.5 = (f32[1024,256]{1,0:T(8,128)}, f32[1024,256]{1,0:T(8,128)S(1)}, u32[]{:S(2)}, u32[]{:S(2)}) collective-permute-start(f32[1024,256]{1,0:T(8,128)} %collective-permute-done.3), channel_id=1, source_target_pairs={{8,0},{9,1},{10,2},{11,3},{12,4},{13,5},{14,6},{15,7}} | collective-permute-start | bytes 3145736 | tf_op jit(solution)/shard_map/ppermute | solution.py:31
  59.2 24.2 %collective-permute-start.4 = (f32[1024,256]{1,0:T(8,128)}, f32[1024,256]{1,0:T(8,128)S(1)}, u32[]{:S(2)}, u32[]{:S(2)}) collective-permute-start(f32[1024,256]{1,0:T(8,128)} %collective-permute-done.2), channel_id=1, source_target_pairs={{16,24},{17,25},{18,26},{19,27},{20,28},{21,29},{22,30},{23,31}} | collective-permute-start | bytes 3145736 | tf_op jit(solution)/shard_map/ppermute | solution.py:26
  63.4 20.0 %copy-start.10 = (f32[1024,256]{1,0:T(8,128)S(1)}, f32[1024,256]{1,0:T(8,128)}, u32[]{:S(2)}) copy-start(f32[1024,256]{1,0:T(8,128)} %copy-done.9) | copy-start | bytes 3145732
  63.4 20.0 %copy-start.12 = (f32[1024,256]{1,0:T(8,128)S(1)}, f32[1024,256]{1,0:T(8,128)}, u32[]{:S(2)}) copy-start(f32[1024,256]{1,0:T(8,128)} %copy-done.11) | copy-start | bytes 3145732
  63.7 23.4 %copy-start.8 = (f32[256,2048]{1,0:T(8,128)}, f32[256,2048]{1,0:T(8,128)S(1)}, u32[]{:S(2)}) copy-start(f32[256,2048]{1,0:T(8,128)S(1)} %get-tuple-element.8.refs_12_) | copy-start | bytes 6291460
  63.7 205.3 %copy-start = (f32[256,2048]{1,0:T(8,128)}, f32[256,2048]{1,0:T(8,128)S(1)}, u32[]{:S(2)}) copy-start(f32[256,2048]{1,0:T(8,128)S(1)} %get-tuple-element.7.refs_7_.refs_6_.refs_5_.refs_4_) | copy-start | bytes 6291460
  85.5 102.9 %copy-start.14 = (s32[1,1,128]{2,1,0:T(1,128)S(1)}, s32[1,1,128]{2,1,0:T(1,128)}, u32[]{:S(2)}) copy-start(s32[1,1,128]{2,1,0:T(1,128)} %param.23) | copy-start | bytes 1540
  85.5 102.9 %copy-start.15 = (s32[1,1,128,1]{2,3,1,0:T(1,128)S(1)}, s32[1,1,128,1]{2,3,1,0:T(1,128)}, u32[]{:S(2)}) copy-start(s32[1,1,128,1]{2,3,1,0:T(1,128)} %param.22) | copy-start | bytes 1540
  85.5 176.8 %copy-start.22 = (s32[4]{0:T(128)S(1)}, s32[4]{0:T(128)}, u32[]{:S(2)}) copy-start(s32[4]{0:T(128)} %constant.107.clone) | copy-start | bytes 52
  85.5 178.5 %copy-start.21 = (s32[4]{0:T(128)S(1)}, s32[4]{0:T(128)}, u32[]{:S(2)}) copy-start(s32[4]{0:T(128)} %constant.109.clone) | copy-start | bytes 52
  85.6 180.6 %copy-start.20 = (s32[4]{0:T(128)S(1)}, s32[4]{0:T(128)}, u32[]{:S(2)}) copy-start(s32[4]{0:T(128)} %constant.111.clone) | copy-start | bytes 52
  85.8 176.5 %copy-start.7 = (f32[3,1024,256]{2,1,0:T(8,128)}, f32[3,1024,256]{2,1,0:T(8,128)S(1)}, u32[]{:S(2)}) copy-start(f32[3,1024,256]{2,1,0:T(8,128)S(1)} %pad_maximum_fusion.refs_0_) | copy-start | bytes 9437188
  85.8 54.6 %collective-permute-start.6 = (f32[3,1024,256]{2,1,0:T(8,128)S(1)}, f32[3,1024,256]{2,1,0:T(8,128)}, u32[]{:S(2)}, u32[]{:S(2)}) collective-permute-start(f32[3,1024,256]{2,1,0:T(8,128)S(1)} %pad_maximum_fusion.refs_0_), channel_id=1, source_target_pairs={{1,0},{2,1},{3,2},{4,3},{5,4},{6,5},{7,6},{0,7},{9,8},{10,9},{11,1... | collective-permute-start | bytes 9437192 | tf_op jit(solution)/shard_map/ppermute | solution.py:238
  85.9 49.9 %collective-permute-start.11 = (f32[256,2048]{1,0:T(8,128)S(1)}, f32[256,2048]{1,0:T(8,128)S(1)}, u32[]{:S(2)}, u32[]{:S(2)}) collective-permute-start(f32[256,2048]{1,0:T(8,128)S(1)} %get-tuple-element.7.refs_7_.refs_6_.refs_5_.refs_4_), channel_id=1, source_target_pairs={{8,0},{16,8},{24,16},{9,1},{17,9},{25,17},{10,2},{18,10},{26,18},{... | collective-permute-start | bytes 6291464 | tf_op jit(solution)/shard_map/ppermute | solution.py:31
  87.2 49.9 %collective-permute-start.9 = (f32[256,2048]{1,0:T(8,128)S(1)}, f32[256,2048]{1,0:T(8,128)S(1)}, u32[]{:S(2)}, u32[]{:S(2)}) collective-permute-start(f32[256,2048]{1,0:T(8,128)S(1)} %get-tuple-element.8.refs_12_), channel_id=1, source_target_pairs={{0,8},{8,16},{16,24},{1,9},{9,17},{17,25},{2,10},{10,18},{18,26},{... | collective-permute-start | bytes 6291464 | tf_op jit(solution)/shard_map/ppermute | solution.py:26
  135.8 126.5 %copy-start.16 = (f32[256,2048]{1,0:T(8,128)}, f32[256,2048]{1,0:T(8,128)S(1)}, u32[]{:S(2)}) copy-start(f32[256,2048]{1,0:T(8,128)S(1)} %collective-permute-done.11.refs_8_.refs_7_.refs_6_.refs_5_) | copy-start | bytes 6291460
  135.8 49.3 %collective-permute-start.12 = (f32[256,2048]{1,0:T(8,128)S(1)}, f32[256,2048]{1,0:T(8,128)}, u32[]{:S(2)}, u32[]{:S(2)}) collective-permute-start(f32[256,2048]{1,0:T(8,128)S(1)} %collective-permute-done.11.refs_8_.refs_7_.refs_6_.refs_5_), channel_id=1, source_target_pairs={{8,0},{16,8},{9,1},{17,9},{10,2},{18,10},{11,3},{19,11},{12,4},{20... | collective-permute-start | bytes 6291464 | tf_op jit(solution)/shard_map/ppermute | solution.py:31
  137.1 125.2 %copy-start.17 = (f32[256,2048]{1,0:T(8,128)}, f32[256,2048]{1,0:T(8,128)S(1)}, u32[]{:S(2)}) copy-start(f32[256,2048]{1,0:T(8,128)S(1)} %collective-permute-done.9.refs_11_.refs_10_) | copy-start | bytes 6291460
  137.1 49.3 %collective-permute-start.10 = (f32[256,2048]{1,0:T(8,128)S(1)}, f32[256,2048]{1,0:T(8,128)}, u32[]{:S(2)}, u32[]{:S(2)}) collective-permute-start(f32[256,2048]{1,0:T(8,128)S(1)} %collective-permute-done.9.refs_11_.refs_10_), channel_id=1, source_target_pairs={{8,16},{16,24},{9,17},{17,25},{10,18},{18,26},{11,19},{19,27},{12,... | collective-permute-start | bytes 6291464 | tf_op jit(solution)/shard_map/ppermute | solution.py:26
  139.1 13.6 %collective-permute-start.20 = (f32[1,1024,256]{2,1,0:T(8,128)S(1)}, f32[1,1024,256]{2,1,0:T(8,128)S(1)}, u32[]{:S(2)}, u32[]{:S(2)}) collective-permute-start(f32[1,1024,256]{2,1,0:T(8,128)S(1)} %bitcast.61), channel_id=1, source_target_pairs={{1,0},{2,1},{3,2},{4,3},{5,4},{6,5},{7,6},{0,7},{9,8},{10,9},{11,1... | collective-permute-start | bytes 3145736 | tf_op jit(solution)/shard_map/ppermute | solution.py:236
  140.4 135.4 %collective-permute-start.7 = (f32[3,1024,256]{2,1,0:T(8,128)}, f32[3,1024,256]{2,1,0:T(8,128)}, u32[]{:S(2)}, u32[]{:S(2)}) collective-permute-start(f32[3,1024,256]{2,1,0:T(8,128)} %collective-permute-done.6.refs_1_), channel_id=1, source_target_pairs={{1,0},{2,1},{3,2},{4,3},{5,4},{6,5},{7,6},{0,7},{9,8},{10,9},{11,1... | collective-permute-start | bytes 9437192 | tf_op jit(solution)/shard_map/ppermute | solution.py:238
  152.7 109.6 %collective-permute-start.21 = (f32[1,1024,256]{2,1,0:T(8,128)S(1)}, f32[1,1024,256]{2,1,0:T(8,128)}, u32[]{:S(2)}, u32[]{:S(2)}) collective-permute-start(f32[1,1024,256]{2,1,0:T(8,128)S(1)} %collective-permute-done.20.refs_1_), channel_id=1, source_target_pairs={{1,0},{2,1},{3,2},{4,3},{5,4},{6,5},{7,6},{0,7},{9,8},{10,9},{11,1... | collective-permute-start | bytes 3145736 | tf_op jit(solution)/shard_map/ppermute | solution.py:236
  185.1 90.8 %collective-permute-start.16 = (f32[256,2048]{1,0:T(8,128)}, f32[256,2048]{1,0:T(8,128)}, u32[]{:S(2)}, u32[]{:S(2)}) collective-permute-start(f32[256,2048]{1,0:T(8,128)} %collective-permute-done.12.refs_9_.refs_8_.refs_7_.refs_6_), channel_id=1, source_target_pairs={{8,0},{9,1},{10,2},{11,3},{12,4},{13,5},{14,6},{15,7}} | collective-permute-start | bytes 6291464 | tf_op jit(solution)/shard_map/ppermute | solution.py:31
  186.4 89.5 %collective-permute-start.19 = (f32[256,2048]{1,0:T(8,128)}, f32[256,2048]{1,0:T(8,128)}, u32[]{:S(2)}, u32[]{:S(2)}) collective-permute-start(f32[256,2048]{1,0:T(8,128)} %collective-permute-done.10.refs_11_.refs_10_.refs_9_), channel_id=1, source_target_pairs={{16,24},{17,25},{18,26},{19,27},{20,28},{21,29},{22,30},{23,31}} | collective-permute-start | bytes 6291464 | tf_op jit(solution)/shard_map/ppermute | solution.py:26
  262.3 13.6 %collective-permute-start.22 = (f32[1,1024,256]{2,1,0:T(8,128)}, f32[1,1024,256]{2,1,0:T(8,128)}, u32[]{:S(2)}, u32[]{:S(2)}) collective-permute-start(f32[1,1024,256]{2,1,0:T(8,128)} %collective-permute-done.21.refs_2_), channel_id=1, source_target_pairs={{1,0},{2,1},{3,2},{4,3},{5,4},{6,5},{7,6},{0,7},{9,8},{10,9},{11,1... | collective-permute-start | bytes 3145736 | tf_op jit(solution)/shard_map/ppermute | solution.py:236
  269.0 47.1 %collective-permute-start.13 = (f32[256,2048]{1,0:T(8,128)S(1)}, f32[256,2048]{1,0:T(8,128)}, u32[]{:S(2)}, u32[]{:S(2)}) collective-permute-start(f32[256,2048]{1,0:T(8,128)S(1)} %get-tuple-element.7.refs_7_.refs_6_.refs_5_.refs_4_), channel_id=1, source_target_pairs={{0,8},{8,16},{16,24},{1,9},{9,17},{17,25},{2,10},{10,18},{18,26},{... | collective-permute-start | bytes 6291464 | tf_op jit(solution)/shard_map/ppermute | solution.py:26
  275.8 79.4 %collective-permute-start.8 = (f32[3,1024,256]{2,1,0:T(8,128)}, f32[3,1024,256]{2,1,0:T(8,128)}, u32[]{:S(2)}, u32[]{:S(2)}) collective-permute-start(f32[3,1024,256]{2,1,0:T(8,128)} %collective-permute-done.7.refs_2_), channel_id=1, source_target_pairs={{1,0},{2,1},{3,2},{4,3},{5,4},{6,5},{7,6},{0,7},{9,8},{10,9},{11,1... | collective-permute-start | bytes 9437192 | tf_op jit(solution)/shard_map/ppermute | solution.py:238
  296.5 82.2 %all-to-all-start.3 = ((f32[64,128,128]{2,1,0:T(8,128)}), f32[64,128,128]{2,1,0:T(8,128)}, u32[]{:S(2)}, u32[]{:S(2)}) async-start(f32[64,128,128]{2,1,0:T(8,128)} %products.7), calls=%async_computation.3 | async-start | bytes 8388608 | tf_op jit(solution)/shard_map/all_to_all | solution.py:256
  303.7 51.5 %collective-permute-start.17 = (f32[256,2048]{1,0:T(8,128)}, f32[256,2048]{1,0:T(8,128)S(1)}, u32[]{:S(2)}, u32[]{:S(2)}) collective-permute-start(f32[256,2048]{1,0:T(8,128)} %copy-done.8), channel_id=1, source_target_pairs={{8,0},{16,8},{9,1},{17,9},{10,2},{18,10},{11,3},{19,11},{12,4},{20... | collective-permute-start | bytes 6291464 | tf_op jit(solution)/shard_map/ppermute | solution.py:31
  316.1 39.2 %collective-permute-start.14 = (f32[256,2048]{1,0:T(8,128)}, f32[256,2048]{1,0:T(8,128)S(1)}, u32[]{:S(2)}, u32[]{:S(2)}) collective-permute-start(f32[256,2048]{1,0:T(8,128)} %collective-permute-done.13.refs_6_.refs_5_.refs_4_), channel_id=1, source_target_pairs={{8,16},{16,24},{9,17},{17,25},{10,18},{18,26},{11,19},{19,27},{12,... | collective-permute-start | bytes 6291464 | tf_op jit(solution)/shard_map/ppermute | solution.py:26
  378.6 5.4 copy-start.1
  378.6 53.9 %all-to-all-start.1 = ((f32[64,128,128]{2,1,0:T(8,128)}), f32[64,128,128]{2,1,0:T(8,128)}, u32[]{:S(2)}, u32[]{:S(2)}) async-start(f32[64,128,128]{2,1,0:T(8,128)} %products.5), calls=%async_computation.1 | async-start | bytes 8388608 | tf_op jit(solution)/shard_map/all_to_all | solution.py:256
  405.1 33.2 %copy-start.3 = (f32[256,2048]{1,0:T(8,128)S(1)}, f32[256,2048]{1,0:T(8,128)}, u32[]{:S(2)}) copy-start(f32[256,2048]{1,0:T(8,128)} %copy-done.2) | copy-start | bytes 6291460
  432.5 90.7 %all-to-all-start.2 = ((f32[64,128,128]{2,1,0:T(8,128)}), f32[64,128,128]{2,1,0:T(8,128)}, u32[]{:S(2)}, u32[]{:S(2)}) async-start(f32[64,128,128]{2,1,0:T(8,128)} %products.6), calls=%async_computation.2 | async-start | bytes 8388608 | tf_op jit(solution)/shard_map/all_to_all | solution.py:256
  437.0 62.0 %collective-permute-start.18 = (f32[256,2048]{1,0:T(8,128)}, f32[256,2048]{1,0:T(8,128)S(1)}, u32[]{:S(2)}, u32[]{:S(2)}) collective-permute-start(f32[256,2048]{1,0:T(8,128)} %copy-done.18), channel_id=1, source_target_pairs={{8,0},{9,1},{10,2},{11,3},{12,4},{13,5},{14,6},{15,7}} | collective-permute-start | bytes 6291464 | tf_op jit(solution)/shard_map/ppermute | solution.py:31
  438.4 60.7 %collective-permute-start.15 = (f32[256,2048]{1,0:T(8,128)S(1)}, f32[256,2048]{1,0:T(8,128)S(1)}, u32[]{:S(2)}, u32[]{:S(2)}) collective-permute-start(f32[256,2048]{1,0:T(8,128)S(1)} %copy-done.3), channel_id=1, source_target_pairs={{16,24},{17,25},{18,26},{19,27},{20,28},{21,29},{22,30},{23,31}} | collective-permute-start | bytes 6291464 | tf_op jit(solution)/shard_map/ppermute | solution.py:26
  523.1 53.7 %all-to-all-start = ((f32[64,128,128]{2,1,0:T(8,128)}), f32[64,128,128]{2,1,0:T(8,128)}, u32[]{:S(2)}, u32[]{:S(2)}) async-start(f32[64,128,128]{2,1,0:T(8,128)} %products.4), calls=%async_computation | async-start | bytes 8388608 | tf_op jit(solution)/shard_map/all_to_all | solution.py:256
  (5 other events, 6.2 us)

commit v2 on v1

--- a/solution.py
+++ b/solution.py
@@ -17,10 +17,6 @@
     return panel * jnp.repeat(jnp.repeat(occupancy.astype(jnp.float32), BLK, axis=0), BLK, axis=1)
 
 
-def after(value, *others):
-    return lax.optimization_barrier((value,) + others)[0]
-
-
 def up_step(value, sources, step, n_row):
     pairs = [(b + step - 1, b + step) for b in sources if b + step < n_row]
     return lax.ppermute(value, "row", pairs) if pairs else None
@@ -46,7 +42,7 @@
     return high, low
 
 
-def product_kernel(place, choices, table, which, *refs):
+def product_kernel(choices, table, which, *refs):
     count = len(choices)
     lefts = refs[:TICKS]
     rights = refs[TICKS : TICKS + count]
@@ -56,7 +52,7 @@
     q_blocks = right_in.shape[2] // BLK
 
     def left_copy(t):
-        return pltpu.make_async_copy(lefts[t].at[place], left_in.at[t], left_sem.at[t])
+        return pltpu.make_async_copy(lefts[t], left_in.at[t], left_sem.at[t])
 
     for t in range(TICKS):
         left_copy(t).start()
@@ -103,14 +99,14 @@
             out[slot] = jnp.zeros((BLK, BLK), jnp.float32)
 
 
-def products(table, which, lefts, rights, choices, place, slots):
-    rows, inner = lefts[0].shape[1:]
+def products(table, which, lefts, rights, choices, slots):
+    rows, inner = lefts[0].shape
     cols = rights[0].shape[1]
     smem = pl.BlockSpec(memory_space=pltpu.SMEM)
     hbm = pl.BlockSpec(memory_space=pl.ANY)
     deep = TICKS * inner
     return pl.pallas_call(
-        functools.partial(product_kernel, place, choices),
+        functools.partial(product_kernel, choices),
         out_shape=jax.ShapeDtypeStruct((slots, BLK, BLK), jnp.float32),
         in_specs=[smem, smem] + [hbm] * (TICKS + len(rights)),
         out_specs=pl.BlockSpec(memory_space=pltpu.VMEM),
@@ -164,8 +160,10 @@
 def tables(owner_device, owner_block, n_row, n_col, capacity):
     row, col = lax.axis_index("row"), lax.axis_index("col")
     mine = jnp.stack([owner_device.reshape(-1), owner_block.reshape(-1)])
-    every = lax.all_gather(mine, ("row", "col"))
     count = mine.shape[1]
+    every = lax.all_to_all(
+        jnp.broadcast_to(mine, (n_row * n_col,) + mine.shape), ("row", "col"), 0, 0, tiled=True
+    )
     every = every.reshape(n_row, n_col, 2, count)
     places = jnp.arange(capacity, dtype=jnp.int32)
 
@@ -194,67 +192,81 @@
     count_blocks = owner_block.size
     capacity = max(2, (2 * count_blocks + n_row * n_col - 1) // (n_row * n_col))
     order = visit_order(n_row)
-
-    left = widen(a_occupancy, a_panels)
-    right = widen(b_occupancy, b_panels)
+    every_row = list(range(n_row))
+    early = list(range(TICKS - 1))
+    backward = [((c + 1) % n_col, c) for c in range(n_col)]
 
     def image(number):
         slot = (row + col + number * n_row) % n_col // n_row
-        return lax.dynamic_slice_in_dim(right, slot * inner, inner, 0)
-
-    held = {("X", 0): image(0), ("Y", 0): image(1)}
-    panels = {0: left}
-    every_row = list(range(n_row))
-    early = list(range(TICKS - 1))
-
-    sent, got = tables(owner_device, owner_block, n_row, n_col, capacity)
-    for d in range(1, n_row):
-        panels[-d] = up_step(panels[1 - d], every_row, d, n_row)
-        panels[d] = down_step(panels[d - 1], every_row, d)
-        held["Y", -d] = up_step(held["Y", 1 - d], early, d, n_row)
-        held["X", d] = down_step(held["X", d - 1], every_row, d)
-    gate = (held["Y", 2 - n_row], held["X", n_row - 2])
-    later = {("X", 0): after(held["X", 0], *gate), ("Y", 0): after(held["Y", 0], *gate)}
-    for d in range(1, n_row):
-        held["X", -d] = later["X", -d] = up_step(later["X", 1 - d], every_row, d, n_row)
-        if d < TICKS - 1:
-            held["Y", d] = later["Y", d] = down_step(later["Y", d - 1], early, d)
-
-    backward = [((c + 1) % n_col, c) for c in range(n_col)]
+        present = lax.dynamic_slice_in_dim(b_occupancy, slot * (inner // BLK), inner // BLK, 0)
+        return widen(present, lax.dynamic_slice_in_dim(b_panels, slot * inner, inner, 0))
+
+    held = {("A", 0): widen(a_occupancy, a_panels), ("X", 0): image(0), ("Y", 0): image(1)}
 
     def chosen(step):
         offsets = [order[r][step] - r for r in range(n_row)]
         kinds = sorted(set(offsets))
         index = jnp.asarray([kinds.index(o) for o in offsets], jnp.int32)[row]
-        return lax.select_n(index, *[panels[k] for k in kinds]) if len(kinds) > 2 else lax.select_n(
-            index == len(kinds) - 1, *[panels[k] for k in kinds]
+        cases = [held["A", k] for k in kinds]
+        return cases[0] if len(cases) == 1 else lax.select_n(
+            index if len(cases) > 2 else index == 1, *cases
         )
 
-    first = [left[None]]
-    rest = [jnp.stack([chosen(step) for step in range(1, n_row)])]
-    for t in range(1, TICKS):
-        first.append(lax.ppermute(first[-1], "col", backward))
-    for t in range(1, TICKS):
-        rest.append(lax.ppermute(rest[-1], "col", backward))
-
+    sent = got = None
+    lefts = []
     total = c_previous.reshape(c_previous.shape[2:])
-    for step in range(n_row):
-        keys = [[image_key(r, order[r][step] + t, n_row) for t in range(TICKS)] for r in range(n_row)]
-        names = sorted({key for of_row in keys for key in of_row})
-        choices = [{t for r in range(n_row) for t in range(TICKS) if keys[r][t] == name} for name in names]
-        which = jnp.asarray([[names.index(key) for key in of_row] for of_row in keys], jnp.int32)[row]
-        visit = jnp.asarray([order[r][step] for r in range(n_row)], jnp.int32)[row]
-        blocks = products(
-            sent[visit],
-            which,
-            first if step == 0 else rest,
-            [held[name] for name in names],
-            choices,
-            0 if step == 0 else step - 1,
-            n_col * capacity,
-        )
-        arrived = lax.all_to_all(blocks, "col", split_axis=0, concat_axis=0, tiled=True)
-        total = add_blocks(got[visit], arrived, total)
+    for phase in range(1, 2 * n_row):
+        moving = {}
+        d = phase if phase < n_row else phase - n_row + 1
+        if d < n_row:
+            upward, downward = ("AY", "AX") if phase < n_row else ("X", "Y")
+            for kind in upward:
+                sources = early if kind == "Y" else every_row
+                moving[kind, -d] = up_step(held[kind, 1 - d], sources, d, n_row)
+            for kind in downward:
+                sources = early if kind == "Y" else every_row
+                if (kind, d - 1) in held:
+                    moving[kind, d] = down_step(held[kind, d - 1], sources, d)
+        if phase <= n_row:
+            lefts.append([chosen(phase - 1)])
+        for step, panels in enumerate(lefts):
+            if len(panels) < TICKS:
+                moving["left", step] = lax.ppermute(panels[-1], "col", backward)
+        if phase == 1:
+            sent, got = tables(owner_device, owner_block, n_row, n_col, capacity)
+        step = phase - n_row
+        if step >= 0:
+            keys = [
+                [image_key(r, order[r][step] + t, n_row) for t in range(TICKS)] for r in range(n_row)
+            ]
+            names = sorted({key for of_row in keys for key in of_row})
+            choices = [
+                {t for r in range(n_row) for t in range(TICKS) if keys[r][t] == name} for name in names
+            ]
+            index = [[names.index(key) for key in of_row] for of_row in keys]
+            which = jnp.asarray(index, jnp.int32)[row]
+            visit = jnp.asarray([order[r][step] for r in range(n_row)], jnp.int32)[row]
+            blocks = products(
+                sent[visit],
+                which,
+                lefts[step],
+                [held[name] for name in names],
+                choices,
+                n_col * capacity,
+            )
+            arrived = lax.all_to_all(blocks, "col", split_axis=0, concat_axis=0, tiled=True)
+            total = add_blocks(got[visit], arrived, total)
+        moving = {key: value for key, value in moving.items() if value is not None}
+        if moving:
+            names = list(moving) + [key for key in held if key not in moving]
+            values = [moving.get(key, held.get(key)) for key in names]
+            values = lax.optimization_barrier(tuple(values) + (sent,))
+            sent = values[-1]
+            for key, value in zip(names, values):
+                if key[0] == "left":
+                    lefts[key[1]].append(value)
+                else:
+                    held[key] = value
     return total.reshape(c_previous.shape)
 
 

time: 586 us -> 622 us (1.061)
  waiting for transfers between devices: 296 us -> 375 us
  blocking collectives: 73.9 us -> 0 us
  starting transfers between devices: 58.3 us -> 79.5 us
    ppermute x6 -> x12, waiting for transfers between devices: 11.5 us -> 209 us  [per_device(): moving['left', step] = lax.ppermute(panels[-1], 'col', backward)]
    ppermute x8, waiting for transfers between devices: 228 us -> 93.5 us  [down_step(): return lax.ppermute(value, 'row', pairs) if pairs else None]
    all_gather x1 -> x0, blocking collectives: 73.9 us -> none  [tables(): every = lax.all_gather(mine, ('row', 'col'))]
    all_to_all x0 -> x1, waiting for transfers between devices: none -> 53.6 us  [tables(): lax.all_to_all(jnp.broadcast_to(mine, (n_row * n_col,) + mine.shape), ('r...]
    all_to_all x4, waiting for transfers between devices: 45.9 us -> 18.8 us  [per_device(): lax.all_to_all(blocks, 'col', split_axis=0, concat_axis=0, tiled=True)]
    ppermute x9, waiting for transfers between devices: 11.1 us -> 0.02 us  [up_step(): return lax.ppermute(value, 'row', pairs) if pairs else None]
    ppermute x6 -> x12, starting transfers between devices: 5.01 us -> 15.4 us  [per_device(): moving['left', step] = lax.ppermute(panels[-1], 'col', backward)]
    ppermute x9, starting transfers between devices: 21.9 us -> 28.8 us  [up_step(): return lax.ppermute(value, 'row', pairs) if pairs else None]
  transfers between devices with their start and end apart: 27 -> 34, of which waited for: 11 -> 15; matrix products, arithmetic and copies ran while one was open for 2% -> 2% of each run, Pallas kernels for 19% -> 15%
where the time goes in v2:
time: 622 us; the launch traced here: 623 us
  waiting for transfers between devices  375 us (60%)
  Pallas kernels  128 us (21%)
  starting transfers between devices  79.5 us (13%)
  local copies, waits for them, and re-layouts  16.7 us (3%)
  other arithmetic  13.5 us (2%)
  between operations  10.1 us (2%)
    ppermute x12, waiting for transfers between devices, per_device(): moving['left', step] = lax.ppermute(panels[-1], 'col', backward)  209 us
    ppermute x8, waiting for transfers between devices, down_step(): return lax.ppermute(value, 'row', pairs) if pairs else None  93.5 us
    pallas_call x4, Pallas kernels, products(): pl.pallas_call(functools.partial(product_kernel, choices), out_shape=jax....  89.9 us
    all_to_all x1, waiting for transfers between devices, tables(): lax.all_to_all(jnp.broadcast_to(mine, (n_row * n_col,) + mine.shape), ('r...  53.6 us
    pallas_call x4, Pallas kernels, add_blocks(): pl.pallas_call(add_kernel, out_shape=jax.ShapeDtypeStruct(start.shape, jn...  38.2 us
    ppermute x9, starting transfers between devices, up_step(): return lax.ppermute(value, 'row', pairs) if pairs else None  28.8 us
    all_to_all x4, starting transfers between devices, per_device(): lax.all_to_all(blocks, 'col', split_axis=0, concat_axis=0, tiled=True)  20.5 us
    all_to_all x4, waiting for transfers between devices, per_device(): lax.all_to_all(blocks, 'col', split_axis=0, concat_axis=0, tiled=True)  18.8 us
  transfers between devices with their start and end apart: 34, of which 15 were waited for; matrix products, arithmetic and copies ran while one was open for 2% of the time, Pallas kernels for 15%

profile of v2, /device:TPU:0, one launch (start us, length us, event | category | flops | bytes accessed | tf_op | source)
XLA Modules:
  0.0 622.6 jit_solution(12704266455092466331)
XLA Ops:
  3.0 4.2 bitcast_multiply_fusion
  7.2 1.4 collective-permute-start.3
  8.6 7.0 %collective-permute-start.1 = (f32[256,2048]{1,0:T(8,128)}, f32[256,2048]{1,0:T(8,128)}, u32[]{:S(2)}, u32[]{:S(2)}) collective-permute-start(f32[256,2048]{1,0:T(8,128)} %get-tuple-element.155.refs_12_), channel_id=1, source_target_pairs={{0,8},{8,16},{16,24},{1,9},{9,17},{17,25},{2,10},{10,18},{18,26},{... | collective-permute-start | bytes 6291464 | tf_op jit(solution)/shard_map/ppermute | solution.py:22
  17.2 1.8 collective-permute-start.4
  20.3 4.6 collective-permute-start
  25.6 4.5 all-to-all-start
  31.4 53.6 %all-to-all-done = s32[32,2,128]{2,1,0:T(2,128)S(1)} async-done(((s32[32,2,128]{2,1,0:T(2,128)}), s32[32,2,128]{2,1,0:T(2,128)S(1)}, u32[]{:S(2)}, u32[]{:S(2)}) %all-to-all-start) | async-done | bytes 32800 | tf_op jit(solution)/shard_map/all_to_all | solution.py:164
  88.1 1.4 broadcast_select_fusion.refs_0_
  89.9 2.0 collective-permute-start.6
  93.1 1.6 collective-permute-start.5
  95.3 6.9 %collective-permute-done.10.refs_1_ = f32[1024,256]{1,0:T(8,128)} collective-permute-done((f32[1024,256]{1,0:T(8,128)S(1)}, f32[1024,256]{1,0:T(8,128)}, u32[]{:S(2)}, u32[]{:S(2)}) %collective-permute-start.10) | collective-permute-done | bytes 1048608 | tf_op jit(solution)/shard_map/ppermute | solution.py:234
  105.4 8.0 %collective-permute-done.9.refs_2_ = f32[1024,256]{1,0:T(8,128)S(1)} collective-permute-done((f32[1024,256]{1,0:T(8,128)S(1)}, f32[1024,256]{1,0:T(8,128)S(1)}, u32[]{:S(2)}, u32[]{:S(2)}) %collective-permute-start.9) | collective-permute-done | bytes 1048608 | tf_op jit(solution)/shard_map/ppermute | solution.py:234
  113.4 53.5 %collective-permute-done.7 = f32[1024,256]{1,0:T(8,128)} collective-permute-done((f32[1024,256]{1,0:T(8,128)}, f32[1024,256]{1,0:T(8,128)}, u32[]{:S(2)}, u32[]{:S(2)}) %collective-permute-start.7) | collective-permute-done | bytes 1048608 | tf_op jit(solution)/shard_map/ppermute | solution.py:27
  166.9 1.4 select_select_fusion.1.refs_0_
  169.5 2.1 collective-permute-start.12
  172.8 1.6 collective-permute-start.11
  174.5 6.3 %collective-permute-done.17.refs_1_ = f32[1024,256]{1,0:T(8,128)} collective-permute-done((f32[1024,256]{1,0:T(8,128)S(1)}, f32[1024,256]{1,0:T(8,128)}, u32[]{:S(2)}, u32[]{:S(2)}) %collective-permute-start.17) | collective-permute-done | bytes 1048608 | tf_op jit(solution)/shard_map/ppermute | solution.py:234
  180.8 2.9 collective-permute-start.16
  183.7 8.3 %collective-permute-done.15.refs_3_ = f32[1024,256]{1,0:T(8,128)S(1)} collective-permute-done((f32[1024,256]{1,0:T(8,128)S(1)}, f32[1024,256]{1,0:T(8,128)S(1)}, u32[]{:S(2)}, u32[]{:S(2)}) %collective-permute-start.15) | collective-permute-done | bytes 1048608 | tf_op jit(solution)/shard_map/ppermute | solution.py:234
  195.0 8.3 %collective-permute-done.16.refs_2_ = f32[1024,256]{1,0:T(8,128)} collective-permute-done((f32[1024,256]{1,0:T(8,128)}, f32[1024,256]{1,0:T(8,128)}, u32[]{:S(2)}, u32[]{:S(2)}) %collective-permute-start.16) | collective-permute-done | bytes 1048608 | tf_op jit(solution)/shard_map/ppermute | solution.py:234
  203.4 39.9 %collective-permute-done.13 = f32[1024,256]{1,0:T(8,128)} collective-permute-done((f32[1024,256]{1,0:T(8,128)}, f32[1024,256]{1,0:T(8,128)}, u32[]{:S(2)}, u32[]{:S(2)}) %collective-permute-start.13) | collective-permute-done | bytes 1048608 | tf_op jit(solution)/shard_map/ppermute | solution.py:27
  247.0 22.0 %products.7 = f32[64,128,128]{2,1,0:T(8,128)} custom-call(s32[64]{0:T(128)S(1)} %fusion.14.table, s32[4]{0:T(128)S(1)} %fusion.15.which, f32[1024,256]{1,0:T(8,128)S(1)} %bitcast_multiply_fusion.2.refs_0_, f32[1024,256]{1,0:T(8,128)S(1)} %copy-done.1, f32[1024,256]{1,0:T(8,128)S(1)} %copy-done.3, f32[1024,256]{1,0:T(8,128)S(1)} %copy-done.5, ...), custom_call_target="tpu_custom_call" | custom-call | flops 12884901888 | bytes 16777216 | tf_op jit(solution)/shard_map/products/pallas_call | solution.py:108
  269.0 4.6 all-to-all-start.4
  273.6 1.3 collective-permute-start.19
  274.9 5.9 collective-permute-start.18
  283.3 1.8 select_select_fusion.refs_0_
  285.1 2.0 collective-permute-start.22
  291.4 39.4 %collective-permute-done.22.refs_1_ = f32[1024,256]{1,0:T(8,128)} collective-permute-done((f32[1024,256]{1,0:T(8,128)S(1)}, f32[1024,256]{1,0:T(8,128)}, u32[]{:S(2)}, u32[]{:S(2)}) %collective-permute-start.22) | collective-permute-done | bytes 1048608 | tf_op jit(solution)/shard_map/ppermute | solution.py:234
  330.8 11.3 %collective-permute-done.20.refs_3_ = f32[1024,256]{1,0:T(8,128)} collective-permute-done((f32[1024,256]{1,0:T(8,128)}, f32[1024,256]{1,0:T(8,128)}, u32[]{:S(2)}, u32[]{:S(2)}) %collective-permute-start.20) | collective-permute-done | bytes 1048608 | tf_op jit(solution)/shard_map/ppermute | solution.py:234
  342.1 11.2 %collective-permute-done.21.refs_2_ = f32[1024,256]{1,0:T(8,128)} collective-permute-done((f32[1024,256]{1,0:T(8,128)}, f32[1024,256]{1,0:T(8,128)}, u32[]{:S(2)}, u32[]{:S(2)}) %collective-permute-start.21) | collective-permute-done | bytes 1048608 | tf_op jit(solution)/shard_map/ppermute | solution.py:234
  353.4 22.5 %products.6 = f32[64,128,128]{2,1,0:T(8,128)} custom-call(s32[64]{0:T(128)S(1)} %fusion.11.table, s32[4]{0:T(128)S(1)} %fusion.12.which, f32[1024,256]{1,0:T(8,128)S(1)} %broadcast_select_fusion.refs_0_, f32[1024,256]{1,0:T(8,128)} %collective-permute-done.10.refs_1_, f32[1024,256]{1,0:T(8,128)} %collective-permute-done.16.refs_2_, ...), custom_call_target="tpu_custom_call" | custom-call | flops 12884901888 | bytes 16777216 | tf_op jit(solution)/shard_map/products/pallas_call | solution.py:108
  375.9 5.5 all-to-all-start.3
  382.7 2.0 collective-permute-start.23
  384.7 3.0 collective-permute-start.25
  391.0 48.1 %collective-permute-done.25.refs_3_ = f32[1024,256]{1,0:T(8,128)} collective-permute-done((f32[1024,256]{1,0:T(8,128)}, f32[1024,256]{1,0:T(8,128)}, u32[]{:S(2)}, u32[]{:S(2)}) %collective-permute-start.25) | collective-permute-done | bytes 1048608 | tf_op jit(solution)/shard_map/ppermute | solution.py:234
  439.1 11.2 %collective-permute-done.26.refs_2_ = f32[1024,256]{1,0:T(8,128)S(1)} collective-permute-done((f32[1024,256]{1,0:T(8,128)}, f32[1024,256]{1,0:T(8,128)S(1)}, u32[]{:S(2)}, u32[]{:S(2)}) %collective-permute-start.26) | collective-permute-done | bytes 1048608 | tf_op jit(solution)/shard_map/ppermute | solution.py:234
  450.3 23.6 %products.5 = f32[64,128,128]{2,1,0:T(8,128)} custom-call(s32[64]{0:T(128)S(1)} %fusion.8.table, s32[4]{0:T(128)S(1)} %fusion.9.which, f32[1024,256]{1,0:T(8,128)S(1)} %select_select_fusion.1.refs_0_, f32[1024,256]{1,0:T(8,128)} %collective-permute-done.17.refs_1_, f32[1024,256]{1,0:T(8,128)} %collective-permute-done.21.refs_2_, ...), custom_call_target="tpu_custom_call" | custom-call | flops 12884901888 | bytes 16777216 | tf_op jit(solution)/shard_map/products/pallas_call | solution.py:108
  474.0 4.6 all-to-all-start.2
  478.6 2.0 collective-permute-start.27
  480.6 2.7 collective-permute-start.28
  486.4 49.7 %collective-permute-done.28.refs_3_ = f32[1024,256]{1,0:T(8,128)S(1)} collective-permute-done((f32[1024,256]{1,0:T(8,128)S(1)}, f32[1024,256]{1,0:T(8,128)S(1)}, u32[]{:S(2)}, u32[]{:S(2)}) %collective-permute-start.28) | collective-permute-done | bytes 1048608 | tf_op jit(solution)/shard_map/ppermute | solution.py:234
  536.1 21.8 %products.4 = f32[64,128,128]{2,1,0:T(8,128)} custom-call(s32[64]{0:T(128)S(1)} %fusion.5.table, s32[4]{0:T(128)S(1)} %fusion.6.which, f32[1024,256]{1,0:T(8,128)S(1)} %select_select_fusion.refs_0_, f32[1024,256]{1,0:T(8,128)} %collective-permute-done.22.refs_1_, f32[1024,256]{1,0:T(8,128)S(1)} %collective-permute-done.26.refs_2_, ...), custom_call_target="tpu_custom_call" | custom-call | flops 12884901888 | bytes 16777216 | tf_op jit(solution)/shard_map/products/pallas_call | solution.py:108
  557.9 5.8 all-to-all-start.1
  565.6 9.6 %add_blocks.4.start = f32[128,128,128]{2,1,0:T(8,128)} custom-call(s32[64]{0:T(128)S(1)} %get-tuple-element.169.targets, f32[64,128,128]{2,1,0:T(8,128)} %all-to-all-done.4.got, f32[128,128,128]{2,1,0:T(8,128)} %bitcast.58), custom_call_target="tpu_custom_call" | custom-call | flops 1048576 | bytes 20971520 | tf_op jit(solution)/shard_map/add_blocks/pallas_call | solution.py:147
  575.3 9.5 %add_blocks.5.start = f32[128,128,128]{2,1,0:T(8,128)} custom-call(s32[64]{0:T(128)S(1)} %get-tuple-element.170.targets, f32[64,128,128]{2,1,0:T(8,128)} %all-to-all-done.3.got, f32[128,128,128]{2,1,0:T(8,128)} %add_blocks.4.start), custom_call_target="tpu_custom_call" | custom-call | flops 1048576 | bytes 20971520 | tf_op jit(solution)/shard_map/add_blocks/pallas_call | solution.py:147
  584.7 9.5 %add_blocks.6.start = f32[128,128,128]{2,1,0:T(8,128)} custom-call(s32[64]{0:T(128)S(1)} %get-tuple-element.171.targets, f32[64,128,128]{2,1,0:T(8,128)} %all-to-all-done.2.got, f32[128,128,128]{2,1,0:T(8,128)} %add_blocks.5.start), custom_call_target="tpu_custom_call" | custom-call | flops 1048576 | bytes 20971520 | tf_op jit(solution)/shard_map/add_blocks/pallas_call | solution.py:147
  594.2 18.8 %all-to-all-done.1.got = f32[64,128,128]{2,1,0:T(8,128)} async-done(((f32[64,128,128]{2,1,0:T(8,128)}), f32[64,128,128]{2,1,0:T(8,128)}, u32[]{:S(2)}, u32[]{:S(2)}) %all-to-all-start.1) | async-done | bytes 4194336 | tf_op jit(solution)/shard_map/all_to_all | solution.py:257
  613.0 9.6 %add_blocks.7 = f32[128,128,128]{2,1,0:T(8,128)} custom-call(s32[64]{0:T(128)S(1)} %get-tuple-element.172.targets, f32[64,128,128]{2,1,0:T(8,128)} %all-to-all-done.1.got, f32[128,128,128]{2,1,0:T(8,128)} %add_blocks.6.start), custom_call_target="tpu_custom_call" | custom-call | flops 1048576 | bytes 20971520 | tf_op jit(solution)/shard_map/add_blocks/pallas_call | solution.py:147
  (110 shorter events, 31.8 us)
Async XLA Ops:
  0.8 2.2 copy-start.6
  3.0 12.6 %copy-start.10 = (s32[8,2]{0,1:T(2,128)S(1)}, s32[8,2]{0,1:T(2,128)}, u32[]{:S(2)}) copy-start(s32[8,2]{0,1:T(2,128)} %param.20) | copy-start | bytes 196
  7.2 9.8 %copy-start.9 = (f32[1024,256]{1,0:T(8,128)S(1)}, f32[1024,256]{1,0:T(8,128)}, u32[]{:S(2)}) copy-start(f32[1024,256]{1,0:T(8,128)} %param.18) | copy-start | bytes 3145732
  7.2 79.8 %collective-permute-start.3 = (f32[256,2048]{1,0:T(8,128)}, f32[256,2048]{1,0:T(8,128)}, u32[]{:S(2)}, u32[]{:S(2)}) collective-permute-start(f32[256,2048]{1,0:T(8,128)} %get-tuple-element.150.refs_7_.refs_6_.refs_5_.refs_4_), channel_id=1, source_target_pairs={{8,0},{16,8},{24,16},{9,1},{17,9},{25,17},{10,2},{18,10},{26,18},{... | collective-permute-start | bytes 6291464 | tf_op jit(solution)/shard_map/ppermute | solution.py:27
  8.6 78.4 %collective-permute-start.1 = (f32[256,2048]{1,0:T(8,128)}, f32[256,2048]{1,0:T(8,128)}, u32[]{:S(2)}, u32[]{:S(2)}) collective-permute-start(f32[256,2048]{1,0:T(8,128)} %get-tuple-element.155.refs_12_), channel_id=1, source_target_pairs={{0,8},{8,16},{16,24},{1,9},{9,17},{17,25},{2,10},{10,18},{18,26},{... | collective-permute-start | bytes 6291464 | tf_op jit(solution)/shard_map/ppermute | solution.py:22
  15.7 9.2 %copy-start.11 = (s32[1,1,128]{2,1,0:T(1,128)S(1)}, s32[1,1,128]{2,1,0:T(1,128)}, u32[]{:S(2)}) copy-start(s32[1,1,128]{2,1,0:T(1,128)} %param.23) | copy-start | bytes 1540
  15.7 9.2 %copy-start.12 = (s32[1,1,128,1]{2,3,1,0:T(1,128)S(1)}, s32[1,1,128,1]{2,3,1,0:T(1,128)}, u32[]{:S(2)}) copy-start(s32[1,1,128,1]{2,3,1,0:T(1,128)} %param.22) | copy-start | bytes 1540
  15.7 14.3 %copy-start.18 = (s32[4]{0:T(128)S(1)}, s32[4]{0:T(128)}, u32[]{:S(2)}) copy-start(s32[4]{0:T(128)} %constant.102.clone) | copy-start | bytes 52
  17.2 86.3 %copy-start.17 = (s32[4]{0:T(128)S(1)}, s32[4]{0:T(128)}, u32[]{:S(2)}) copy-start(s32[4]{0:T(128)} %constant.103.clone) | copy-start | bytes 52
  17.2 69.8 %collective-permute-start.4 = (f32[1024,256]{1,0:T(8,128)S(1)}, f32[1024,256]{1,0:T(8,128)S(1)}, u32[]{:S(2)}, u32[]{:S(2)}) collective-permute-start(f32[1024,256]{1,0:T(8,128)S(1)} %bitcast_multiply_fusion.2.refs_0_), channel_id=1, source_target_pairs={{1,0},{2,1},{3,2},{4,3},{5,4},{6,5},{7,6},{0,7},{9,8},{10,9},{11,1... | collective-permute-start | bytes 3145736 | tf_op jit(solution)/shard_map/ppermute | solution.py:234
  19.0 68.0 %collective-permute-start.2 = (f32[1024,256]{1,0:T(8,128)S(1)}, f32[1024,256]{1,0:T(8,128)}, u32[]{:S(2)}, u32[]{:S(2)}) collective-permute-start(f32[1024,256]{1,0:T(8,128)S(1)} %bitcast_multiply_fusion.2.refs_0_), channel_id=1, source_target_pairs={{8,0},{16,8},{24,16},{9,1},{17,9},{25,17},{10,2},{18,10},{26,18},{... | collective-permute-start | bytes 3145736 | tf_op jit(solution)/shard_map/ppermute | solution.py:27
  20.3 66.8 %collective-permute-start = (f32[1024,256]{1,0:T(8,128)S(1)}, f32[1024,256]{1,0:T(8,128)S(1)}, u32[]{:S(2)}, u32[]{:S(2)}) collective-permute-start(f32[1024,256]{1,0:T(8,128)S(1)} %bitcast_multiply_fusion.2.refs_0_), channel_id=1, source_target_pairs={{0,8},{8,16},{16,24},{1,9},{9,17},{17,25},{2,10},{10,18},{18,26},{... | collective-permute-start | bytes 3145736 | tf_op jit(solution)/shard_map/ppermute | solution.py:22
  25.6 59.5 %all-to-all-start = ((s32[32,2,128]{2,1,0:T(2,128)}), s32[32,2,128]{2,1,0:T(2,128)S(1)}, u32[]{:S(2)}, u32[]{:S(2)}) async-start(s32[32,2,128]{2,1,0:T(2,128)} %broadcast_in_dim.47), calls=%async_computation | async-start | bytes 65536 | tf_op jit(solution)/shard_map/all_to_all | solution.py:164
  87.0 79.9 %copy-start = (f32[1024,256]{1,0:T(8,128)}, f32[1024,256]{1,0:T(8,128)S(1)}, u32[]{:S(2)}) copy-start(f32[1024,256]{1,0:T(8,128)S(1)} %collective-permute-done.4.refs_1_) | copy-start | bytes 3145732
  88.1 5.1 copy-start.8
  89.5 12.6 %collective-permute-start.10 = (f32[1024,256]{1,0:T(8,128)S(1)}, f32[1024,256]{1,0:T(8,128)}, u32[]{:S(2)}, u32[]{:S(2)}) collective-permute-start(f32[1024,256]{1,0:T(8,128)S(1)} %broadcast_select_fusion.refs_0_), channel_id=1, source_target_pairs={{1,0},{2,1},{3,2},{4,3},{5,4},{6,5},{7,6},{0,7},{9,8},{10,9},{11,1... | collective-permute-start | bytes 3145736 | tf_op jit(solution)/shard_map/ppermute | solution.py:234
  89.9 77.1 %collective-permute-start.6 = (f32[256,2048]{1,0:T(8,128)}, f32[256,2048]{1,0:T(8,128)}, u32[]{:S(2)}, u32[]{:S(2)}) collective-permute-start(f32[256,2048]{1,0:T(8,128)} %collective-permute-done.1.refs_11_.refs_10_), channel_id=1, source_target_pairs={{8,16},{16,24},{9,17},{17,25},{10,18},{18,26},{11,19},{19,27},{12,... | collective-permute-start | bytes 6291464 | tf_op jit(solution)/shard_map/ppermute | solution.py:22
  91.8 75.1 %collective-permute-start.8 = (f32[256,2048]{1,0:T(8,128)}, f32[256,2048]{1,0:T(8,128)}, u32[]{:S(2)}, u32[]{:S(2)}) collective-permute-start(f32[256,2048]{1,0:T(8,128)} %collective-permute-done.3.refs_8_.refs_7_.refs_6_.refs_5_), channel_id=1, source_target_pairs={{8,0},{16,8},{9,1},{17,9},{10,2},{18,10},{11,3},{19,11},{12,4},{20... | collective-permute-start | bytes 6291464 | tf_op jit(solution)/shard_map/ppermute | solution.py:27
  93.1 20.3 %collective-permute-start.5 = (f32[1024,256]{1,0:T(8,128)S(1)}, f32[1024,256]{1,0:T(8,128)}, u32[]{:S(2)}, u32[]{:S(2)}) collective-permute-start(f32[1024,256]{1,0:T(8,128)S(1)} %copy-done.8), channel_id=1, source_target_pairs={{8,16},{16,24},{9,17},{17,25},{10,18},{18,26},{11,19},{19,27},{12,... | collective-permute-start | bytes 3145736 | tf_op jit(solution)/shard_map/ppermute | solution.py:22
  94.8 18.6 %collective-permute-start.9 = (f32[1024,256]{1,0:T(8,128)S(1)}, f32[1024,256]{1,0:T(8,128)S(1)}, u32[]{:S(2)}, u32[]{:S(2)}) collective-permute-start(f32[1024,256]{1,0:T(8,128)S(1)} %collective-permute-done.4.refs_1_), channel_id=1, source_target_pairs={{1,0},{2,1},{3,2},{4,3},{5,4},{6,5},{7,6},{0,7},{9,8},{10,9},{11,1... | collective-permute-start | bytes 3145736 | tf_op jit(solution)/shard_map/ppermute | solution.py:234
  102.2 64.8 %collective-permute-start.7 = (f32[1024,256]{1,0:T(8,128)}, f32[1024,256]{1,0:T(8,128)}, u32[]{:S(2)}, u32[]{:S(2)}) collective-permute-start(f32[1024,256]{1,0:T(8,128)} %collective-permute-done.2), channel_id=1, source_target_pairs={{8,0},{16,8},{9,1},{17,9},{10,2},{18,10},{11,3},{19,11},{12,4},{20... | collective-permute-start | bytes 3145736 | tf_op jit(solution)/shard_map/ppermute | solution.py:27
  113.4 55.1 %copy-start.2 = (f32[1024,256]{1,0:T(8,128)}, f32[1024,256]{1,0:T(8,128)S(1)}, u32[]{:S(2)}) copy-start(f32[1024,256]{1,0:T(8,128)S(1)} %collective-permute-done.9.refs_2_) | copy-start | bytes 3145732
  168.4 12.4 %collective-permute-start.17 = (f32[1024,256]{1,0:T(8,128)S(1)}, f32[1024,256]{1,0:T(8,128)}, u32[]{:S(2)}, u32[]{:S(2)}) collective-permute-start(f32[1024,256]{1,0:T(8,128)S(1)} %select_select_fusion.1.refs_0_), channel_id=1, source_target_pairs={{1,0},{2,1},{3,2},{4,3},{5,4},{6,5},{7,6},{0,7},{9,8},{10,9},{11,1... | collective-permute-start | bytes 3145736 | tf_op jit(solution)/shard_map/ppermute | solution.py:234
  168.5 23.5 %collective-permute-start.15 = (f32[1024,256]{1,0:T(8,128)S(1)}, f32[1024,256]{1,0:T(8,128)S(1)}, u32[]{:S(2)}, u32[]{:S(2)}) collective-permute-start(f32[1024,256]{1,0:T(8,128)S(1)} %collective-permute-done.9.refs_2_), channel_id=1, source_target_pairs={{1,0},{2,1},{3,2},{4,3},{5,4},{6,5},{7,6},{0,7},{9,8},{10,9},{11,1... | collective-permute-start | bytes 3145736 | tf_op jit(solution)/shard_map/ppermute | solution.py:234
  169.5 73.8 %collective-permute-start.12 = (f32[256,2048]{1,0:T(8,128)}, f32[256,2048]{1,0:T(8,128)}, u32[]{:S(2)}, u32[]{:S(2)}) collective-permute-start(f32[256,2048]{1,0:T(8,128)} %collective-permute-done.6.refs_11_.refs_10_.refs_9_), channel_id=1, source_target_pairs={{16,24},{17,25},{18,26},{19,27},{20,28},{21,29},{22,30},{23,31}} | collective-permute-start | bytes 6291464 | tf_op jit(solution)/shard_map/ppermute | solution.py:22
  171.6 71.8 %collective-permute-start.14 = (f32[256,2048]{1,0:T(8,128)}, f32[256,2048]{1,0:T(8,128)}, u32[]{:S(2)}, u32[]{:S(2)}) collective-permute-start(f32[256,2048]{1,0:T(8,128)} %collective-permute-done.8.refs_9_.refs_8_.refs_7_.refs_6_), channel_id=1, source_target_pairs={{8,0},{9,1},{10,2},{11,3},{12,4},{13,5},{14,6},{15,7}} | collective-permute-start | bytes 6291464 | tf_op jit(solution)/shard_map/ppermute | solution.py:27
  172.8 30.5 %collective-permute-start.11 = (f32[1024,256]{1,0:T(8,128)}, f32[1024,256]{1,0:T(8,128)}, u32[]{:S(2)}, u32[]{:S(2)}) collective-permute-start(f32[1024,256]{1,0:T(8,128)} %collective-permute-done.5), channel_id=1, source_target_pairs={{16,24},{17,25},{18,26},{19,27},{20,28},{21,29},{22,30},{23,31}} | collective-permute-start | bytes 3145736 | tf_op jit(solution)/shard_map/ppermute | solution.py:22
  180.8 22.6 %collective-permute-start.16 = (f32[1024,256]{1,0:T(8,128)}, f32[1024,256]{1,0:T(8,128)}, u32[]{:S(2)}, u32[]{:S(2)}) collective-permute-start(f32[1024,256]{1,0:T(8,128)} %collective-permute-done.10.refs_1_), channel_id=1, source_target_pairs={{1,0},{2,1},{3,2},{4,3},{5,4},{6,5},{7,6},{0,7},{9,8},{10,9},{11,1... | collective-permute-start | bytes 3145736 | tf_op jit(solution)/shard_map/ppermute | solution.py:234
  193.0 50.3 %collective-permute-start.13 = (f32[1024,256]{1,0:T(8,128)}, f32[1024,256]{1,0:T(8,128)}, u32[]{:S(2)}, u32[]{:S(2)}) collective-permute-start(f32[1024,256]{1,0:T(8,128)} %collective-permute-done.7), channel_id=1, source_target_pairs={{8,0},{9,1},{10,2},{11,3},{12,4},{13,5},{14,6},{15,7}} | collective-permute-start | bytes 3145736 | tf_op jit(solution)/shard_map/ppermute | solution.py:27
  269.0 11.8 %copy-start.16 = (s32[4]{0:T(128)S(1)}, s32[4]{0:T(128)}, u32[]{:S(2)}) copy-start(s32[4]{0:T(128)} %constant.104.clone) | copy-start | bytes 52
  269.0 106.9 %all-to-all-start.4 = ((f32[64,128,128]{2,1,0:T(8,128)}), f32[64,128,128]{2,1,0:T(8,128)}, u32[]{:S(2)}, u32[]{:S(2)}) async-start(f32[64,128,128]{2,1,0:T(8,128)} %products.7), calls=%async_computation.4 | async-start | bytes 8388608 | tf_op jit(solution)/shard_map/all_to_all | solution.py:257
  273.6 79.8 %collective-permute-start.19 = (f32[256,2048]{1,0:T(8,128)}, f32[256,2048]{1,0:T(8,128)}, u32[]{:S(2)}, u32[]{:S(2)}) collective-permute-start(f32[256,2048]{1,0:T(8,128)} %get-tuple-element.155.refs_12_), channel_id=1, source_target_pairs={{8,0},{16,8},{9,1},{17,9},{10,2},{18,10},{11,3},{19,11},{12,4},{20... | collective-permute-start | bytes 6291464 | tf_op jit(solution)/shard_map/ppermute | solution.py:27
  274.9 78.5 %collective-permute-start.18 = (f32[256,2048]{1,0:T(8,128)}, f32[256,2048]{1,0:T(8,128)}, u32[]{:S(2)}, u32[]{:S(2)}) collective-permute-start(f32[256,2048]{1,0:T(8,128)} %get-tuple-element.150.refs_7_.refs_6_.refs_5_.refs_4_), channel_id=1, source_target_pairs={{0,8},{8,16},{16,24},{1,9},{9,17},{17,25},{2,10},{10,18},{18,26},{... | collective-permute-start | bytes 6291464 | tf_op jit(solution)/shard_map/ppermute | solution.py:22
  283.3 4.9 copy-start.15
  285.1 45.7 %collective-permute-start.22 = (f32[1024,256]{1,0:T(8,128)S(1)}, f32[1024,256]{1,0:T(8,128)}, u32[]{:S(2)}, u32[]{:S(2)}) collective-permute-start(f32[1024,256]{1,0:T(8,128)S(1)} %select_select_fusion.refs_0_), channel_id=1, source_target_pairs={{1,0},{2,1},{3,2},{4,3},{5,4},{6,5},{7,6},{0,7},{9,8},{10,9},{11,1... | collective-permute-start | bytes 3145736 | tf_op jit(solution)/shard_map/ppermute | solution.py:234
  287.2 55.0 %collective-permute-start.20 = (f32[1024,256]{1,0:T(8,128)}, f32[1024,256]{1,0:T(8,128)}, u32[]{:S(2)}, u32[]{:S(2)}) collective-permute-start(f32[1024,256]{1,0:T(8,128)} %collective-permute-done.16.refs_2_), channel_id=1, source_target_pairs={{1,0},{2,1},{3,2},{4,3},{5,4},{6,5},{7,6},{0,7},{9,8},{10,9},{11,1... | collective-permute-start | bytes 3145736 | tf_op jit(solution)/shard_map/ppermute | solution.py:234
  288.1 65.3 %collective-permute-start.21 = (f32[1024,256]{1,0:T(8,128)}, f32[1024,256]{1,0:T(8,128)}, u32[]{:S(2)}, u32[]{:S(2)}) collective-permute-start(f32[1024,256]{1,0:T(8,128)} %collective-permute-done.17.refs_1_), channel_id=1, source_target_pairs={{1,0},{2,1},{3,2},{4,3},{5,4},{6,5},{7,6},{0,7},{9,8},{10,9},{11,1... | collective-permute-start | bytes 3145736 | tf_op jit(solution)/shard_map/ppermute | solution.py:234
  375.9 11.9 %copy-start.14 = (s32[4]{0:T(128)S(1)}, s32[4]{0:T(128)}, u32[]{:S(2)}) copy-start(s32[4]{0:T(128)} %constant.109.clone) | copy-start | bytes 52
  375.9 98.1 %all-to-all-start.3 = ((f32[64,128,128]{2,1,0:T(8,128)}), f32[64,128,128]{2,1,0:T(8,128)}, u32[]{:S(2)}, u32[]{:S(2)}) async-start(f32[64,128,128]{2,1,0:T(8,128)} %products.6), calls=%async_computation.3 | async-start | bytes 8388608 | tf_op jit(solution)/shard_map/all_to_all | solution.py:257
  381.4 68.9 %collective-permute-start.24 = (f32[256,2048]{1,0:T(8,128)}, f32[256,2048]{1,0:T(8,128)}, u32[]{:S(2)}, u32[]{:S(2)}) collective-permute-start(f32[256,2048]{1,0:T(8,128)} %collective-permute-done.19.refs_13_), channel_id=1, source_target_pairs={{8,0},{9,1},{10,2},{11,3},{12,4},{13,5},{14,6},{15,7}} | collective-permute-start | bytes 6291464 | tf_op jit(solution)/shard_map/ppermute | solution.py:27
  382.7 67.6 %collective-permute-start.23 = (f32[256,2048]{1,0:T(8,128)}, f32[256,2048]{1,0:T(8,128)}, u32[]{:S(2)}, u32[]{:S(2)}) collective-permute-start(f32[256,2048]{1,0:T(8,128)} %collective-permute-done.18.refs_6_.refs_5_.refs_4_), channel_id=1, source_target_pairs={{8,16},{16,24},{9,17},{17,25},{10,18},{18,26},{11,19},{19,27},{12,... | collective-permute-start | bytes 6291464 | tf_op jit(solution)/shard_map/ppermute | solution.py:22
  384.7 54.4 %collective-permute-start.25 = (f32[1024,256]{1,0:T(8,128)}, f32[1024,256]{1,0:T(8,128)}, u32[]{:S(2)}, u32[]{:S(2)}) collective-permute-start(f32[1024,256]{1,0:T(8,128)} %collective-permute-done.21.refs_2_), channel_id=1, source_target_pairs={{1,0},{2,1},{3,2},{4,3},{5,4},{6,5},{7,6},{0,7},{9,8},{10,9},{11,1... | collective-permute-start | bytes 3145736 | tf_op jit(solution)/shard_map/ppermute | solution.py:234
  387.7 62.6 %collective-permute-start.26 = (f32[1024,256]{1,0:T(8,128)}, f32[1024,256]{1,0:T(8,128)S(1)}, u32[]{:S(2)}, u32[]{:S(2)}) collective-permute-start(f32[1024,256]{1,0:T(8,128)} %collective-permute-done.22.refs_1_), channel_id=1, source_target_pairs={{1,0},{2,1},{3,2},{4,3},{5,4},{6,5},{7,6},{0,7},{9,8},{10,9},{11,1... | collective-permute-start | bytes 3145736 | tf_op jit(solution)/shard_map/ppermute | solution.py:234
  473.9 9.3 %copy-start.13 = (s32[4]{0:T(128)S(1)}, s32[4]{0:T(128)}, u32[]{:S(2)}) copy-start(s32[4]{0:T(128)} %constant.111.clone) | copy-start | bytes 52
  474.0 84.0 %all-to-all-start.2 = ((f32[64,128,128]{2,1,0:T(8,128)}), f32[64,128,128]{2,1,0:T(8,128)}, u32[]{:S(2)}, u32[]{:S(2)}) async-start(f32[64,128,128]{2,1,0:T(8,128)} %products.5), calls=%async_computation.2 | async-start | bytes 8388608 | tf_op jit(solution)/shard_map/all_to_all | solution.py:257
  478.6 57.6 %collective-permute-start.27 = (f32[256,2048]{1,0:T(8,128)}, f32[256,2048]{1,0:T(8,128)}, u32[]{:S(2)}, u32[]{:S(2)}) collective-permute-start(f32[256,2048]{1,0:T(8,128)} %collective-permute-done.23.refs_5_.refs_4_), channel_id=1, source_target_pairs={{16,24},{17,25},{18,26},{19,27},{20,28},{21,29},{22,30},{23,31}} | collective-permute-start | bytes 6291464 | tf_op jit(solution)/shard_map/ppermute | solution.py:22
  480.6 55.6 %collective-permute-start.28 = (f32[1024,256]{1,0:T(8,128)S(1)}, f32[1024,256]{1,0:T(8,128)S(1)}, u32[]{:S(2)}, u32[]{:S(2)}) collective-permute-start(f32[1024,256]{1,0:T(8,128)S(1)} %collective-permute-done.26.refs_2_), channel_id=1, source_target_pairs={{1,0},{2,1},{3,2},{4,3},{5,4},{6,5},{7,6},{0,7},{9,8},{10,9},{11,1... | collective-permute-start | bytes 3145736 | tf_op jit(solution)/shard_map/ppermute | solution.py:234
  557.9 55.0 %all-to-all-start.1 = ((f32[64,128,128]{2,1,0:T(8,128)}), f32[64,128,128]{2,1,0:T(8,128)}, u32[]{:S(2)}, u32[]{:S(2)}) async-start(f32[64,128,128]{2,1,0:T(8,128)} %products.4), calls=%async_computation.1 | async-start | bytes 8388608 | tf_op jit(solution)/shard_map/all_to_all | solution.py:257
  (5 other events, 5.7 us)

commit v3 on v1

v3 whole, which is shorter than its diff:
```python
import functools

import jax
import jax.numpy as jnp
import numpy as np
from jax import lax
from jax.experimental import pallas as pl
from jax.experimental.pallas import tpu as pltpu
from jax.sharding import PartitionSpec as P

BLK = 128
TICKS = 4
PARTS = 2
ABREAST = 8
VMEM_LIMIT = 48 * 1024 * 1024


def widen(occupancy, panel):
    return panel * jnp.repeat(jnp.repeat(occupancy.astype(jnp.float32), BLK, axis=0), BLK, axis=1)


def up_step(value, sources, step, n_row):
    pairs = [(b + step - 1, b + step) for b in sources if b + step < n_row]
    return lax.ppermute(value, "row", pairs) if pairs else None


def down_step(value, sources, step):
    pairs = [(b - step + 1, b - step) for b in sources if b - step >= 0]
    return lax.ppermute(value, "row", pairs) if pairs else None


def visit_order(n_row):
    return [sorted(range(n_row), key=lambda i: (abs(i - r), i < r)) for r in range(n_row)]


def image_key(row, inner, n_row):
    source, kind = inner % n_row, "XY"[inner // n_row]
    return (kind, source - row)


def split(value):
    high = value.astype(jnp.bfloat16)
    low = (value - high.astype(jnp.float32)).astype(jnp.bfloat16)
    return high, low


def product_kernel(place, choices, table, full, used, which, *refs):
    count = len(choices) * PARTS
    lefts = refs[:TICKS]
    rights = refs[TICKS : TICKS + count]
    out = refs[TICKS + count]
    left_in, right_in, left_two, right_two, left_sem, right_sem = refs[TICKS + count + 1 :]
    inner = right_in.shape[1]
    q_blocks = right_in.shape[2] // BLK

    def left_copy(t):
        return pltpu.make_async_copy(lefts[t].at[place], left_in.at[t], left_sem.at[t])

    for t in range(TICKS):
        left_copy(t).start()
        for position, ticks in enumerate(choices):
            of_image = rights[position * PARTS : (position + 1) * PARTS]
            if t in ticks:

                @pl.when(which[t] == position)
                def _():
                    for part, ref in enumerate(of_image):
                        rows = pl.ds(part * ref.shape[0], ref.shape[0])
                        pltpu.make_async_copy(ref, right_in.at[t, rows], right_sem.at[t]).start()

    for t in range(TICKS):
        left_copy(t).wait()
        pltpu.make_async_copy(right_in.at[t], right_in.at[t], right_sem.at[t]).wait()
        cols = pl.ds(t * inner, inner)

        @pl.loop(0, left_in.shape[1] // BLK)
        def _(p):
            rows = pl.ds(pl.multiple_of(p * BLK, BLK), BLK)
            high, low = split(left_in[t, rows, :])
            left_two[pl.ds(pl.multiple_of(p * 2 * BLK, 2 * BLK), BLK), cols] = high
            left_two[pl.ds(pl.multiple_of(p * 2 * BLK + BLK, BLK), BLK), cols] = low

        @pl.loop(0, inner // 32)
        def _(p):
            rows = pl.ds(pl.multiple_of(p * 32, 32), 32)
            to = pl.ds(pl.multiple_of(t * inner + p * 32, 32), 32)
            for q in range(q_blocks):
                high, low = split(right_in[t, rows, q * BLK : (q + 1) * BLK])
                right_two[to, 2 * q * BLK : (2 * q + 1) * BLK] = high
                right_two[to, (2 * q + 1) * BLK : (2 * q + 2) * BLK] = low

    def one(slot):
        block = jnp.maximum(table[slot], 0)
        rows = pl.ds(pl.multiple_of((block // q_blocks) * 2 * BLK, 2 * BLK), 2 * BLK)
        cols = pl.ds(pl.multiple_of((block % q_blocks) * 2 * BLK, 2 * BLK), 2 * BLK)
        four = jnp.dot(left_two[rows, :], right_two[:, cols], preferred_element_type=jnp.float32)
        out[slot] = (four[:BLK, :BLK] + (four[:BLK, BLK:] + four[BLK:, :BLK])) + four[BLK:, BLK:]

    @pl.loop(0, (used[0] + ABREAST - 1) // ABREAST)
    def _(turn):
        for extra in range(ABREAST):
            one(full[turn * ABREAST + extra])


def products(slots_used, which, lefts, rights, choices, place, slots):
    rows, inner = lefts[0].shape[-2:]
    cols = rights[0][0].shape[1]
    rights = [part for of_image in rights for part in of_image]
    smem = pl.BlockSpec(memory_space=pltpu.SMEM)
    hbm = pl.BlockSpec(memory_space=pl.ANY)
    deep = TICKS * inner
    return pl.pallas_call(
        functools.partial(product_kernel, place, choices),
        out_shape=jax.ShapeDtypeStruct((slots, BLK, BLK), jnp.float32),
        in_specs=[smem] * 4 + [hbm] * (TICKS + len(rights)),
        out_specs=pl.BlockSpec(memory_space=pltpu.VMEM),
        scratch_shapes=[
            pltpu.VMEM((TICKS, rows, inner), jnp.float32),
            pltpu.VMEM((TICKS, inner, cols), jnp.float32),
            pltpu.VMEM((2 * rows, deep), jnp.bfloat16),
            pltpu.VMEM((deep, 2 * cols), jnp.bfloat16),
            pltpu.SemaphoreType.DMA((TICKS,)),
            pltpu.SemaphoreType.DMA((TICKS,)),
        ],
        compiler_params=pltpu.CompilerParams(vmem_limit_bytes=VMEM_LIMIT),
        cost_estimate=pl.CostEstimate(
            flops=2 * 6 * slots * BLK * BLK * deep,
            bytes_accessed=4 * (deep * (rows + cols) + slots * BLK * BLK),
            transcendentals=0,
        ),
        name="products",
    )(*slots_used, which, *lefts, *rights)


def add_kernel(targets, leader, got, start, out, got_in, total, got_sem, start_sem, out_sem):
    slots = got.shape[0]

    def got_copy(slot):
        return pltpu.make_async_copy(got.at[slot], got_in.at[slot], got_sem.at[slot])

    def start_copy(slot):
        return pltpu.make_async_copy(out.at[targets[slot]], total.at[slot], start_sem.at[slot])

    def out_copy(slot):
        return pltpu.make_async_copy(total.at[slot], out.at[targets[slot]], out_sem.at[slot])

    def every(leads, work):
        @pl.loop(0, slots)
        def _(slot):
            there = targets[slot] >= 0
            if leads:
                there = jnp.logical_and(there, leader[slot] == slot)

            @pl.when(there)
            def _():
                work(slot)

    every(True, lambda slot: start_copy(slot).start())
    every(False, lambda slot: got_copy(slot).start())
    every(True, lambda slot: start_copy(slot).wait())

    def add(slot):
        got_copy(slot).wait()
        total[leader[slot]] = total[leader[slot]] + got_in[slot]

    every(False, add)
    every(True, lambda slot: out_copy(slot).start())
    every(True, lambda slot: out_copy(slot).wait())


def add_blocks(targets, leader, got, start):
    smem = pl.BlockSpec(memory_space=pltpu.SMEM)
    hbm = pl.BlockSpec(memory_space=pl.ANY)
    slots = got.shape[0]
    return pl.pallas_call(
        add_kernel,
        out_shape=jax.ShapeDtypeStruct(start.shape, jnp.float32),
        in_specs=[smem, smem, hbm, hbm],
        out_specs=hbm,
        input_output_aliases={3: 0},
        scratch_shapes=[
            pltpu.VMEM(got.shape, jnp.float32),
            pltpu.VMEM(got.shape, jnp.float32),
            pltpu.SemaphoreType.DMA((slots,)),
            pltpu.SemaphoreType.DMA((slots,)),
            pltpu.SemaphoreType.DMA((slots,)),
        ],
        compiler_params=pltpu.CompilerParams(vmem_limit_bytes=VMEM_LIMIT),
        cost_estimate=pl.CostEstimate(
            flops=got.size, bytes_accessed=4 * 3 * got.size, transcendentals=0
        ),
        name="add_blocks",
    )(targets, leader, got, start)


def first_kernel(targets, got, start, out):
    out[...] = start[...]

    @pl.loop(0, got.shape[0])
    def _(slot):
        target = targets[slot]

        @pl.when(target >= 0)
        def _():
            out[target] = out[target] + got[slot]


def first_blocks(targets, got, start):
    vmem = pl.BlockSpec(memory_space=pltpu.VMEM)
    return pl.pallas_call(
        first_kernel,
        out_shape=jax.ShapeDtypeStruct(start.shape, jnp.float32),
        in_specs=[pl.BlockSpec(memory_space=pltpu.SMEM), vmem, vmem],
        out_specs=vmem,
        compiler_params=pltpu.CompilerParams(vmem_limit_bytes=VMEM_LIMIT),
        cost_estimate=pl.CostEstimate(
            flops=got.size, bytes_accessed=4 * (got.size + 2 * start.size), transcendentals=0
        ),
        name="first_blocks",
    )(targets, got, start)


def tables(every, n_row, n_col, capacity):
    row, col = lax.axis_index("row"), lax.axis_index("col")
    count = every.shape[-1]
    every = every.reshape(n_row, n_col, 2, count)
    places = jnp.arange(capacity, dtype=jnp.int32)

    def spread(match, values):
        rank = jnp.cumsum(match.astype(jnp.int32), axis=-1) - 1
        hit = match[..., None, :] & (rank[..., None, :] == places[:, None])
        return jnp.max(jnp.where(hit, values[..., None, :], -1), axis=-1)

    column = lax.dynamic_index_in_dim(every[:, :, 0], col, axis=1, keepdims=False)
    owners = row * n_col + jnp.arange(n_col, dtype=jnp.int32)
    numbers = jnp.arange(count, dtype=jnp.int32)
    sent = spread(
        column[:, None, :] == owners[None, :, None],
        jnp.broadcast_to(numbers, (n_row, n_col, count)),
    )
    got = spread(every[:, :, 0] == row * n_col + col, every[:, :, 1])
    sent, got = (value.reshape(n_row, n_col * capacity) for value in (sent, got))
    slots = jnp.arange(n_col * capacity, dtype=jnp.int32)

    used = jnp.sum((sent >= 0).astype(jnp.int32), axis=-1, keepdims=True)
    rank = jnp.cumsum((sent >= 0).astype(jnp.int32), axis=-1)
    wanted = jnp.minimum(slots + 1, used)
    full = jnp.argmax(rank[:, None, :] >= wanted[..., None], axis=-1).astype(jnp.int32)
    leader = jnp.argmax(got[:, :, None] == got[:, None, :], axis=-1).astype(jnp.int32)
    return {"sent": sent, "full": full, "used": used, "got": got, "leader": leader}


def per_device(a_panels, b_panels, a_occupancy, b_occupancy, owner_device, owner_block, c_previous):
    n_row = lax.axis_size("row")
    n_col = lax.axis_size("col")
    row, col = lax.axis_index("row"), lax.axis_index("col")
    images = n_col // n_row
    inner = b_panels.shape[0] // images
    count_blocks = owner_block.size
    capacity = max(2, (2 * count_blocks + n_row * n_col - 1) // (n_row * n_col))
    order = visit_order(n_row)
    every_row = list(range(n_row))
    early = list(range(TICKS - 1))
    backward = [((c + 1) % n_col, c) for c in range(n_col)]

    def image(number, part):
        depth = inner // PARTS
        start = (row + col + number * n_row) % n_col // n_row * inner + part * depth
        present = lax.dynamic_slice_in_dim(b_occupancy, start // BLK, depth // BLK, 0)
        return widen(present, lax.dynamic_slice_in_dim(b_panels, start, depth, 0))

    held = {("A", 0, 0): widen(a_occupancy, a_panels)}
    for part in range(PARTS):
        held["Y", part, 0] = image(1, part)
        held["X", part, 0] = image(0, part)
    mine = jnp.stack([owner_device.reshape(-1), owner_block.reshape(-1)])
    held["owners"] = jnp.broadcast_to(mine, (n_row * n_col,) + mine.shape)

    first = [(("A", 0, -d), ("A", 0, d)) for d in range(1, n_row)]
    lower = [(("Y", part, -d), ("X", part, d)) for d in range(1, n_row) for part in range(PARTS)]
    steps = []
    for number in range(max(len(first), len(lower))):
        steps += first[number : number + 1] + lower[number : number + 1]
    steps += [(("X", part, -d), ("Y", part, d)) for d in range(1, n_row) for part in range(PARTS)]
    ends = {keys[0]: number for number, keys in enumerate(steps)}

    def relay(key):
        kind, part, offset = key
        sources = early if kind == "Y" else every_row
        if offset < 0:
            return up_step(held[kind, part, offset + 1], sources, -offset, n_row)
        if (kind, part, offset - 1) in held:
            return down_step(held[kind, part, offset - 1], sources, offset)

    def close(due):
        held.update(due)
        held.update(zip(list(held), lax.optimization_barrier(tuple(held.values()))))

    def chosen(step):
        offsets = [order[r][step] - r for r in range(n_row)]
        kinds = sorted(set(offsets))
        index = jnp.asarray([kinds.index(o) for o in offsets], jnp.int32)[row]
        cases = [held["A", 0, k] for k in kinds]
        return lax.select_n(index if len(cases) > 2 else index == 1, *cases)

    def product(step):
        keys = [
            [image_key(r, order[r][step] + t, n_row) for t in range(TICKS)] for r in range(n_row)
        ]
        names = sorted({key for of_row in keys for key in of_row})
        choices = [
            {t for r in range(n_row) for t in range(TICKS) if keys[r][t] == name} for name in names
        ]
        index = [[names.index(key) for key in of_row] for of_row in keys]
        which = jnp.asarray(index, jnp.int32)[row]
        visit = jnp.asarray([order[r][step] for r in range(n_row)], jnp.int32)[row]
        return products(
            [held[name][visit] for name in ("sent", "full", "used")],
            which,
            [held["own" if step == 0 else "rest", t] for t in range(TICKS)],
            [[held[kind, part, offset] for part in range(PARTS)] for kind, offset in names],
            choices,
            max(step - 1, 0),
            n_col * capacity,
        )

    def exchange(step, total):
        visit = jnp.asarray([order[r][step] for r in range(n_row)], jnp.int32)[row]
        blocks = held["blocks", step]
        arrived = lax.all_to_all(blocks, "col", split_axis=0, concat_axis=0, tiled=True)
        targets, leader = held["got"][visit], held["leader"][visit]
        if step == 0:
            return first_blocks(targets, arrived, total)
        return add_blocks(targets, leader, arrived, total)

    held["own", 0] = held["A", 0, 0][None]
    start_of = {ends["Y", PARTS - 1, -(n_row - 1)] + 2: 0}
    for d in range(1, n_row):
        start_of[ends["X", PARTS - 1, -d] + 2] = d
    total = c_previous.reshape(c_previous.shape[2:])
    flying = {2: {}, 3: {}, 4: {}}
    for number in range(len(steps) + 2):
        if number >= 2:
            close(flying.pop(number))
        if number == 2:
            every = lax.all_to_all(held["owners"], ("row", "col"), 0, 0, tiled=True)
            flying[number + 2]["every"] = every
        if number == 4:
            flying[number + 1].update(tables(held["every"], n_row, n_col, capacity))
        if number - 1 in start_of:
            total = exchange(start_of[number - 1], total)
        if number < len(steps):
            moving = {key: relay(key) for key in steps[number]}
            flying.setdefault(number + 2, {}).update(
                {key: value for key, value in moving.items() if value is not None}
            )
        for name in ("own", "rest"):
            if name == "rest" and number == ends["A", 0, 1 - n_row] + 2:
                held["rest", 0] = jnp.stack([chosen(step) for step in range(1, n_row)])
            ahead = [t for t in range(1, TICKS) if (name, t) not in held]
            if ahead and (name, ahead[0] - 1) in held and not any(
                (name, ahead[0]) in of_step for of_step in flying.values()
            ):
                hop = lax.ppermute(held[name, ahead[0] - 1], "col", backward)
                flying.setdefault(number + 2, {})[name, ahead[0]] = hop
        if number in start_of:
            flying.setdefault(number + 1, {})["blocks", start_of[number]] = product(start_of[number])
    for due in flying.values():
        held.update(due)
    total = exchange(n_row - 1, total)
    return total.reshape(c_previous.shape)


def solution(mesh):
    in_specs = (
        P("row", "col"),
        P("row", "col"),
        P("row", "col"),
        P("row", "col"),
        P("row", "col", None, None),
        P("row", "col", None),
        P("row", "col", None, None, None),
    )
    out_specs = P("row", "col", None, None, None)
    return jax.shard_map(
        per_device, mesh=mesh, in_specs=in_specs, out_specs=out_specs, check_vma=False
    )
```

time: 586 us -> 488 us (0.83)
  blocking collectives: 73.9 us -> 0 us
  Pallas kernels: 122 us -> 89 us
  starting transfers between devices: 58.3 us -> 81.8 us
  waiting for transfers between devices: 296 us -> 276 us
    all_gather x1 -> x0, blocking collectives: 73.9 us -> none  [tables(): every = lax.all_gather(mine, ('row', 'col'))]
    ppermute x8 -> x13, waiting for transfers between devices: 228 us -> 170 us  [down_step(): return lax.ppermute(value, 'row', pairs) if pairs else None]
    all_to_all x4 -> x5, waiting for transfers between devices: 45.9 us -> 82.3 us  [the longest x4 62.2 us: exchange(): lax.all_to_all(blocks, 'col', split_axis=0, concat_axis=0, tiled=True)]
    pallas_call x4, Pallas kernels: 83.8 us -> 59.1 us  [products(): pl.pallas_call(functools.partial(product_kernel, place, choices), out_sha...]
    pallas_call x4 -> x3, Pallas kernels: 38.3 us -> 20.3 us  [add_blocks(): pl.pallas_call(add_kernel, out_shape=jax.ShapeDtypeStruct(start.shape, jn...]
    ppermute x9 -> x15, waiting for transfers between devices: 11.1 us -> 24.4 us  [up_step(): return lax.ppermute(value, 'row', pairs) if pairs else None]
    ppermute x6, waiting for transfers between devices: 11.5 us -> 0.02 us  [per_device(): hop = lax.ppermute(held[name, ahead[0] - 1], 'col', backward)]
    ppermute x9 -> x15, starting transfers between devices: 21.9 us -> 33.3 us  [up_step(): return lax.ppermute(value, 'row', pairs) if pairs else None]
  transfers between devices with their start and end apart: 27 -> 39, of which waited for: 11 -> 19; matrix products, arithmetic and copies ran while one was open for 2% -> 4% of each run, Pallas kernels for 19% -> 17%
where the time goes in v3:
time: 488 us; the launch traced here: 487 us
  waiting for transfers between devices  276 us (57%)
  Pallas kernels  89 us (18%)
  starting transfers between devices  81.8 us (17%)
  local copies, waits for them, and re-layouts  15 us (3%)
  other arithmetic  15 us (3%)
  between operations  9.96 us (2%)
    ppermute x13, waiting for transfers between devices, down_step(): return lax.ppermute(value, 'row', pairs) if pairs else None  170 us
    all_to_all x4, waiting for transfers between devices, exchange(): lax.all_to_all(blocks, 'col', split_axis=0, concat_axis=0, tiled=True)  62.2 us
    pallas_call x4, Pallas kernels, products(): pl.pallas_call(functools.partial(product_kernel, place, choices), out_sha...  59.1 us
    ppermute x15, starting transfers between devices, up_step(): return lax.ppermute(value, 'row', pairs) if pairs else None  33.3 us
    ppermute x15, waiting for transfers between devices, up_step(): return lax.ppermute(value, 'row', pairs) if pairs else None  24.4 us
    pallas_call x3, Pallas kernels, add_blocks(): pl.pallas_call(add_kernel, out_shape=jax.ShapeDtypeStruct(start.shape, jn...  20.3 us
    all_to_all x1, waiting for transfers between devices, per_device(): every = lax.all_to_all(held['owners'], ('row', 'col'), 0, 0, tiled=True)  20.1 us
    all_to_all x4, starting transfers between devices, exchange(): lax.all_to_all(blocks, 'col', split_axis=0, concat_axis=0, tiled=True)  18.5 us
  transfers between devices with their start and end apart: 39, of which 19 were waited for; matrix products, arithmetic and copies ran while one was open for 4% of the time, Pallas kernels for 17%

profile of v3, /device:TPU:0, one launch (start us, length us, event | category | flops | bytes accessed | tf_op | source)
XLA Modules:
  0.0 487.0 jit_solution(15278874837332332734)
XLA Ops:
  3.4 5.9 %collective-permute-start = (f32[1024,256]{1,0:T(8,128)S(1)}, f32[1024,256]{1,0:T(8,128)}, u32[]{:S(2)}, u32[]{:S(2)}) collective-permute-start(f32[1024,256]{1,0:T(8,128)S(1)} %bitcast_multiply_fusion), channel_id=1, source_target_pairs={{0,8},{8,16},{16,24},{1,9},{9,17},{17,25},{2,10},{10,18},{18,26},{... | collective-permute-start | bytes 3145736 | tf_op jit(solution)/shard_map/ppermute | solution.py:24
  10.6 1.7 collective-permute-start.2
  12.5 4.1 dynamic-slice_multiply_fusion
  16.6 5.2 %collective-permute-start.3 = (f32[128,2048]{1,0:T(8,128)}, f32[128,2048]{1,0:T(8,128)}, u32[]{:S(2)}, u32[]{:S(2)}) collective-permute-start(f32[128,2048]{1,0:T(8,128)} %get-tuple-element.713.refs_20_), channel_id=1, source_target_pairs={{0,8},{8,16},{16,24},{1,9},{9,17},{17,25},{2,10},{10,18},{18,26},{... | collective-permute-start | bytes 3145736 | tf_op jit(solution)/shard_map/ppermute | solution.py:24
  23.1 8.8 %collective-permute-done = f32[1024,256]{1,0:T(8,128)} collective-permute-done((f32[1024,256]{1,0:T(8,128)S(1)}, f32[1024,256]{1,0:T(8,128)}, u32[]{:S(2)}, u32[]{:S(2)}) %collective-permute-start) | collective-permute-done | bytes 1048608 | tf_op jit(solution)/shard_map/ppermute | solution.py:24
  31.9 5.5 %collective-permute-done.1 = f32[1024,256]{1,0:T(8,128)} collective-permute-done((f32[1024,256]{1,0:T(8,128)S(1)}, f32[1024,256]{1,0:T(8,128)}, u32[]{:S(2)}, u32[]{:S(2)}) %collective-permute-start.1) | collective-permute-done | bytes 1048608 | tf_op jit(solution)/shard_map/ppermute | solution.py:29
  38.0 1.7 collective-permute-start.5
  46.7 8.8 %all-to-all-start = ((s32[32,2,128]{2,1,0:T(2,128)}), s32[32,2,128]{2,1,0:T(2,128)S(1)}, u32[]{:S(2)}, u32[]{:S(2)}) async-start(s32[32,2,128]{2,1,0:T(2,128)} %broadcast_in_dim.90), calls=%async_computation | async-start | bytes 65536 | tf_op jit(solution)/shard_map/all_to_all | solution.py:346
  55.5 4.4 collective-permute-done.4.refs_6_.refs_8_.refs_10_.refs_12_
  59.9 3.5 collective-permute-start.8
  64.7 20.1 %all-to-all-done = s32[32,2,128]{2,1,0:T(2,128)S(1)} async-done(((s32[32,2,128]{2,1,0:T(2,128)}), s32[32,2,128]{2,1,0:T(2,128)S(1)}, u32[]{:S(2)}, u32[]{:S(2)}) %all-to-all-start) | async-done | bytes 32800 | tf_op jit(solution)/shard_map/all_to_all | solution.py:346
  88.2 1.7 collective-permute-start.10
  94.1 11.3 %collective-permute-done.9.refs_7_.refs_9_.refs_11_.refs_13_ = f32[128,2048]{1,0:T(8,128)} collective-permute-done((f32[128,2048]{1,0:T(8,128)S(1)}, f32[128,2048]{1,0:T(8,128)}, u32[]{:S(2)}, u32[]{:S(2)}) %collective-permute-start.9) | collective-permute-done | bytes 1048608 | tf_op jit(solution)/shard_map/ppermute | solution.py:29
  105.4 21.0 %collective-permute-done.11 = f32[1024,256]{1,0:T(8,128)} collective-permute-done((f32[1024,256]{1,0:T(8,128)}, f32[1024,256]{1,0:T(8,128)}, u32[]{:S(2)}, u32[]{:S(2)}) %collective-permute-start.11) | collective-permute-done | bytes 1048608 | tf_op jit(solution)/shard_map/ppermute | solution.py:29
  126.4 2.9 select_bitcast_fusion.1
  131.8 1.7 collective-permute-start.13
  134.8 1.7 collective-permute-start.15
  137.7 23.9 %collective-permute-done.14.refs_8_.refs_10_.refs_12_.refs_14_ = f32[128,2048]{1,0:T(8,128)S(1)} collective-permute-done((f32[128,2048]{1,0:T(8,128)}, f32[128,2048]{1,0:T(8,128)S(1)}, u32[]{:S(2)}, u32[]{:S(2)}) %collective-permute-start.14) | collective-permute-done | bytes 1048608 | tf_op jit(solution)/shard_map/ppermute | solution.py:29
  161.6 21.4 %collective-permute-done.16.refs_9_.refs_11_.refs_13_.refs_15_ = f32[128,2048]{1,0:T(8,128)} collective-permute-done((f32[128,2048]{1,0:T(8,128)}, f32[128,2048]{1,0:T(8,128)}, u32[]{:S(2)}, u32[]{:S(2)}) %collective-permute-start.16) | collective-permute-done | bytes 1048608 | tf_op jit(solution)/shard_map/ppermute | solution.py:29
  183.0 1.8 collective-permute-start.22
  184.8 1.7 collective-permute-start.18
  187.8 1.6 collective-permute-start.20
  191.4 23.1 %collective-permute-done.19.refs_10_.refs_12_.refs_14_.refs_16_ = f32[128,2048]{1,0:T(8,128)} collective-permute-done((f32[128,2048]{1,0:T(8,128)S(1)}, f32[128,2048]{1,0:T(8,128)}, u32[]{:S(2)}, u32[]{:S(2)}) %collective-permute-start.19) | collective-permute-done | bytes 1048608 | tf_op jit(solution)/shard_map/ppermute | solution.py:29
  217.3 19.8 %collective-permute-done.21.refs_11_.refs_13_.refs_15_.refs_17_ = f32[128,2048]{1,0:T(8,128)} collective-permute-done((f32[128,2048]{1,0:T(8,128)}, f32[128,2048]{1,0:T(8,128)}, u32[]{:S(2)}, u32[]{:S(2)}) %collective-permute-start.21) | collective-permute-done | bytes 1048608 | tf_op jit(solution)/shard_map/ppermute | solution.py:29
  237.7 15.1 %products.4 = f32[64,128,128]{2,1,0:T(8,128)} custom-call(s32[64]{0:T(128)S(1)} %fusion.10.table, s32[64]{0:T(128)S(1)} %fusion.11.full, s32[1]{0:T(128)} %bitcast.28.used, s32[4]{0:T(128)S(1)} %fusion.12.which, f32[1,1024,256]{2,1,0:T(8,128)S(1)} %bitcast.91, f32[1,1024,256]{2,1,0:T(8,128)} %collective-permute-done.2.refs_1_, ...), custom_call_target="tpu_custom_call" | custom-call | flops 12884901888 | bytes 16777216 | tf_op jit(solution)/shard_map/products/pallas_call | solution.py:112
  252.9 4.3 collective-permute-done.24.refs_22_
  257.2 4.6 all-to-all-start.4
  261.8 2.5 collective-permute-start.25
  270.7 15.6 %collective-permute-done.25.refs_5_.refs_7_.refs_9_ = f32[128,2048]{1,0:T(8,128)} collective-permute-done((f32[128,2048]{1,0:T(8,128)S(1)}, f32[128,2048]{1,0:T(8,128)}, u32[]{:S(2)}, u32[]{:S(2)}) %collective-permute-start.25) | collective-permute-done | bytes 1048608 | tf_op jit(solution)/shard_map/ppermute | solution.py:24
  286.3 6.2 %collective-permute-done.26.refs_23_ = f32[128,2048]{1,0:T(8,128)} collective-permute-done((f32[128,2048]{1,0:T(8,128)}, f32[128,2048]{1,0:T(8,128)}, u32[]{:S(2)}, u32[]{:S(2)}) %collective-permute-start.26) | collective-permute-done | bytes 1048608 | tf_op jit(solution)/shard_map/ppermute | solution.py:29
  293.1 13.7 %products.5 = f32[64,128,128]{2,1,0:T(8,128)} custom-call(s32[64]{0:T(128)S(1)} %fusion.13.table, s32[64]{0:T(128)S(1)} %fusion.14.full, s32[1]{0:T(128)} %bitcast.33.used, s32[4]{0:T(128)S(1)} %fusion.15.which, f32[3,1024,256]{2,1,0:T(8,128)} %copy-done.7, f32[3,1024,256]{2,1,0:T(8,128)} %collective-permute-done.17.refs_1_, ...), custom_call_target="tpu_custom_call" | custom-call | flops 12884901888 | bytes 16777216 | tf_op jit(solution)/shard_map/products/pallas_call | solution.py:112
  307.9 6.3 %collective-permute-done.29.refs_24_ = f32[128,2048]{1,0:T(8,128)} collective-permute-done((f32[128,2048]{1,0:T(8,128)}, f32[128,2048]{1,0:T(8,128)}, u32[]{:S(2)}, u32[]{:S(2)}) %collective-permute-start.29) | collective-permute-done | bytes 1048608 | tf_op jit(solution)/shard_map/ppermute | solution.py:29
  314.2 4.5 all-to-all-done.4.got
  318.7 4.6 all-to-all-start.3
  323.3 1.7 collective-permute-start.30
  330.2 22.4 %collective-permute-done.31.refs_25_ = f32[128,2048]{1,0:T(8,128)} collective-permute-done((f32[128,2048]{1,0:T(8,128)}, f32[128,2048]{1,0:T(8,128)}, u32[]{:S(2)}, u32[]{:S(2)}) %collective-permute-start.31) | collective-permute-done | bytes 1048608 | tf_op jit(solution)/shard_map/ppermute | solution.py:29
  353.2 15.1 %products.6 = f32[64,128,128]{2,1,0:T(8,128)} custom-call(s32[64]{0:T(128)S(1)} %fusion.16.table, s32[64]{0:T(128)S(1)} %fusion.17.full, s32[1]{0:T(128)} %bitcast.38.used, s32[4]{0:T(128)S(1)} %fusion.18.which, f32[3,1024,256]{2,1,0:T(8,128)} %copy-done.7, f32[3,1024,256]{2,1,0:T(8,128)} %collective-permute-done.17.refs_1_, ...), custom_call_target="tpu_custom_call" | custom-call | flops 12884901888 | bytes 16777216 | tf_op jit(solution)/shard_map/products/pallas_call | solution.py:112
  369.4 3.0 all-to-all-done.3.got
  372.4 4.8 all-to-all-start.2
  377.2 1.6 collective-permute-start.33
  382.5 15.1 %products.7 = f32[64,128,128]{2,1,0:T(8,128)} custom-call(s32[64]{0:T(128)S(1)} %fusion.22.table, s32[64]{0:T(128)S(1)} %fusion.23.full, s32[1]{0:T(128)} %bitcast.45.used, s32[4]{0:T(128)S(1)} %fusion.24.which, f32[3,1024,256]{2,1,0:T(8,128)} %copy-done.7, f32[3,1024,256]{2,1,0:T(8,128)} %collective-permute-done.17.refs_1_, ...), custom_call_target="tpu_custom_call" | custom-call | flops 12884901888 | bytes 16777216 | tf_op jit(solution)/shard_map/products/pallas_call | solution.py:112
  397.5 28.8 %all-to-all-done.2.got = f32[64,128,128]{2,1,0:T(8,128)} async-done(((f32[64,128,128]{2,1,0:T(8,128)}), f32[64,128,128]{2,1,0:T(8,128)}, u32[]{:S(2)}, u32[]{:S(2)}) %all-to-all-start.2) | async-done | bytes 4194336 | tf_op jit(solution)/shard_map/all_to_all | solution.py:330
  426.3 4.6 all-to-all-start.1
  431.0 9.6 %first_blocks.1.start = f32[128,128,128]{2,1,0:T(8,128)} custom-call(s32[64]{0:T(128)S(1)} %fusion.21.targets, f32[64,128,128]{2,1,0:T(8,128)} %all-to-all-done.4.got, f32[128,128,128]{2,1,0:T(8,128)} %bitcast.92), custom_call_target="tpu_custom_call" | custom-call | flops 1048576 | bytes 20971520 | tf_op jit(solution)/shard_map/first_blocks/pallas_call | solution.py:210
  440.7 6.8 %add_blocks.3.start = f32[128,128,128]{2,1,0:T(8,128)} custom-call(s32[64]{0:T(128)S(1)} %fusion.25.targets, s32[64]{0:T(128)S(1)} %fusion.28.leader, f32[64,128,128]{2,1,0:T(8,128)} %all-to-all-done.3.got, f32[128,128,128]{2,1,0:T(8,128)} %first_blocks.1.start), custom_call_target="tpu_custom_call", output_to_operand_aliasing={{}: (3, {})} | custom-call | flops 1048576 | bytes 12582912 | tf_op jit(solution)/shard_map/add_blocks/pallas_call | solution.py:175
  447.5 6.7 %add_blocks.4.start = f32[128,128,128]{2,1,0:T(8,128)} custom-call(s32[64]{0:T(128)S(1)} %fusion.26.targets, s32[64]{0:T(128)S(1)} %fusion.27.leader, f32[64,128,128]{2,1,0:T(8,128)} %all-to-all-done.2.got, f32[128,128,128]{2,1,0:T(8,128)} %add_blocks.3.start), custom_call_target="tpu_custom_call", output_to_operand_aliasing={{}: (3, {})} | custom-call | flops 1048576 | bytes 12582912 | tf_op jit(solution)/shard_map/add_blocks/pallas_call | solution.py:175
  454.2 25.8 %all-to-all-done.1.got = f32[64,128,128]{2,1,0:T(8,128)} async-done(((f32[64,128,128]{2,1,0:T(8,128)}), f32[64,128,128]{2,1,0:T(8,128)}, u32[]{:S(2)}, u32[]{:S(2)}) %all-to-all-start.1) | async-done | bytes 4194336 | tf_op jit(solution)/shard_map/all_to_all | solution.py:330
  480.1 6.7 %add_blocks.5 = f32[128,128,128]{2,1,0:T(8,128)} custom-call(s32[64]{0:T(128)S(1)} %fusion.19.targets, s32[64]{0:T(128)S(1)} %fusion.20.leader, f32[64,128,128]{2,1,0:T(8,128)} %all-to-all-done.1.got, f32[128,128,128]{2,1,0:T(8,128)} %add_blocks.4.start), custom_call_target="tpu_custom_call", output_to_operand_aliasing={{}: (3, {})} | custom-call | flops 1048576 | bytes 12582912 | tf_op jit(solution)/shard_map/add_blocks/pallas_call | solution.py:175
  (136 shorter events, 43.6 us)
Async XLA Ops:
  3.4 28.5 %collective-permute-start = (f32[1024,256]{1,0:T(8,128)S(1)}, f32[1024,256]{1,0:T(8,128)}, u32[]{:S(2)}, u32[]{:S(2)}) collective-permute-start(f32[1024,256]{1,0:T(8,128)S(1)} %bitcast_multiply_fusion), channel_id=1, source_target_pairs={{0,8},{8,16},{16,24},{1,9},{9,17},{17,25},{2,10},{10,18},{18,26},{... | collective-permute-start | bytes 3145736 | tf_op jit(solution)/shard_map/ppermute | solution.py:24
  9.3 28.1 %collective-permute-start.1 = (f32[1024,256]{1,0:T(8,128)S(1)}, f32[1024,256]{1,0:T(8,128)}, u32[]{:S(2)}, u32[]{:S(2)}) collective-permute-start(f32[1024,256]{1,0:T(8,128)S(1)} %bitcast_multiply_fusion), channel_id=1, source_target_pairs={{8,0},{16,8},{24,16},{9,1},{17,9},{25,17},{10,2},{18,10},{26,18},{... | collective-permute-start | bytes 3145736 | tf_op jit(solution)/shard_map/ppermute | solution.py:29
  10.6 26.8 %collective-permute-start.2 = (f32[1,1024,256]{2,1,0:T(8,128)S(1)}, f32[1,1024,256]{2,1,0:T(8,128)}, u32[]{:S(2)}, u32[]{:S(2)}) collective-permute-start(f32[1,1024,256]{2,1,0:T(8,128)S(1)} %bitcast.90), channel_id=1, source_target_pairs={{1,0},{2,1},{3,2},{4,3},{5,4},{6,5},{7,6},{0,7},{9,8},{10,9},{11,1... | collective-permute-start | bytes 3145736 | tf_op jit(solution)/shard_map/ppermute | solution.py:364
  12.5 28.6 %copy-start.17 = (s32[4]{0:T(128)S(1)}, s32[4]{0:T(128)}, u32[]{:S(2)}) copy-start(s32[4]{0:T(128)} %constant.158.clone) | copy-start | bytes 52
  12.5 30.5 %copy-start.16 = (s32[4]{0:T(128)S(1)}, s32[4]{0:T(128)}, u32[]{:S(2)}) copy-start(s32[4]{0:T(128)} %constant.159.clone) | copy-start | bytes 52
  12.5 32.9 %copy-start.15 = (s32[4]{0:T(128)S(1)}, s32[4]{0:T(128)}, u32[]{:S(2)}) copy-start(s32[4]{0:T(128)} %constant.157.clone) | copy-start | bytes 52
  16.6 112.7 %copy-start = (f32[128,2048]{1,0:T(8,128)}, f32[128,2048]{1,0:T(8,128)S(1)}, u32[]{:S(2)}) copy-start(f32[128,2048]{1,0:T(8,128)S(1)} %get-tuple-element.704.refs_5_.refs_7_.refs_9_.refs_11_) | copy-start | bytes 3145732
  16.6 336.7 %copy-start.2 = (f32[128,2048]{1,0:T(8,128)}, f32[128,2048]{1,0:T(8,128)S(1)}, u32[]{:S(2)}) copy-start(f32[128,2048]{1,0:T(8,128)S(1)} %get-tuple-element.703.refs_4_.refs_6_.refs_8_.refs_10_) | copy-start | bytes 3145732
  16.6 38.9 %collective-permute-start.3 = (f32[128,2048]{1,0:T(8,128)}, f32[128,2048]{1,0:T(8,128)}, u32[]{:S(2)}, u32[]{:S(2)}) collective-permute-start(f32[128,2048]{1,0:T(8,128)} %get-tuple-element.713.refs_20_), channel_id=1, source_target_pairs={{0,8},{8,16},{16,24},{1,9},{9,17},{17,25},{2,10},{10,18},{18,26},{... | collective-permute-start | bytes 3145736 | tf_op jit(solution)/shard_map/ppermute | solution.py:24
  21.8 38.1 %collective-permute-start.4 = (f32[128,2048]{1,0:T(8,128)S(1)}, f32[128,2048]{1,0:T(8,128)}, u32[]{:S(2)}, u32[]{:S(2)}) collective-permute-start(f32[128,2048]{1,0:T(8,128)S(1)} %get-tuple-element.703.refs_4_.refs_6_.refs_8_.refs_10_), channel_id=1, source_target_pairs={{8,0},{16,8},{24,16},{9,1},{17,9},{25,17},{10,2},{18,10},{26,18},{... | collective-permute-start | bytes 3145736 | tf_op jit(solution)/shard_map/ppermute | solution.py:29
  38.0 46.7 %collective-permute-start.5 = (f32[1024,256]{1,0:T(8,128)}, f32[1024,256]{1,0:T(8,128)}, u32[]{:S(2)}, u32[]{:S(2)}) collective-permute-start(f32[1024,256]{1,0:T(8,128)} %collective-permute-done), channel_id=1, source_target_pairs={{8,16},{16,24},{9,17},{17,25},{10,18},{18,26},{11,19},{19,27},{12,... | collective-permute-start | bytes 3145736 | tf_op jit(solution)/shard_map/ppermute | solution.py:24
  39.7 45.1 %collective-permute-start.6 = (f32[1024,256]{1,0:T(8,128)}, f32[1024,256]{1,0:T(8,128)}, u32[]{:S(2)}, u32[]{:S(2)}) collective-permute-start(f32[1024,256]{1,0:T(8,128)} %collective-permute-done.1), channel_id=1, source_target_pairs={{8,0},{16,8},{9,1},{17,9},{10,2},{18,10},{11,3},{19,11},{12,4},{20... | collective-permute-start | bytes 3145736 | tf_op jit(solution)/shard_map/ppermute | solution.py:29
  41.0 43.8 %collective-permute-start.7 = (f32[1,1024,256]{2,1,0:T(8,128)}, f32[1,1024,256]{2,1,0:T(8,128)}, u32[]{:S(2)}, u32[]{:S(2)}) collective-permute-start(f32[1,1024,256]{2,1,0:T(8,128)} %collective-permute-done.2.refs_1_), channel_id=1, source_target_pairs={{1,0},{2,1},{3,2},{4,3},{5,4},{6,5},{7,6},{0,7},{9,8},{10,9},{11,1... | collective-permute-start | bytes 3145736 | tf_op jit(solution)/shard_map/ppermute | solution.py:364
  46.7 38.1 %all-to-all-start = ((s32[32,2,128]{2,1,0:T(2,128)}), s32[32,2,128]{2,1,0:T(2,128)S(1)}, u32[]{:S(2)}, u32[]{:S(2)}) async-start(s32[32,2,128]{2,1,0:T(2,128)} %broadcast_in_dim.90), calls=%async_computation | async-start | bytes 65536 | tf_op jit(solution)/shard_map/all_to_all | solution.py:346
  59.9 34.2 %collective-permute-start.8 = (f32[128,2048]{1,0:T(8,128)}, f32[128,2048]{1,0:T(8,128)}, u32[]{:S(2)}, u32[]{:S(2)}) collective-permute-start(f32[128,2048]{1,0:T(8,128)} %get-tuple-element.714.refs_21_), channel_id=1, source_target_pairs={{0,8},{8,16},{16,24},{1,9},{9,17},{17,25},{2,10},{10,18},{18,26},{... | collective-permute-start | bytes 3145736 | tf_op jit(solution)/shard_map/ppermute | solution.py:24
  63.4 42.0 %collective-permute-start.9 = (f32[128,2048]{1,0:T(8,128)S(1)}, f32[128,2048]{1,0:T(8,128)}, u32[]{:S(2)}, u32[]{:S(2)}) collective-permute-start(f32[128,2048]{1,0:T(8,128)S(1)} %get-tuple-element.704.refs_5_.refs_7_.refs_9_.refs_11_), channel_id=1, source_target_pairs={{8,0},{16,8},{24,16},{9,1},{17,9},{25,17},{10,2},{18,10},{26,18},{... | collective-permute-start | bytes 3145736 | tf_op jit(solution)/shard_map/ppermute | solution.py:29
  88.2 17.2 %collective-permute-start.10 = (f32[1024,256]{1,0:T(8,128)}, f32[1024,256]{1,0:T(8,128)}, u32[]{:S(2)}, u32[]{:S(2)}) collective-permute-start(f32[1024,256]{1,0:T(8,128)} %collective-permute-done.5), channel_id=1, source_target_pairs={{16,24},{17,25},{18,26},{19,27},{20,28},{21,29},{22,30},{23,31}} | collective-permute-start | bytes 3145736 | tf_op jit(solution)/shard_map/ppermute | solution.py:24
  89.9 36.5 %collective-permute-start.11 = (f32[1024,256]{1,0:T(8,128)}, f32[1024,256]{1,0:T(8,128)}, u32[]{:S(2)}, u32[]{:S(2)}) collective-permute-start(f32[1024,256]{1,0:T(8,128)} %collective-permute-done.6), channel_id=1, source_target_pairs={{8,0},{9,1},{10,2},{11,3},{12,4},{13,5},{14,6},{15,7}} | collective-permute-start | bytes 3145736 | tf_op jit(solution)/shard_map/ppermute | solution.py:29
  91.2 35.2 %collective-permute-start.12 = (f32[1,1024,256]{2,1,0:T(8,128)}, f32[1,1024,256]{2,1,0:T(8,128)}, u32[]{:S(2)}, u32[]{:S(2)}) collective-permute-start(f32[1,1024,256]{2,1,0:T(8,128)} %collective-permute-done.7.refs_2_), channel_id=1, source_target_pairs={{1,0},{2,1},{3,2},{4,3},{5,4},{6,5},{7,6},{0,7},{9,8},{10,9},{11,1... | collective-permute-start | bytes 3145736 | tf_op jit(solution)/shard_map/ppermute | solution.py:364
  131.1 51.9 %collective-permute-start.17 = (f32[3,1024,256]{2,1,0:T(8,128)S(1)}, f32[3,1024,256]{2,1,0:T(8,128)}, u32[]{:S(2)}, u32[]{:S(2)}) collective-permute-start(f32[3,1024,256]{2,1,0:T(8,128)S(1)} %pad_maximum_fusion.refs_0_), channel_id=1, source_target_pairs={{1,0},{2,1},{3,2},{4,3},{5,4},{6,5},{7,6},{0,7},{9,8},{10,9},{11,1... | collective-permute-start | bytes 9437192 | tf_op jit(solution)/shard_map/ppermute | solution.py:364
  131.8 5.9 %collective-permute-start.13 = (f32[128,2048]{1,0:T(8,128)}, f32[128,2048]{1,0:T(8,128)}, u32[]{:S(2)}, u32[]{:S(2)}) collective-permute-start(f32[128,2048]{1,0:T(8,128)} %collective-permute-done.3.refs_16_.refs_18_), channel_id=1, source_target_pairs={{8,16},{16,24},{9,17},{17,25},{10,18},{18,26},{11,19},{19,27},{12,... | collective-permute-start | bytes 3145736 | tf_op jit(solution)/shard_map/ppermute | solution.py:24
  133.5 28.1 %collective-permute-start.14 = (f32[128,2048]{1,0:T(8,128)}, f32[128,2048]{1,0:T(8,128)S(1)}, u32[]{:S(2)}, u32[]{:S(2)}) collective-permute-start(f32[128,2048]{1,0:T(8,128)} %collective-permute-done.4.refs_6_.refs_8_.refs_10_.refs_12_), channel_id=1, source_target_pairs={{8,0},{16,8},{9,1},{17,9},{10,2},{18,10},{11,3},{19,11},{12,4},{20... | collective-permute-start | bytes 3145736 | tf_op jit(solution)/shard_map/ppermute | solution.py:29
  134.8 26.9 %collective-permute-start.15 = (f32[128,2048]{1,0:T(8,128)}, f32[128,2048]{1,0:T(8,128)}, u32[]{:S(2)}, u32[]{:S(2)}) collective-permute-start(f32[128,2048]{1,0:T(8,128)} %collective-permute-done.8.refs_17_.refs_19_), channel_id=1, source_target_pairs={{8,16},{16,24},{9,17},{17,25},{10,18},{18,26},{11,19},{19,27},{12,... | collective-permute-start | bytes 3145736 | tf_op jit(solution)/shard_map/ppermute | solution.py:24
  136.4 46.6 %collective-permute-start.16 = (f32[128,2048]{1,0:T(8,128)}, f32[128,2048]{1,0:T(8,128)}, u32[]{:S(2)}, u32[]{:S(2)}) collective-permute-start(f32[128,2048]{1,0:T(8,128)} %collective-permute-done.9.refs_7_.refs_9_.refs_11_.refs_13_), channel_id=1, source_target_pairs={{8,0},{16,8},{9,1},{17,9},{10,2},{18,10},{11,3},{19,11},{12,4},{20... | collective-permute-start | bytes 3145736 | tf_op jit(solution)/shard_map/ppermute | solution.py:29
  161.6 29.8 %copy-start.11 = (f32[128,2048]{1,0:T(8,128)}, f32[128,2048]{1,0:T(8,128)S(1)}, u32[]{:S(2)}) copy-start(f32[128,2048]{1,0:T(8,128)S(1)} %collective-permute-done.14.refs_8_.refs_10_.refs_12_.refs_14_) | copy-start | bytes 3145732
  183.0 54.0 %collective-permute-start.22 = (f32[3,1024,256]{2,1,0:T(8,128)}, f32[3,1024,256]{2,1,0:T(8,128)}, u32[]{:S(2)}, u32[]{:S(2)}) collective-permute-start(f32[3,1024,256]{2,1,0:T(8,128)} %collective-permute-done.17.refs_1_), channel_id=1, source_target_pairs={{1,0},{2,1},{3,2},{4,3},{5,4},{6,5},{7,6},{0,7},{9,8},{10,9},{11,1... | collective-permute-start | bytes 9437192 | tf_op jit(solution)/shard_map/ppermute | solution.py:364
  184.8 6.6 %collective-permute-start.18 = (f32[128,2048]{1,0:T(8,128)}, f32[128,2048]{1,0:T(8,128)}, u32[]{:S(2)}, u32[]{:S(2)}) collective-permute-start(f32[128,2048]{1,0:T(8,128)} %collective-permute-done.13.refs_14_.refs_16_.refs_18_), channel_id=1, source_target_pairs={{16,24},{17,25},{18,26},{19,27},{20,28},{21,29},{22,30},{23,31}} | collective-permute-start | bytes 3145736 | tf_op jit(solution)/shard_map/ppermute | solution.py:24
  186.5 28.1 %collective-permute-start.19 = (f32[128,2048]{1,0:T(8,128)S(1)}, f32[128,2048]{1,0:T(8,128)}, u32[]{:S(2)}, u32[]{:S(2)}) collective-permute-start(f32[128,2048]{1,0:T(8,128)S(1)} %collective-permute-done.14.refs_8_.refs_10_.refs_12_.refs_14_), channel_id=1, source_target_pairs={{8,0},{9,1},{10,2},{11,3},{12,4},{13,5},{14,6},{15,7}} | collective-permute-start | bytes 3145736 | tf_op jit(solution)/shard_map/ppermute | solution.py:29
  187.8 29.5 %collective-permute-start.20 = (f32[128,2048]{1,0:T(8,128)}, f32[128,2048]{1,0:T(8,128)}, u32[]{:S(2)}, u32[]{:S(2)}) collective-permute-start(f32[128,2048]{1,0:T(8,128)} %collective-permute-done.15.refs_15_.refs_17_.refs_19_), channel_id=1, source_target_pairs={{16,24},{17,25},{18,26},{19,27},{20,28},{21,29},{22,30},{23,31}} | collective-permute-start | bytes 3145736 | tf_op jit(solution)/shard_map/ppermute | solution.py:24
  189.4 47.6 %collective-permute-start.21 = (f32[128,2048]{1,0:T(8,128)}, f32[128,2048]{1,0:T(8,128)}, u32[]{:S(2)}, u32[]{:S(2)}) collective-permute-start(f32[128,2048]{1,0:T(8,128)} %collective-permute-done.16.refs_9_.refs_11_.refs_13_.refs_15_), channel_id=1, source_target_pairs={{8,0},{9,1},{10,2},{11,3},{12,4},{13,5},{14,6},{15,7}} | collective-permute-start | bytes 3145736 | tf_op jit(solution)/shard_map/ppermute | solution.py:29
  214.6 38.3 %collective-permute-start.23 = (f32[128,2048]{1,0:T(8,128)S(1)}, f32[128,2048]{1,0:T(8,128)S(1)}, u32[]{:S(2)}, u32[]{:S(2)}) collective-permute-start(f32[128,2048]{1,0:T(8,128)S(1)} %get-tuple-element.703.refs_4_.refs_6_.refs_8_.refs_10_), channel_id=1, source_target_pairs={{0,8},{8,16},{16,24},{1,9},{9,17},{17,25},{2,10},{10,18},{18,26},{... | collective-permute-start | bytes 3145736 | tf_op jit(solution)/shard_map/ppermute | solution.py:24
  216.0 41.2 %collective-permute-start.24 = (f32[128,2048]{1,0:T(8,128)}, f32[128,2048]{1,0:T(8,128)}, u32[]{:S(2)}, u32[]{:S(2)}) collective-permute-start(f32[128,2048]{1,0:T(8,128)} %get-tuple-element.713.refs_20_), channel_id=1, source_target_pairs={{8,0},{16,8},{9,1},{17,9},{10,2},{18,10},{11,3},{19,11},{12,4},{20... | collective-permute-start | bytes 3145736 | tf_op jit(solution)/shard_map/ppermute | solution.py:29
  237.7 54.8 %collective-permute-start.27 = (f32[3,1024,256]{2,1,0:T(8,128)}, f32[3,1024,256]{2,1,0:T(8,128)}, u32[]{:S(2)}, u32[]{:S(2)}) collective-permute-start(f32[3,1024,256]{2,1,0:T(8,128)} %collective-permute-done.22.refs_2_), channel_id=1, source_target_pairs={{1,0},{2,1},{3,2},{4,3},{5,4},{6,5},{7,6},{0,7},{9,8},{10,9},{11,1... | collective-permute-start | bytes 9437192 | tf_op jit(solution)/shard_map/ppermute | solution.py:364
  252.9 12.7 %copy-start.14 = (s32[4]{0:T(128)S(1)}, s32[4]{0:T(128)}, u32[]{:S(2)}) copy-start(s32[4]{0:T(128)} %constant.162.clone) | copy-start | bytes 52
  257.2 61.5 %all-to-all-start.4 = ((f32[64,128,128]{2,1,0:T(8,128)}), f32[64,128,128]{2,1,0:T(8,128)}, u32[]{:S(2)}, u32[]{:S(2)}) async-start(f32[64,128,128]{2,1,0:T(8,128)} %products.4), calls=%async_computation.4 | async-start | bytes 8388608 | tf_op jit(solution)/shard_map/all_to_all | solution.py:330
  261.8 24.5 %collective-permute-start.25 = (f32[128,2048]{1,0:T(8,128)S(1)}, f32[128,2048]{1,0:T(8,128)}, u32[]{:S(2)}, u32[]{:S(2)}) collective-permute-start(f32[128,2048]{1,0:T(8,128)S(1)} %copy-done.1), channel_id=1, source_target_pairs={{0,8},{8,16},{16,24},{1,9},{9,17},{17,25},{2,10},{10,18},{18,26},{... | collective-permute-start | bytes 3145736 | tf_op jit(solution)/shard_map/ppermute | solution.py:24
  264.3 28.2 %collective-permute-start.26 = (f32[128,2048]{1,0:T(8,128)}, f32[128,2048]{1,0:T(8,128)}, u32[]{:S(2)}, u32[]{:S(2)}) collective-permute-start(f32[128,2048]{1,0:T(8,128)} %get-tuple-element.714.refs_21_), channel_id=1, source_target_pairs={{8,0},{16,8},{9,1},{17,9},{10,2},{18,10},{11,3},{19,11},{12,4},{20... | collective-permute-start | bytes 3145736 | tf_op jit(solution)/shard_map/ppermute | solution.py:29
  268.7 38.2 %collective-permute-start.28 = (f32[128,2048]{1,0:T(8,128)S(1)}, f32[128,2048]{1,0:T(8,128)S(1)}, u32[]{:S(2)}, u32[]{:S(2)}) collective-permute-start(f32[128,2048]{1,0:T(8,128)S(1)} %collective-permute-done.23.refs_4_.refs_6_.refs_8_), channel_id=1, source_target_pairs={{8,16},{16,24},{9,17},{17,25},{10,18},{18,26},{11,19},{19,27},{12,... | collective-permute-start | bytes 3145736 | tf_op jit(solution)/shard_map/ppermute | solution.py:24
  269.4 44.8 %collective-permute-start.29 = (f32[128,2048]{1,0:T(8,128)}, f32[128,2048]{1,0:T(8,128)}, u32[]{:S(2)}, u32[]{:S(2)}) collective-permute-start(f32[128,2048]{1,0:T(8,128)} %collective-permute-done.24.refs_22_), channel_id=1, source_target_pairs={{8,0},{9,1},{10,2},{11,3},{12,4},{13,5},{14,6},{15,7}} | collective-permute-start | bytes 3145736 | tf_op jit(solution)/shard_map/ppermute | solution.py:29
  306.8 19.4 %copy-start.13 = (s32[4]{0:T(128)S(1)}, s32[4]{0:T(128)}, u32[]{:S(2)}) copy-start(s32[4]{0:T(128)} %constant.164.clone) | copy-start | bytes 52
  314.2 15.3 %copy-start.4 = (f32[128,2048]{1,0:T(8,128)S(1)}, f32[128,2048]{1,0:T(8,128)}, u32[]{:S(2)}) copy-start(f32[128,2048]{1,0:T(8,128)} %copy-done.3) | copy-start | bytes 3145732
  318.7 53.7 %all-to-all-start.3 = ((f32[64,128,128]{2,1,0:T(8,128)}), f32[64,128,128]{2,1,0:T(8,128)}, u32[]{:S(2)}, u32[]{:S(2)}) async-start(f32[64,128,128]{2,1,0:T(8,128)} %products.5), calls=%async_computation.3 | async-start | bytes 8388608 | tf_op jit(solution)/shard_map/all_to_all | solution.py:330
  323.3 6.9 %collective-permute-start.30 = (f32[128,2048]{1,0:T(8,128)}, f32[128,2048]{1,0:T(8,128)}, u32[]{:S(2)}, u32[]{:S(2)}) collective-permute-start(f32[128,2048]{1,0:T(8,128)} %collective-permute-done.25.refs_5_.refs_7_.refs_9_), channel_id=1, source_target_pairs={{8,16},{16,24},{9,17},{17,25},{10,18},{18,26},{11,19},{19,27},{12,... | collective-permute-start | bytes 3145736 | tf_op jit(solution)/shard_map/ppermute | solution.py:24
  325.0 27.6 %collective-permute-start.31 = (f32[128,2048]{1,0:T(8,128)}, f32[128,2048]{1,0:T(8,128)}, u32[]{:S(2)}, u32[]{:S(2)}) collective-permute-start(f32[128,2048]{1,0:T(8,128)} %collective-permute-done.26.refs_23_), channel_id=1, source_target_pairs={{8,0},{9,1},{10,2},{11,3},{12,4},{13,5},{14,6},{15,7}} | collective-permute-start | bytes 3145736 | tf_op jit(solution)/shard_map/ppermute | solution.py:29
  329.5 38.9 %collective-permute-start.32 = (f32[128,2048]{1,0:T(8,128)S(1)}, f32[128,2048]{1,0:T(8,128)S(1)}, u32[]{:S(2)}, u32[]{:S(2)}) collective-permute-start(f32[128,2048]{1,0:T(8,128)S(1)} %copy-done.4), channel_id=1, source_target_pairs={{16,24},{17,25},{18,26},{19,27},{20,28},{21,29},{22,30},{23,31}} | collective-permute-start | bytes 3145736 | tf_op jit(solution)/shard_map/ppermute | solution.py:24
  372.4 53.9 %all-to-all-start.2 = ((f32[64,128,128]{2,1,0:T(8,128)}), f32[64,128,128]{2,1,0:T(8,128)}, u32[]{:S(2)}, u32[]{:S(2)}) async-start(f32[64,128,128]{2,1,0:T(8,128)} %products.6), calls=%async_computation.2 | async-start | bytes 8388608 | tf_op jit(solution)/shard_map/all_to_all | solution.py:330
  377.2 4.6 collective-permute-start.33
  426.3 53.7 %all-to-all-start.1 = ((f32[64,128,128]{2,1,0:T(8,128)}), f32[64,128,128]{2,1,0:T(8,128)}, u32[]{:S(2)}, u32[]{:S(2)}) async-start(f32[64,128,128]{2,1,0:T(8,128)} %products.7), calls=%async_computation.1 | async-start | bytes 8388608 | tf_op jit(solution)/shard_map/all_to_all | solution.py:330
  (9 other events, 66.7 us)

commit v4 on v3

--- a/solution.py
+++ b/solution.py
@@ -35,6 +35,11 @@
 
 def image_key(row, inner, n_row):
     source, kind = inner % n_row, "XY"[inner // n_row]
+    last = n_row - 1
+    if kind == "X" and source < row:
+        return ("C", source - row + (row < last))
+    if kind == "Y" and source - row == -last:
+        return ("C", 0)
     return (kind, source - row)
 
 
@@ -44,12 +49,12 @@
     return high, low
 
 
-def product_kernel(place, choices, table, full, used, which, *refs):
+def product_kernel(place, choices, pieces, table, full, used, which, *refs):
     count = len(choices) * PARTS
     lefts = refs[:TICKS]
     rights = refs[TICKS : TICKS + count]
-    out = refs[TICKS + count]
-    left_in, right_in, left_two, right_two, left_sem, right_sem = refs[TICKS + count + 1 :]
+    outs = refs[TICKS + count : TICKS + count + pieces]
+    left_in, right_in, left_two, right_two, out, left_sem, right_sem, out_sem = refs[TICKS + count + pieces :]
     inner = right_in.shape[1]
     q_blocks = right_in.shape[2] // BLK
 
@@ -101,26 +106,37 @@
         for extra in range(ABREAST):
             one(full[turn * ABREAST + extra])
 
-
-def products(slots_used, which, lefts, rights, choices, place, slots):
+    copies = []
+    for piece, ref in enumerate(outs):
+        slots = pl.ds(piece * ref.shape[0], ref.shape[0])
+        copies.append(pltpu.make_async_copy(out.at[slots], ref, out_sem.at[piece]))
+        copies[-1].start()
+    for copy in copies:
+        copy.wait()
+
+
+def products(slots_used, which, lefts, rights, choices, place, pieces):
     rows, inner = lefts[0].shape[-2:]
     cols = rights[0][0].shape[1]
     rights = [part for of_image in rights for part in of_image]
     smem = pl.BlockSpec(memory_space=pltpu.SMEM)
     hbm = pl.BlockSpec(memory_space=pl.ANY)
     deep = TICKS * inner
+    slots = slots_used[0].shape[0]
     return pl.pallas_call(
-        functools.partial(product_kernel, place, choices),
-        out_shape=jax.ShapeDtypeStruct((slots, BLK, BLK), jnp.float32),
+        functools.partial(product_kernel, place, choices, pieces),
+        out_shape=[jax.ShapeDtypeStruct((slots // pieces, BLK, BLK), jnp.float32)] * pieces,
         in_specs=[smem] * 4 + [hbm] * (TICKS + len(rights)),
-        out_specs=pl.BlockSpec(memory_space=pltpu.VMEM),
+        out_specs=[hbm] * pieces,
         scratch_shapes=[
             pltpu.VMEM((TICKS, rows, inner), jnp.float32),
             pltpu.VMEM((TICKS, inner, cols), jnp.float32),
             pltpu.VMEM((2 * rows, deep), jnp.bfloat16),
             pltpu.VMEM((deep, 2 * cols), jnp.bfloat16),
+            pltpu.VMEM((slots, BLK, BLK), jnp.float32),
             pltpu.SemaphoreType.DMA((TICKS,)),
             pltpu.SemaphoreType.DMA((TICKS,)),
+            pltpu.SemaphoreType.DMA((pieces,)),
         ],
         compiler_params=pltpu.CompilerParams(vmem_limit_bytes=VMEM_LIMIT),
         cost_estimate=pl.CostEstimate(
@@ -220,34 +236,47 @@
     )(targets, got, start)
 
 
-def tables(every, n_row, n_col, capacity):
+def tables(every, n_row, n_col, capacity, order):
     row, col = lax.axis_index("row"), lax.axis_index("col")
     count = every.shape[-1]
     every = every.reshape(n_row, n_col, 2, count)
     places = jnp.arange(capacity, dtype=jnp.int32)
+    columns = jnp.arange(n_col, dtype=jnp.int32)
+    visits = jnp.asarray(order, jnp.int32)[row]
 
     def spread(match, values):
         rank = jnp.cumsum(match.astype(jnp.int32), axis=-1) - 1
         hit = match[..., None, :] & (rank[..., None, :] == places[:, None])
         return jnp.max(jnp.where(hit, values[..., None, :], -1), axis=-1)
 
-    column = lax.dynamic_index_in_dim(every[:, :, 0], col, axis=1, keepdims=False)
-    owners = row * n_col + jnp.arange(n_col, dtype=jnp.int32)
+    column = lax.dynamic_index_in_dim(every[:, :, 0], col, axis=1, keepdims=False)[visits]
     numbers = jnp.arange(count, dtype=jnp.int32)
-    sent = spread(
-        column[:, None, :] == owners[None, :, None],
-        jnp.broadcast_to(numbers, (n_row, n_col, count)),
-    )
-    got = spread(every[:, :, 0] == row * n_col + col, every[:, :, 1])
-    sent, got = (value.reshape(n_row, n_col * capacity) for value in (sent, got))
-    slots = jnp.arange(n_col * capacity, dtype=jnp.int32)
-
-    used = jnp.sum((sent >= 0).astype(jnp.int32), axis=-1, keepdims=True)
-    rank = jnp.cumsum((sent >= 0).astype(jnp.int32), axis=-1)
-    wanted = jnp.minimum(slots + 1, used)
-    full = jnp.argmax(rank[:, None, :] >= wanted[..., None], axis=-1).astype(jnp.int32)
+
+    def slots_of(blocks, owners):
+        match = blocks[:, None, :] == owners[..., None]
+        return spread(match, jnp.broadcast_to(numbers, match.shape)).reshape(len(blocks), -1)
+
+    def listed(sent):
+        there = (sent >= 0).astype(jnp.int32)
+        used = jnp.sum(there, axis=-1, keepdims=True)
+        rank = jnp.cumsum(there, axis=-1)
+        wanted = jnp.minimum(jnp.arange(sent.shape[-1], dtype=jnp.int32) + 1, used)
+        full = jnp.argmax(rank[:, None, :] >= wanted[..., None], axis=-1).astype(jnp.int32)
+        return sent, full, used
+
+    sent = listed(slots_of(column[:-1], jnp.broadcast_to(row * n_col + columns, (n_row - 1, n_col))))
+    beside = jnp.where(row == 1, 0, jnp.where(row == n_row - 2, n_row - 1, -1))
+    inside = jnp.where((row == 0) | (row == n_row - 1), -1, row)
+    rows = jnp.stack([inside, beside])
+    owners = jnp.where(rows[:, None] >= 0, rows[:, None] * n_col + columns, -1)
+    final = listed(slots_of(column[-1:], owners.reshape(1, -1)))
+
+    arriving = every[visits]
+    got = spread(arriving[:, :, 0] == row * n_col + col, arriving[:, :, 1])
+    got = got.reshape(n_row, n_col * capacity)
     leader = jnp.argmax(got[:, :, None] == got[:, None, :], axis=-1).astype(jnp.int32)
-    return {"sent": sent, "full": full, "used": used, "got": got, "leader": leader}
+    names = ("sent", "full", "used", "last sent", "last full", "last used", "got", "leader")
+    return dict(zip(names, (*sent, *final, got, leader)))
 
 
 def per_device(a_panels, b_panels, a_occupancy, b_occupancy, owner_device, owner_block, c_previous):
@@ -276,28 +305,41 @@
     mine = jnp.stack([owner_device.reshape(-1), owner_block.reshape(-1)])
     held["owners"] = jnp.broadcast_to(mine, (n_row * n_col,) + mine.shape)
 
-    first = [(("A", 0, -d), ("A", 0, d)) for d in range(1, n_row)]
+    reach = n_row - 1
+    first = [(("A", 0, -d), ("A", 0, d)) for d in range(1, reach)]
     lower = [(("Y", part, -d), ("X", part, d)) for d in range(1, n_row) for part in range(PARTS)]
     steps = []
     for number in range(max(len(first), len(lower))):
         steps += first[number : number + 1] + lower[number : number + 1]
-    steps += [(("X", part, -d), ("Y", part, d)) for d in range(1, n_row) for part in range(PARTS)]
+    for d in range(1, reach):
+        steps += [(("C", part, -d), ("Y", part, d)) for part in range(PARTS)]
+    steps = [((("C", key[1], 0), other) if key[::2] == ("Y", -reach) else (key, other)) for key, other in steps]
     ends = {keys[0]: number for number, keys in enumerate(steps)}
 
     def relay(key):
         kind, part, offset = key
         sources = early if kind == "Y" else every_row
+        if kind == "C":
+            lower = held.get(("C", part, offset + 1), held["X", part, 0])
+            later = held.get(("C", part, offset + 2), held["X", part, 0])
+            later = held["Y", part, 1 - reach] if offset == 0 else later
+            pairs = [(r, r + 1) for r in range(n_row - 1) if r == reach - 1 or -offset < reach - 1]
+            return lax.ppermute(jnp.where(row == reach - 1, later, lower), "row", pairs)
         if offset < 0:
             return up_step(held[kind, part, offset + 1], sources, -offset, n_row)
-        if (kind, part, offset - 1) in held:
-            return down_step(held[kind, part, offset - 1], sources, offset)
+        if kind == "Y" and offset > TICKS - 3:
+            return None
+        return down_step(held[kind, part, offset - 1], sources, offset)
 
     def close(due):
         held.update(due)
         held.update(zip(list(held), lax.optimization_barrier(tuple(held.values()))))
 
+    def working(step):
+        return [min(max(r, 1), n_row - 2) if step == n_row - 1 else r for r in range(n_row)]
+
     def chosen(step):
-        offsets = [order[r][step] - r for r in range(n_row)]
+        offsets = [order[r][step] - r for r in working(step)]
         kinds = sorted(set(offsets))
         index = jnp.asarray([kinds.index(o) for o in offsets], jnp.int32)[row]
         cases = [held["A", 0, k] for k in kinds]
@@ -305,7 +347,7 @@
 
     def product(step):
         keys = [
-            [image_key(r, order[r][step] + t, n_row) for t in range(TICKS)] for r in range(n_row)
+            [image_key(r, order[r][step] + t, n_row) for t in range(TICKS)] for r in working(step)
         ]
         names = sorted({key for of_row in keys for key in of_row})
         choices = [
@@ -313,61 +355,74 @@
         ]
         index = [[names.index(key) for key in of_row] for of_row in keys]
         which = jnp.asarray(index, jnp.int32)[row]
-        visit = jnp.asarray([order[r][step] for r in range(n_row)], jnp.int32)[row]
+        last = step == n_row - 1
+        of_step = ["last sent", "last full", "last used"] if last else ["sent", "full", "used"]
         return products(
-            [held[name][visit] for name in ("sent", "full", "used")],
+            [held[name][0 if last else step] for name in of_step],
             which,
             [held["own" if step == 0 else "rest", t] for t in range(TICKS)],
             [[held[kind, part, offset] for part in range(PARTS)] for kind, offset in names],
             choices,
             max(step - 1, 0),
-            n_col * capacity,
+            4 if last else 1,
         )
 
-    def exchange(step, total):
-        visit = jnp.asarray([order[r][step] for r in range(n_row)], jnp.int32)[row]
-        blocks = held["blocks", step]
+    def exchange(step, blocks, total):
+        targets, leader = held["got"][step], held["leader"][step]
         arrived = lax.all_to_all(blocks, "col", split_axis=0, concat_axis=0, tiled=True)
-        targets, leader = held["got"][visit], held["leader"][visit]
         if step == 0:
             return first_blocks(targets, arrived, total)
         return add_blocks(targets, leader, arrived, total)
 
     held["own", 0] = held["A", 0, 0][None]
-    start_of = {ends["Y", PARTS - 1, -(n_row - 1)] + 2: 0}
-    for d in range(1, n_row):
-        start_of[ends["X", PARTS - 1, -d] + 2] = d
+    start_of = {ends["C", PARTS - 1, -step] + 2: step for step in range(reach)}
+    last_number = ends["C", PARTS - 1, 2 - reach] + 2
     total = c_previous.reshape(c_previous.shape[2:])
-    flying = {2: {}, 3: {}, 4: {}}
+    exchange_at = {at + (1 if step < reach - 2 else 2): step for at, step in start_of.items()}
+    beside = [(1, 0), (n_row - 2, n_row - 1)]
+    flying = {number: {} for number in range(2, 7)}
     for number in range(len(steps) + 2):
         if number >= 2:
             close(flying.pop(number))
-        if number == 2:
-            every = lax.all_to_all(held["owners"], ("row", "col"), 0, 0, tiled=True)
-            flying[number + 2]["every"] = every
-        if number == 4:
-            flying[number + 1].update(tables(held["every"], n_row, n_col, capacity))
-        if number - 1 in start_of:
-            total = exchange(start_of[number - 1], total)
+        if number == last_number + 1:
+            flying[len(steps) + 2] = {"half": lax.ppermute(held["side", 2], "row", beside)}
+        step = exchange_at.get(number)
+        if step is not None:
+            total = exchange(step, held["blocks", step], total)
         if number < len(steps):
             moving = {key: relay(key) for key in steps[number]}
             flying.setdefault(number + 2, {}).update(
                 {key: value for key, value in moving.items() if value is not None}
             )
         for name in ("own", "rest"):
-            if name == "rest" and number == ends["A", 0, 1 - n_row] + 2:
+            if name == "rest" and number == ends["A", 0, 1 - reach] + 2:
                 held["rest", 0] = jnp.stack([chosen(step) for step in range(1, n_row)])
             ahead = [t for t in range(1, TICKS) if (name, t) not in held]
             if ahead and (name, ahead[0] - 1) in held and not any(
                 (name, ahead[0]) in of_step for of_step in flying.values()
             ):
-                hop = lax.ppermute(held[name, ahead[0] - 1], "col", backward)
-                flying.setdefault(number + 2, {})[name, ahead[0]] = hop
-        if number in start_of:
-            flying.setdefault(number + 1, {})["blocks", start_of[number]] = product(start_of[number])
-    for due in flying.values():
-        held.update(due)
-    total = exchange(n_row - 1, total)
+                hop = held[name, ahead[0] - 1]
+                for t in ahead[: 2 if number == 0 else 1]:
+                    hop = lax.ppermute(hop, "col", backward)
+                    flying.setdefault(number + 2, {})[name, t] = hop
+        if number == 2:
+            every = lax.all_to_all(held["owners"], ("row", "col"), 0, 0, tiled=True)
+            flying[5]["every"] = every
+        if number == 5:
+            flying[number + 1].update(tables(held["every"], n_row, n_col, capacity, order))
+        if number in start_of and number < len(steps) + 1:
+            (blocks,) = product(start_of[number])
+            flying.setdefault(number + 1, {})["blocks", start_of[number]] = blocks
+        if number == last_number:
+            sides = product(n_row - 1)
+            flying.setdefault(number + 1, {}).update({("side", k): v for k, v in enumerate(sides)})
+    (blocks,) = product(n_row - 2)
+    close({"blocks": blocks, **flying.pop(len(steps) + 2)})
+    far = [held["half"], lax.ppermute(held["side", 3], "row", beside)]
+    total = exchange(n_row - 2, held["blocks"], total)
+    edge = (row == 0) | (row == n_row - 1)
+    blocks = jnp.concatenate([jnp.where(edge, far[k], held["side", k]) for k in range(2)])
+    total = exchange(n_row - 1, blocks, total)
     return total.reshape(c_previous.shape)
 
 

time: 488 us -> 478 us (0.980); the launches traced: 487 us -> 471 us
  other arithmetic: 15 us -> 28.8 us
  starting transfers between devices: 81.8 us -> 74.5 us
  waiting for transfers between devices: 276 us -> 269 us
  between operations: 9.96 us -> 3.78 us
  Pallas kernels: 89 us -> 83.6 us
    ppermute x6 -> x14, waiting for transfers between devices: 0.02 us -> 140 us  [the longest x1 46.8 us: per_device(): far = [held['half'], lax.ppermute(held['side', 3], 'row', beside)]]
    ppermute x13 -> x10, waiting for transfers between devices: 170 us -> 69.1 us  [down_step(): return lax.ppermute(value, 'row', pairs) if pairs else None]
    all_to_all x4, waiting for transfers between devices: 62.2 us -> 35.2 us  [exchange(): lax.all_to_all(blocks, 'col', split_axis=0, concat_axis=0, tiled=True)]
    ppermute x6 -> x14, starting transfers between devices: 4.52 us -> 22.5 us  [the longest x6 10.8 us: relay(): return lax.ppermute(jnp.where(row == reach - 1, later, lower), 'row', pairs)]
    ppermute x15 -> x6, starting transfers between devices: 33.3 us -> 15.5 us  [up_step(): return lax.ppermute(value, 'row', pairs) if pairs else None]
    ppermute x15 -> x6, waiting for transfers between devices: 24.4 us -> 9.23 us  [up_step(): return lax.ppermute(value, 'row', pairs) if pairs else None]
    select_n x0 -> x10, other arithmetic: none -> 7.47 us  [the longest x6 4.59 us: relay(): return lax.ppermute(jnp.where(row == reach - 1, later, lower), 'row', pairs)]
    all_to_all x1, starting transfers between devices: 8.78 us -> 3.01 us  [per_device(): every = lax.all_to_all(held['owners'], ('row', 'col'), 0, 0, tiled=True)]
  transfers between devices with their start and end apart: 39 -> 35, of which waited for: 19 -> 18; matrix products, arithmetic and copies ran while one was open for 4% -> 7% of each run, Pallas kernels for 17% -> 16%
where the time goes in v4:
time: 478 us; the launch traced here: 471 us
  waiting for transfers between devices  269 us (56%)
  Pallas kernels  83.6 us (17%)
  starting transfers between devices  74.5 us (16%)
  other arithmetic  28.8 us (6%)
  local copies, waits for them, and re-layouts  11.5 us (2%)
    ppermute x10, waiting for transfers between devices, down_step(): return lax.ppermute(value, 'row', pairs) if pairs else None  69.1 us
    pallas_call x4, Pallas kernels, products(): pl.pallas_call(functools.partial(product_kernel, place, choices, pieces),...  53.8 us
    ppermute x1, waiting for transfers between devices, per_device(): far = [held['half'], lax.ppermute(held['side', 3], 'row', beside)]  46.8 us
    ppermute x6, waiting for transfers between devices, relay(): return lax.ppermute(jnp.where(row == reach - 1, later, lower), 'row', pairs)  45.7 us
    ppermute x1, waiting for transfers between devices, per_device(): lax.ppermute(held['side', 2], 'row', beside)  40.9 us
    all_to_all x4, waiting for transfers between devices, exchange(): lax.all_to_all(blocks, 'col', split_axis=0, concat_axis=0, tiled=True)  35.2 us
    all_to_all x4, starting transfers between devices, exchange(): lax.all_to_all(blocks, 'col', split_axis=0, concat_axis=0, tiled=True)  20.4 us
    pallas_call x3, Pallas kernels, add_blocks(): pl.pallas_call(add_kernel, out_shape=jax.ShapeDtypeStruct(start.shape, jn...  20.1 us
  transfers between devices with their start and end apart: 35, of which 18 were waited for; matrix products, arithmetic and copies ran while one was open for 7% of the time, Pallas kernels for 16%

profile of v4, /device:TPU:0, one launch (start us, length us, event | category | flops | bytes accessed | tf_op | source)
XLA Modules:
  0.0 471.0 jit_solution(11991535898409716603)
XLA Ops:
  3.4 3.4 collective-permute-start.2
  6.8 4.5 collective-permute-start
  12.9 6.3 %collective-permute-done.2.refs_1_ = f32[1,1024,256]{2,1,0:T(8,128)S(1)} collective-permute-done((f32[1,1024,256]{2,1,0:T(8,128)S(1)}, f32[1,1024,256]{2,1,0:T(8,128)S(1)}, u32[]{:S(2)}, u32[]{:S(2)}) %collective-permute-start.2) | collective-permute-done | bytes 1048608 | tf_op jit(solution)/shard_map/ppermute | solution.py:406
  19.1 2.8 collective-permute-start.3
  22.0 4.1 dynamic-slice_multiply_fusion
  26.1 4.5 collective-permute-start.4
  31.9 2.0 collective-permute-done
  33.9 5.5 %collective-permute-done.1 = f32[1024,256]{1,0:T(8,128)} collective-permute-done((f32[1024,256]{1,0:T(8,128)S(1)}, f32[1024,256]{1,0:T(8,128)}, u32[]{:S(2)}, u32[]{:S(2)}) %collective-permute-start.1) | collective-permute-done | bytes 1048608 | tf_op jit(solution)/shard_map/ppermute | solution.py:29
  46.8 7.2 %collective-permute-done.4.refs_16_.refs_18_.refs_14_ = f32[128,2048]{1,0:T(8,128)} collective-permute-done((f32[128,2048]{1,0:T(8,128)}, f32[128,2048]{1,0:T(8,128)}, u32[]{:S(2)}, u32[]{:S(2)}) %collective-permute-start.4) | collective-permute-done | bytes 1048608 | tf_op jit(solution)/shard_map/ppermute | solution.py:24
  54.1 7.8 %collective-permute-done.5.refs_8_.refs_10_.refs_12_ = f32[128,2048]{1,0:T(8,128)} collective-permute-done((f32[128,2048]{1,0:T(8,128)S(1)}, f32[128,2048]{1,0:T(8,128)}, u32[]{:S(2)}, u32[]{:S(2)}) %collective-permute-start.5) | collective-permute-done | bytes 1048608 | tf_op jit(solution)/shard_map/ppermute | solution.py:29
  61.9 3.5 collective-permute-start.9
  67.3 3.0 all-to-all-start
  70.4 14.0 %collective-permute-done.7 = f32[1024,256]{1,0:T(8,128)} collective-permute-done((f32[1024,256]{1,0:T(8,128)}, f32[1024,256]{1,0:T(8,128)}, u32[]{:S(2)}, u32[]{:S(2)}) %collective-permute-start.7) | collective-permute-done | bytes 1048608 | tf_op jit(solution)/shard_map/ppermute | solution.py:29
  84.4 1.6 collective-permute-start.11
  87.4 2.5 select_bitcast_fusion.1
  89.8 1.9 pad_maximum_fusion.1.refs_0_
  91.7 15.7 %all-to-all-done = s32[32,2,128]{2,1,0:T(2,128)S(1)} async-done(((s32[32,2,128]{2,1,0:T(2,128)}), s32[32,2,128]{2,1,0:T(2,128)S(1)}, u32[]{:S(2)}, u32[]{:S(2)}) %all-to-all-start) | async-done | bytes 32800 | tf_op jit(solution)/shard_map/all_to_all | solution.py:409
  117.2 9.9 %collective-permute-done.12.refs_10_.refs_12_.refs_14_ = f32[128,2048]{1,0:T(8,128)} collective-permute-done((f32[128,2048]{1,0:T(8,128)}, f32[128,2048]{1,0:T(8,128)}, u32[]{:S(2)}, u32[]{:S(2)}) %collective-permute-start.12) | collective-permute-done | bytes 1048608 | tf_op jit(solution)/shard_map/ppermute | solution.py:29
  127.1 2.7 collective-permute-start.18
  133.2 29.8 %collective-permute-done.15.refs_11_.refs_13_.refs_15_ = f32[128,2048]{1,0:T(8,128)S(1)} collective-permute-done((f32[128,2048]{1,0:T(8,128)}, f32[128,2048]{1,0:T(8,128)S(1)}, u32[]{:S(2)}, u32[]{:S(2)}) %collective-permute-start.15) | collective-permute-done | bytes 1048608 | tf_op jit(solution)/shard_map/ppermute | solution.py:29
  163.1 1.8 collective-permute-start.16
  166.3 1.9 collective-permute-start.19
  169.5 18.9 %collective-permute-done.16.refs_4_.refs_6_.refs_8_ = f32[128,2048]{1,0:T(8,128)S(1)} collective-permute-done((f32[128,2048]{1,0:T(8,128)S(1)}, f32[128,2048]{1,0:T(8,128)S(1)}, u32[]{:S(2)}, u32[]{:S(2)}) %collective-permute-start.16) | collective-permute-done | bytes 1048608 | tf_op jit(solution)/shard_map/ppermute | solution.py:327
  190.6 1.6 collective-permute-start.22
  192.2 13.8 %collective-permute-done.19.refs_5_.refs_7_.refs_9_ = f32[128,2048]{1,0:T(8,128)S(1)} collective-permute-done((f32[128,2048]{1,0:T(8,128)S(1)}, f32[128,2048]{1,0:T(8,128)S(1)}, u32[]{:S(2)}, u32[]{:S(2)}) %collective-permute-start.19) | collective-permute-done | bytes 1048608 | tf_op jit(solution)/shard_map/ppermute | solution.py:327
  206.0 2.0 collective-permute-done.20.refs_13_.refs_15_.refs_17_
  208.1 3.4 collective-permute-start.21
  211.6 2.3 collective-permute-start.24
  215.2 13.7 %products.4 = f32[64,128,128]{2,1,0:T(8,128)} custom-call(s32[64]{0:T(128)S(1)} %slice_bitcast_fusion.13.table, s32[64]{0:T(128)S(1)} %slice_bitcast_fusion.12.full, s32[1]{0:T(128)S(1)} %bitcast.101, s32[4]{0:T(128)S(1)} %fusion.14.which, f32[1,1024,256]{2,1,0:T(8,128)S(1)} %bitcast.100, f32[1,1024,256]{2,1,0:T(8,128)S(1)} %copy-done.7, ...), custom_call_target="tpu_custom_call" | custom-call | flops 12884901888 | bytes 16777216 | tf_op jit(solution)/shard_map/products/pallas_call | solution.py:126
  229.0 5.1 %collective-permute-done.21.refs_4_.refs_6_ = f32[128,2048]{1,0:T(8,128)} collective-permute-done((f32[128,2048]{1,0:T(8,128)S(1)}, f32[128,2048]{1,0:T(8,128)}, u32[]{:S(2)}, u32[]{:S(2)}) %collective-permute-start.21) | collective-permute-done | bytes 1048608 | tf_op jit(solution)/shard_map/ppermute | solution.py:327
  234.1 6.5 %all-to-all-start.4 = ((f32[64,128,128]{2,1,0:T(8,128)}), f32[64,128,128]{2,1,0:T(8,128)}, u32[]{:S(2)}, u32[]{:S(2)}) async-start(f32[64,128,128]{2,1,0:T(8,128)} %products.4), calls=%async_computation.4 | async-start | bytes 8388608 | tf_op jit(solution)/shard_map/all_to_all | solution.py:372
  242.1 7.9 %collective-permute-done.24.refs_5_.refs_7_ = f32[128,2048]{1,0:T(8,128)} collective-permute-done((f32[128,2048]{1,0:T(8,128)S(1)}, f32[128,2048]{1,0:T(8,128)}, u32[]{:S(2)}, u32[]{:S(2)}) %collective-permute-start.24) | collective-permute-done | bytes 1048608 | tf_op jit(solution)/shard_map/ppermute | solution.py:327
  253.5 10.0 %products.6 = (f32[32,128,128]{2,1,0:T(8,128)}, f32[32,128,128]{2,1,0:T(8,128)}, f32[32,128,128]{2,1,0:T(8,128)}, f32[32,128,128]{2,1,0:T(8,128)}) custom-call(s32[128]{0:T(128)S(1)} %bitcast.104, s32[128]{0:T(128)S(1)} %bitcast.105, s32[1]{0:T(128)} %bitcast.41.used, s32[4]{0:T(128)S(1)} %fusion.16.which, f32[3,1024,256]{2,1,0:T(8,128)} %pad_maximum_fusion.1.refs_0_, ...), custom_call_target="tpu_custom_call" | custom-call | flops 25769803776 | bytes 20971520 | tf_op jit(solution)/shard_map/products/pallas_call | solution.py:126
  263.5 15.1 %products.5 = f32[64,128,128]{2,1,0:T(8,128)} custom-call(s32[64]{0:T(128)S(1)} %slice_bitcast_fusion.11.table, s32[64]{0:T(128)S(1)} %slice_bitcast_fusion.10.full, s32[1]{0:T(128)} %bitcast.37.used, s32[4]{0:T(128)S(1)} %fusion.15.which, f32[3,1024,256]{2,1,0:T(8,128)} %pad_maximum_fusion.1.refs_0_, f32[3,1024,256]{2,1,0:T(8,128)} %collective-permute-done.13.refs_1_, ...), custom_call_target="tpu_custom_call" | custom-call | flops 12884901888 | bytes 16777216 | tf_op jit(solution)/shard_map/products/pallas_call | solution.py:126
  280.7 9.2 %all-to-all-done.4.got = f32[64,128,128]{2,1,0:T(8,128)} async-done(((f32[64,128,128]{2,1,0:T(8,128)}), f32[64,128,128]{2,1,0:T(8,128)}, u32[]{:S(2)}, u32[]{:S(2)}) %all-to-all-start.4) | async-done | bytes 4194336 | tf_op jit(solution)/shard_map/all_to_all | solution.py:372
  289.8 4.7 all-to-all-start.3
  297.1 15.0 %products.7 = f32[64,128,128]{2,1,0:T(8,128)} custom-call(s32[64]{0:T(128)S(1)} %slice_bitcast_fusion.9.table, s32[64]{0:T(128)S(1)} %slice_bitcast_fusion.8.full, s32[1]{0:T(128)} %bitcast.45.used, s32[4]{0:T(128)S(1)} %fusion.17.which, f32[3,1024,256]{2,1,0:T(8,128)} %pad_maximum_fusion.1.refs_0_, f32[3,1024,256]{2,1,0:T(8,128)} %collective-permute-done.13.refs_1_, ...), custom_call_target="tpu_custom_call" | custom-call | flops 12884901888 | bytes 16777216 | tf_op jit(solution)/shard_map/products/pallas_call | solution.py:126
  312.1 40.9 %collective-permute-done.28 = f32[32,128,128]{2,1,0:T(8,128)} collective-permute-done((f32[32,128,128]{2,1,0:T(8,128)}, f32[32,128,128]{2,1,0:T(8,128)}, u32[]{:S(2)}, u32[]{:S(2)}) %collective-permute-start.28) | collective-permute-done | bytes 2097184 | tf_op jit(solution)/shard_map/ppermute | solution.py:388
  353.0 4.6 all-to-all-start.2
  359.0 1.9 broadcast_select_fusion.1
  360.9 46.8 %collective-permute-done.29 = f32[32,128,128]{2,1,0:T(8,128)S(1)} collective-permute-done((f32[32,128,128]{2,1,0:T(8,128)}, f32[32,128,128]{2,1,0:T(8,128)S(1)}, u32[]{:S(2)}, u32[]{:S(2)}) %collective-permute-start.29) | collective-permute-done | bytes 2097184 | tf_op jit(solution)/shard_map/ppermute | solution.py:421
  408.0 2.5 pad_maximum_fusion
  410.4 4.6 all-to-all-start.1
  415.1 9.6 %first_blocks.1.start = f32[128,128,128]{2,1,0:T(8,128)} custom-call(s32[64]{0:T(128)S(1)} %slice_bitcast_fusion.1.targets, f32[64,128,128]{2,1,0:T(8,128)} %all-to-all-done.4.got, f32[128,128,128]{2,1,0:T(8,128)} %bitcast.106), custom_call_target="tpu_custom_call" | custom-call | flops 1048576 | bytes 20971520 | tf_op jit(solution)/shard_map/first_blocks/pallas_call | solution.py:226
  424.7 6.7 %add_blocks.3.start = f32[128,128,128]{2,1,0:T(8,128)} custom-call(s32[64]{0:T(128)S(1)} %slice_bitcast_fusion.3.targets, s32[64]{0:T(128)S(1)} %slice_bitcast_fusion.2.leader, f32[64,128,128]{2,1,0:T(8,128)} %all-to-all-done.3.got, f32[128,128,128]{2,1,0:T(8,128)} %first_blocks.1.start), custom_call_target="tpu_custom_call", output_to_operand_aliasing={{}: (3, {})} | custom-call | flops 1048576 | bytes 12582912 | tf_op jit(solution)/shard_map/add_blocks/pallas_call | solution.py:191
  431.4 6.7 %add_blocks.4.start = f32[128,128,128]{2,1,0:T(8,128)} custom-call(s32[64]{0:T(128)S(1)} %get-tuple-element.622.targets, s32[64]{0:T(128)S(1)} %get-tuple-element.620.leader, f32[64,128,128]{2,1,0:T(8,128)} %all-to-all-done.2.got, f32[128,128,128]{2,1,0:T(8,128)} %add_blocks.3.start), custom_call_target="tpu_custom_call", output_to_operand_aliasing={{}: (3, {})} | custom-call | flops 1048576 | bytes 12582912 | tf_op jit(solution)/shard_map/add_blocks/pallas_call | solution.py:191
  438.2 26.0 %all-to-all-done.1.got = f32[64,128,128]{2,1,0:T(8,128)} async-done(((f32[64,128,128]{2,1,0:T(8,128)}), f32[64,128,128]{2,1,0:T(8,128)}, u32[]{:S(2)}, u32[]{:S(2)}) %all-to-all-start.1) | async-done | bytes 4194336 | tf_op jit(solution)/shard_map/all_to_all | solution.py:372
  464.2 6.7 %add_blocks.5 = f32[128,128,128]{2,1,0:T(8,128)} custom-call(s32[64]{0:T(128)S(1)} %get-tuple-element.623.targets, s32[64]{0:T(128)S(1)} %get-tuple-element.621.leader, f32[64,128,128]{2,1,0:T(8,128)} %all-to-all-done.1.got, f32[128,128,128]{2,1,0:T(8,128)} %add_blocks.4.start), custom_call_target="tpu_custom_call", output_to_operand_aliasing={{}: (3, {})} | custom-call | flops 1048576 | bytes 12582912 | tf_op jit(solution)/shard_map/add_blocks/pallas_call | solution.py:191
  (172 shorter events, 45.0 us)
Async XLA Ops:
  3.4 22.7 %copy-start.4 = (f32[1024,256]{1,0:T(8,128)}, f32[1024,256]{1,0:T(8,128)S(1)}, u32[]{:S(2)}) copy-start(f32[1024,256]{1,0:T(8,128)S(1)} %bitcast_multiply_fusion) | copy-start | bytes 3145732
  3.4 15.7 %collective-permute-start.2 = (f32[1,1024,256]{2,1,0:T(8,128)S(1)}, f32[1,1024,256]{2,1,0:T(8,128)S(1)}, u32[]{:S(2)}, u32[]{:S(2)}) collective-permute-start(f32[1,1024,256]{2,1,0:T(8,128)S(1)} %bitcast.99), channel_id=1, source_target_pairs={{1,0},{2,1},{3,2},{4,3},{5,4},{6,5},{7,6},{0,7},{9,8},{10,9},{11,1... | collective-permute-start | bytes 3145736 | tf_op jit(solution)/shard_map/ppermute | solution.py:406
  6.8 27.1 %collective-permute-start = (f32[1024,256]{1,0:T(8,128)S(1)}, f32[1024,256]{1,0:T(8,128)}, u32[]{:S(2)}, u32[]{:S(2)}) collective-permute-start(f32[1024,256]{1,0:T(8,128)S(1)} %bitcast_multiply_fusion), channel_id=1, source_target_pairs={{0,8},{8,16},{16,24},{1,9},{9,17},{17,25},{2,10},{10,18},{18,26},{... | collective-permute-start | bytes 3145736 | tf_op jit(solution)/shard_map/ppermute | solution.py:24
  11.3 28.1 %collective-permute-start.1 = (f32[1024,256]{1,0:T(8,128)S(1)}, f32[1024,256]{1,0:T(8,128)}, u32[]{:S(2)}, u32[]{:S(2)}) collective-permute-start(f32[1024,256]{1,0:T(8,128)S(1)} %bitcast_multiply_fusion), channel_id=1, source_target_pairs={{8,0},{16,8},{24,16},{9,1},{17,9},{25,17},{10,2},{18,10},{26,18},{... | collective-permute-start | bytes 3145736 | tf_op jit(solution)/shard_map/ppermute | solution.py:29
  19.1 20.2 %collective-permute-start.3 = (f32[1,1024,256]{2,1,0:T(8,128)S(1)}, f32[1,1024,256]{2,1,0:T(8,128)}, u32[]{:S(2)}, u32[]{:S(2)}) collective-permute-start(f32[1,1024,256]{2,1,0:T(8,128)S(1)} %collective-permute-done.2.refs_1_), channel_id=1, source_target_pairs={{1,0},{2,1},{3,2},{4,3},{5,4},{6,5},{7,6},{0,7},{9,8},{10,9},{11,1... | collective-permute-start | bytes 3145736 | tf_op jit(solution)/shard_map/ppermute | solution.py:406
  22.0 22.0 %copy-start.27 = (s32[4]{0:T(128)S(1)}, s32[4]{0:T(128)}, u32[]{:S(2)}) copy-start(s32[4]{0:T(128)} %constant.173.clone) | copy-start | bytes 52
  22.0 23.2 %copy-start.26 = (s32[4]{0:T(128)S(1)}, s32[4]{0:T(128)}, u32[]{:S(2)}) copy-start(s32[4]{0:T(128)} %constant.171.clone) | copy-start | bytes 52
  26.1 181.8 %copy-start = (f32[128,2048]{1,0:T(8,128)}, f32[128,2048]{1,0:T(8,128)S(1)}, u32[]{:S(2)}) copy-start(f32[128,2048]{1,0:T(8,128)S(1)} %get-tuple-element.570.refs_6_.refs_8_.refs_10_) | copy-start | bytes 3145732
  26.1 28.0 %collective-permute-start.4 = (f32[128,2048]{1,0:T(8,128)}, f32[128,2048]{1,0:T(8,128)}, u32[]{:S(2)}, u32[]{:S(2)}) collective-permute-start(f32[128,2048]{1,0:T(8,128)} %get-tuple-element.569.refs_20_.refs_16_), channel_id=1, source_target_pairs={{0,8},{8,16},{16,24},{1,9},{9,17},{17,25},{2,10},{10,18},{18,26},{... | collective-permute-start | bytes 3145736 | tf_op jit(solution)/shard_map/ppermute | solution.py:24
  30.6 31.3 %collective-permute-start.5 = (f32[128,2048]{1,0:T(8,128)S(1)}, f32[128,2048]{1,0:T(8,128)}, u32[]{:S(2)}, u32[]{:S(2)}) collective-permute-start(f32[128,2048]{1,0:T(8,128)S(1)} %get-tuple-element.570.refs_6_.refs_8_.refs_10_), channel_id=1, source_target_pairs={{8,0},{16,8},{24,16},{9,1},{17,9},{25,17},{10,2},{18,10},{26,18},{... | collective-permute-start | bytes 3145736 | tf_op jit(solution)/shard_map/ppermute | solution.py:29
  40.0 30.4 %collective-permute-start.6 = (f32[1024,256]{1,0:T(8,128)}, f32[1024,256]{1,0:T(8,128)S(1)}, u32[]{:S(2)}, u32[]{:S(2)}) collective-permute-start(f32[1024,256]{1,0:T(8,128)} %collective-permute-done), channel_id=1, source_target_pairs={{8,16},{16,24},{9,17},{17,25},{10,18},{18,26},{11,19},{19,27},{12,... | collective-permute-start | bytes 3145736 | tf_op jit(solution)/shard_map/ppermute | solution.py:24
  40.7 43.7 %collective-permute-start.7 = (f32[1024,256]{1,0:T(8,128)}, f32[1024,256]{1,0:T(8,128)}, u32[]{:S(2)}, u32[]{:S(2)}) collective-permute-start(f32[1024,256]{1,0:T(8,128)} %collective-permute-done.1), channel_id=1, source_target_pairs={{8,0},{16,8},{9,1},{17,9},{10,2},{18,10},{11,3},{19,11},{12,4},{20... | collective-permute-start | bytes 3145736 | tf_op jit(solution)/shard_map/ppermute | solution.py:29
  42.0 42.4 %collective-permute-start.8 = (f32[1,1024,256]{2,1,0:T(8,128)}, f32[1,1024,256]{2,1,0:T(8,128)S(1)}, u32[]{:S(2)}, u32[]{:S(2)}) collective-permute-start(f32[1,1024,256]{2,1,0:T(8,128)} %collective-permute-done.3.refs_2_), channel_id=1, source_target_pairs={{1,0},{2,1},{3,2},{4,3},{5,4},{6,5},{7,6},{0,7},{9,8},{10,9},{11,1... | collective-permute-start | bytes 3145736 | tf_op jit(solution)/shard_map/ppermute | solution.py:406
  61.9 45.6 %collective-permute-start.9 = (f32[128,2048]{1,0:T(8,128)}, f32[128,2048]{1,0:T(8,128)}, u32[]{:S(2)}, u32[]{:S(2)}) collective-permute-start(f32[128,2048]{1,0:T(8,128)} %get-tuple-element.571.refs_21_.refs_17_), channel_id=1, source_target_pairs={{0,8},{8,16},{16,24},{1,9},{9,17},{17,25},{2,10},{10,18},{18,26},{... | collective-permute-start | bytes 3145736 | tf_op jit(solution)/shard_map/ppermute | solution.py:24
  65.3 42.1 %collective-permute-start.10 = (f32[128,2048]{1,0:T(8,128)}, f32[128,2048]{1,0:T(8,128)}, u32[]{:S(2)}, u32[]{:S(2)}) collective-permute-start(f32[128,2048]{1,0:T(8,128)} %get-tuple-element.572.refs_7_.refs_9_.refs_11_), channel_id=1, source_target_pairs={{8,0},{16,8},{24,16},{9,1},{17,9},{25,17},{10,2},{18,10},{26,18},{... | collective-permute-start | bytes 3145736 | tf_op jit(solution)/shard_map/ppermute | solution.py:29
  67.3 40.1 %all-to-all-start = ((s32[32,2,128]{2,1,0:T(2,128)}), s32[32,2,128]{2,1,0:T(2,128)S(1)}, u32[]{:S(2)}, u32[]{:S(2)}) async-start(s32[32,2,128]{2,1,0:T(2,128)} %broadcast_in_dim.133), calls=%async_computation | async-start | bytes 65536 | tf_op jit(solution)/shard_map/all_to_all | solution.py:409
  84.4 32.8 %collective-permute-start.11 = (f32[128,2048]{1,0:T(8,128)}, f32[128,2048]{1,0:T(8,128)}, u32[]{:S(2)}, u32[]{:S(2)}) collective-permute-start(f32[128,2048]{1,0:T(8,128)} %collective-permute-done.4.refs_16_.refs_18_.refs_14_), channel_id=1, source_target_pairs={{8,16},{16,24},{9,17},{17,25},{10,18},{18,26},{11,19},{19,27},{12,... | collective-permute-start | bytes 3145736 | tf_op jit(solution)/shard_map/ppermute | solution.py:24
  86.1 41.1 %collective-permute-start.12 = (f32[128,2048]{1,0:T(8,128)}, f32[128,2048]{1,0:T(8,128)}, u32[]{:S(2)}, u32[]{:S(2)}) collective-permute-start(f32[128,2048]{1,0:T(8,128)} %collective-permute-done.5.refs_8_.refs_10_.refs_12_), channel_id=1, source_target_pairs={{8,0},{16,8},{9,1},{17,9},{10,2},{18,10},{11,3},{19,11},{12,4},{20... | collective-permute-start | bytes 3145736 | tf_op jit(solution)/shard_map/ppermute | solution.py:29
  91.7 35.4 %collective-permute-start.13 = (f32[3,1024,256]{2,1,0:T(8,128)}, f32[3,1024,256]{2,1,0:T(8,128)}, u32[]{:S(2)}, u32[]{:S(2)}) collective-permute-start(f32[3,1024,256]{2,1,0:T(8,128)} %pad_maximum_fusion.1.refs_0_), channel_id=1, source_target_pairs={{1,0},{2,1},{3,2},{4,3},{5,4},{6,5},{7,6},{0,7},{9,8},{10,9},{11,1... | collective-permute-start | bytes 9437192 | tf_op jit(solution)/shard_map/ppermute | solution.py:406
  127.1 61.3 %collective-permute-start.18 = (f32[3,1024,256]{2,1,0:T(8,128)}, f32[3,1024,256]{2,1,0:T(8,128)S(1)}, u32[]{:S(2)}, u32[]{:S(2)}) collective-permute-start(f32[3,1024,256]{2,1,0:T(8,128)} %collective-permute-done.13.refs_1_), channel_id=1, source_target_pairs={{1,0},{2,1},{3,2},{4,3},{5,4},{6,5},{7,6},{0,7},{9,8},{10,9},{11,1... | collective-permute-start | bytes 9437192 | tf_op jit(solution)/shard_map/ppermute | solution.py:406
  129.8 3.3 collective-permute-start.14
  130.5 32.5 %collective-permute-start.15 = (f32[128,2048]{1,0:T(8,128)}, f32[128,2048]{1,0:T(8,128)S(1)}, u32[]{:S(2)}, u32[]{:S(2)}) collective-permute-start(f32[128,2048]{1,0:T(8,128)} %collective-permute-done.10.refs_9_.refs_11_.refs_13_), channel_id=1, source_target_pairs={{8,0},{16,8},{9,1},{17,9},{10,2},{18,10},{11,3},{19,11},{12,4},{20... | collective-permute-start | bytes 3145736 | tf_op jit(solution)/shard_map/ppermute | solution.py:29
  131.8 56.6 %collective-permute-start.17 = (f32[128,2048]{1,0:T(8,128)}, f32[128,2048]{1,0:T(8,128)S(1)}, u32[]{:S(2)}, u32[]{:S(2)}) collective-permute-start(f32[128,2048]{1,0:T(8,128)} %collective-permute-done.12.refs_10_.refs_12_.refs_14_), channel_id=1, source_target_pairs={{8,0},{9,1},{10,2},{11,3},{12,4},{13,5},{14,6},{15,7}} | collective-permute-start | bytes 3145736 | tf_op jit(solution)/shard_map/ppermute | solution.py:29
  133.1 33.1 %copy-start.17 = (f32[128,2048]{1,0:T(8,128)}, f32[128,2048]{1,0:T(8,128)S(1)}, u32[]{:S(2)}) copy-start(f32[128,2048]{1,0:T(8,128)S(1)} %collective-permute-done.14.refs_15_.refs_17_.refs_19_) | copy-start | bytes 3145732
  163.1 48.3 %copy-start.14 = (f32[128,2048]{1,0:T(8,128)S(1)}, f32[128,2048]{1,0:T(8,128)}, u32[]{:S(2)}) copy-start(f32[128,2048]{1,0:T(8,128)} %get-tuple-element.572.refs_7_.refs_9_.refs_11_) | copy-start | bytes 3145732
  163.1 25.3 %collective-permute-start.16 = (f32[128,2048]{1,0:T(8,128)S(1)}, f32[128,2048]{1,0:T(8,128)S(1)}, u32[]{:S(2)}, u32[]{:S(2)}) collective-permute-start(f32[128,2048]{1,0:T(8,128)S(1)} %broadcast_select_fusion.7), channel_id=1, source_target_pairs={{0,8},{8,16},{16,24},{1,9},{9,17},{17,25},{2,10},{10,18},{18,26},{... | collective-permute-start | bytes 3145736 | tf_op jit(solution)/shard_map/ppermute | solution.py:327
  166.3 39.7 %collective-permute-start.19 = (f32[128,2048]{1,0:T(8,128)S(1)}, f32[128,2048]{1,0:T(8,128)S(1)}, u32[]{:S(2)}, u32[]{:S(2)}) collective-permute-start(f32[128,2048]{1,0:T(8,128)S(1)} %broadcast_select_fusion.6), channel_id=1, source_target_pairs={{0,8},{8,16},{16,24},{1,9},{9,17},{17,25},{2,10},{10,18},{18,26},{... | collective-permute-start | bytes 3145736 | tf_op jit(solution)/shard_map/ppermute | solution.py:327
  168.2 39.7 %collective-permute-start.20 = (f32[128,2048]{1,0:T(8,128)S(1)}, f32[128,2048]{1,0:T(8,128)S(1)}, u32[]{:S(2)}, u32[]{:S(2)}) collective-permute-start(f32[128,2048]{1,0:T(8,128)S(1)} %collective-permute-done.15.refs_11_.refs_13_.refs_15_), channel_id=1, source_target_pairs={{8,0},{9,1},{10,2},{11,3},{12,4},{13,5},{14,6},{15,7}} | collective-permute-start | bytes 3145736 | tf_op jit(solution)/shard_map/ppermute | solution.py:29
  188.4 23.2 %copy-start.24 = (f32[128,2048]{1,0:T(8,128)}, f32[128,2048]{1,0:T(8,128)S(1)}, u32[]{:S(2)}) copy-start(f32[128,2048]{1,0:T(8,128)S(1)} %collective-permute-done.17.refs_12_.refs_14_.refs_16_) | copy-start | bytes 3145732
  188.4 23.2 %copy-start.22 = (f32[3,1024,256]{2,1,0:T(8,128)}, f32[3,1024,256]{2,1,0:T(8,128)S(1)}, u32[]{:S(2)}) copy-start(f32[3,1024,256]{2,1,0:T(8,128)S(1)} %collective-permute-done.18.refs_2_) | copy-start | bytes 9437188
  188.4 45.7 %collective-permute-start.23 = (f32[3,1024,256]{2,1,0:T(8,128)S(1)}, f32[3,1024,256]{2,1,0:T(8,128)}, u32[]{:S(2)}, u32[]{:S(2)}) collective-permute-start(f32[3,1024,256]{2,1,0:T(8,128)S(1)} %collective-permute-done.18.refs_2_), channel_id=1, source_target_pairs={{1,0},{2,1},{3,2},{4,3},{5,4},{6,5},{7,6},{0,7},{9,8},{10,9},{11,1... | collective-permute-start | bytes 9437192 | tf_op jit(solution)/shard_map/ppermute | solution.py:406
  190.6 24.6 %copy-start.5 = (f32[1024,256]{1,0:T(8,128)S(1)}, f32[1024,256]{1,0:T(8,128)}, u32[]{:S(2)}) copy-start(f32[1024,256]{1,0:T(8,128)} %copy-done.4) | copy-start | bytes 3145732
  190.6 24.6 %copy-start.7 = (f32[1,1024,256]{2,1,0:T(8,128)S(1)}, f32[1,1024,256]{2,1,0:T(8,128)}, u32[]{:S(2)}) copy-start(f32[1,1024,256]{2,1,0:T(8,128)} %copy-done.6) | copy-start | bytes 3145732
  190.6 24.6 %copy-start.9 = (f32[1,1024,256]{2,1,0:T(8,128)S(1)}, f32[1,1024,256]{2,1,0:T(8,128)}, u32[]{:S(2)}) copy-start(f32[1,1024,256]{2,1,0:T(8,128)} %copy-done.8) | copy-start | bytes 3145732
  190.6 43.5 %collective-permute-start.22 = (f32[128,2048]{1,0:T(8,128)}, f32[128,2048]{1,0:T(8,128)}, u32[]{:S(2)}, u32[]{:S(2)}) collective-permute-start(f32[128,2048]{1,0:T(8,128)} %get-tuple-element.569.refs_20_.refs_16_), channel_id=1, source_target_pairs={{8,0},{16,8},{9,1},{17,9},{10,2},{18,10},{11,3},{19,11},{12,4},{20... | collective-permute-start | bytes 3145736 | tf_op jit(solution)/shard_map/ppermute | solution.py:29
  208.1 26.0 %collective-permute-start.21 = (f32[128,2048]{1,0:T(8,128)S(1)}, f32[128,2048]{1,0:T(8,128)}, u32[]{:S(2)}, u32[]{:S(2)}) collective-permute-start(f32[128,2048]{1,0:T(8,128)S(1)} %broadcast_select_fusion.5), channel_id=1, source_target_pairs={{0,8},{8,16},{16,24},{1,9},{9,17},{17,25},{2,10},{10,18},{18,26},{... | collective-permute-start | bytes 3145736 | tf_op jit(solution)/shard_map/ppermute | solution.py:327
  211.6 38.4 %collective-permute-start.24 = (f32[128,2048]{1,0:T(8,128)S(1)}, f32[128,2048]{1,0:T(8,128)}, u32[]{:S(2)}, u32[]{:S(2)}) collective-permute-start(f32[128,2048]{1,0:T(8,128)S(1)} %broadcast_select_fusion.4), channel_id=1, source_target_pairs={{0,8},{8,16},{16,24},{1,9},{9,17},{17,25},{2,10},{10,18},{18,26},{... | collective-permute-start | bytes 3145736 | tf_op jit(solution)/shard_map/ppermute | solution.py:327
  213.9 36.1 %collective-permute-start.25 = (f32[128,2048]{1,0:T(8,128)}, f32[128,2048]{1,0:T(8,128)}, u32[]{:S(2)}, u32[]{:S(2)}) collective-permute-start(f32[128,2048]{1,0:T(8,128)} %get-tuple-element.571.refs_21_.refs_17_), channel_id=1, source_target_pairs={{8,0},{16,8},{9,1},{17,9},{10,2},{18,10},{11,3},{19,11},{12,4},{20... | collective-permute-start | bytes 3145736 | tf_op jit(solution)/shard_map/ppermute | solution.py:29
  234.1 55.7 %all-to-all-start.4 = ((f32[64,128,128]{2,1,0:T(8,128)}), f32[64,128,128]{2,1,0:T(8,128)}, u32[]{:S(2)}, u32[]{:S(2)}) async-start(f32[64,128,128]{2,1,0:T(8,128)} %products.4), calls=%async_computation.4 | async-start | bytes 8388608 | tf_op jit(solution)/shard_map/all_to_all | solution.py:372
  250.0 28.6 %collective-permute-start.26 = (f32[128,2048]{1,0:T(8,128)S(1)}, f32[128,2048]{1,0:T(8,128)S(1)}, u32[]{:S(2)}, u32[]{:S(2)}) collective-permute-start(f32[128,2048]{1,0:T(8,128)S(1)} %broadcast_select_fusion.3), channel_id=1, source_target_pairs={{16,24},{17,25},{18,26},{19,27},{20,28},{21,29},{22,30},{23,31}} | collective-permute-start | bytes 3145736 | tf_op jit(solution)/shard_map/ppermute | solution.py:327
  252.8 26.9 %collective-permute-start.27 = (f32[128,2048]{1,0:T(8,128)S(1)}, f32[128,2048]{1,0:T(8,128)S(1)}, u32[]{:S(2)}, u32[]{:S(2)}) collective-permute-start(f32[128,2048]{1,0:T(8,128)S(1)} %broadcast_select_fusion.2), channel_id=1, source_target_pairs={{16,24},{17,25},{18,26},{19,27},{20,28},{21,29},{22,30},{23,31}} | collective-permute-start | bytes 3145736 | tf_op jit(solution)/shard_map/ppermute | solution.py:327
  289.8 63.1 %all-to-all-start.3 = ((f32[64,128,128]{2,1,0:T(8,128)}), f32[64,128,128]{2,1,0:T(8,128)}, u32[]{:S(2)}, u32[]{:S(2)}) async-start(f32[64,128,128]{2,1,0:T(8,128)} %products.5), calls=%async_computation.3 | async-start | bytes 8388608 | tf_op jit(solution)/shard_map/all_to_all | solution.py:372
  294.5 58.5 %collective-permute-start.28 = (f32[32,128,128]{2,1,0:T(8,128)}, f32[32,128,128]{2,1,0:T(8,128)}, u32[]{:S(2)}, u32[]{:S(2)}) collective-permute-start(f32[32,128,128]{2,1,0:T(8,128)} %get-tuple-element.567), channel_id=1, source_target_pairs={{8,0},{16,24},{9,1},{17,25},{10,2},{18,26},{11,3},{19,27},{12,4},{... | collective-permute-start | bytes 6291464 | tf_op jit(solution)/shard_map/ppermute | solution.py:388
  312.1 46.9 %copy-start.16 = (f32[32,128,128]{2,1,0:T(8,128)S(1)}, f32[32,128,128]{2,1,0:T(8,128)}, u32[]{:S(2)}) copy-start(f32[32,128,128]{2,1,0:T(8,128)} %get-tuple-element.605) | copy-start | bytes 6291460
  353.0 57.5 %all-to-all-start.2 = ((f32[64,128,128]{2,1,0:T(8,128)}), f32[64,128,128]{2,1,0:T(8,128)}, u32[]{:S(2)}, u32[]{:S(2)}) async-start(f32[64,128,128]{2,1,0:T(8,128)} %products.7), calls=%async_computation.2 | async-start | bytes 8388608 | tf_op jit(solution)/shard_map/all_to_all | solution.py:372
  357.6 50.1 %copy-start.15 = (f32[32,128,128]{2,1,0:T(8,128)S(1)}, f32[32,128,128]{2,1,0:T(8,128)}, u32[]{:S(2)}) copy-start(f32[32,128,128]{2,1,0:T(8,128)} %get-tuple-element.607) | copy-start | bytes 6291460
  357.6 50.1 %collective-permute-start.29 = (f32[32,128,128]{2,1,0:T(8,128)}, f32[32,128,128]{2,1,0:T(8,128)S(1)}, u32[]{:S(2)}, u32[]{:S(2)}) collective-permute-start(f32[32,128,128]{2,1,0:T(8,128)} %get-tuple-element.606), channel_id=1, source_target_pairs={{8,0},{16,24},{9,1},{17,25},{10,2},{18,26},{11,3},{19,27},{12,4},{... | collective-permute-start | bytes 6291464 | tf_op jit(solution)/shard_map/ppermute | solution.py:421
  410.4 53.7 %all-to-all-start.1 = ((f32[64,128,128]{2,1,0:T(8,128)}), f32[64,128,128]{2,1,0:T(8,128)}, u32[]{:S(2)}, u32[]{:S(2)}) async-start(f32[64,128,128]{2,1,0:T(8,128)} %pad_maximum_fusion), calls=%async_computation.1 | async-start | bytes 8388608 | tf_op jit(solution)/shard_map/all_to_all | solution.py:372
  (16 other events, 146.1 us)

commit v5 on v4

--- a/solution.py
+++ b/solution.py
@@ -335,6 +335,12 @@
         held.update(due)
         held.update(zip(list(held), lax.optimization_barrier(tuple(held.values()))))
 
+    def hops(name, panels):
+        found = {(name, 0): panels}
+        for t in range(1, TICKS):
+            found[name, t] = lax.ppermute(found[name, t - 1], "col", backward)
+        return found
+
     def working(step):
         return [min(max(r, 1), n_row - 2) if step == n_row - 1 else r for r in range(n_row)]
 
@@ -374,16 +380,15 @@
             return first_blocks(targets, arrived, total)
         return add_blocks(targets, leader, arrived, total)
 
-    held["own", 0] = held["A", 0, 0][None]
     start_of = {ends["C", PARTS - 1, -step] + 2: step for step in range(reach)}
     last_number = ends["C", PARTS - 1, 2 - reach] + 2
     total = c_previous.reshape(c_previous.shape[2:])
     exchange_at = {at + (1 if step < reach - 2 else 2): step for at, step in start_of.items()}
     beside = [(1, 0), (n_row - 2, n_row - 1)]
-    flying = {number: {} for number in range(2, 7)}
+    flying = {number: {} for number in range(2, 11)}
     for number in range(len(steps) + 2):
         if number >= 2:
-            close(flying.pop(number))
+            close(flying.pop(number, {}))
         if number == last_number + 1:
             flying[len(steps) + 2] = {"half": lax.ppermute(held["side", 2], "row", beside)}
         step = exchange_at.get(number)
@@ -394,17 +399,11 @@
             flying.setdefault(number + 2, {}).update(
                 {key: value for key, value in moving.items() if value is not None}
             )
-        for name in ("own", "rest"):
-            if name == "rest" and number == ends["A", 0, 1 - reach] + 2:
-                held["rest", 0] = jnp.stack([chosen(step) for step in range(1, n_row)])
-            ahead = [t for t in range(1, TICKS) if (name, t) not in held]
-            if ahead and (name, ahead[0] - 1) in held and not any(
-                (name, ahead[0]) in of_step for of_step in flying.values()
-            ):
-                hop = held[name, ahead[0] - 1]
-                for t in ahead[: 2 if number == 0 else 1]:
-                    hop = lax.ppermute(hop, "col", backward)
-                    flying.setdefault(number + 2, {})[name, t] = hop
+        if number == 0:
+            flying[3].update(hops("own", held["A", 0, 0][None]))
+        if number == ends["A", 0, 1 - reach] + 2:
+            panels = jnp.stack([chosen(step) for step in range(1, n_row)])
+            flying.setdefault(number + 6, {}).update(hops("rest", panels))
         if number == 2:
             every = lax.all_to_all(held["owners"], ("row", "col"), 0, 0, tiled=True)
             flying[5]["every"] = every

time: 478 us -> 467 us (0.977)
  waiting for transfers between devices: 269 us -> 257 us
    ppermute x6, waiting for transfers between devices: 45.7 us -> 0.02 us  [relay(): return lax.ppermute(jnp.where(row == reach - 1, later, lower), 'row', pairs)]
    ppermute x10, waiting for transfers between devices: 69.1 us -> 104 us  [down_step(): return lax.ppermute(value, 'row', pairs) if pairs else None]
    all_to_all x1, waiting for transfers between devices: 15.7 us -> 24.6 us  [per_device(): every = lax.all_to_all(held['owners'], ('row', 'col'), 0, 0, tiled=True)]
    all_to_all x4, waiting for transfers between devices: 35.2 us -> 28.7 us  [exchange(): lax.all_to_all(blocks, 'col', split_axis=0, concat_axis=0, tiled=True)]
    ppermute x6, starting transfers between devices: 9.01 us -> 14.3 us  [hops(): found[name, t] = lax.ppermute(found[name, t - 1], 'col', backward)]
  transfers between devices with their start and end apart: 35 -> 35, of which waited for: 18 -> 17; matrix products, arithmetic and copies ran while one was open for 7% -> 7% of each run, Pallas kernels for 16% -> 17%
where the time goes in v5:
time: 467 us; the launch traced here: 463 us
  waiting for transfers between devices  257 us (55%)
  Pallas kernels  83.7 us (18%)
  starting transfers between devices  77.9 us (17%)
  other arithmetic  28.7 us (6%)
  local copies, waits for them, and re-layouts  11.5 us (2%)
    ppermute x10, waiting for transfers between devices, down_step(): return lax.ppermute(value, 'row', pairs) if pairs else None  104 us
    pallas_call x4, Pallas kernels, products(): pl.pallas_call(functools.partial(product_kernel, place, choices, pieces),...  53.6 us
    ppermute x1, waiting for transfers between devices, per_device(): far = [held['half'], lax.ppermute(held['side', 3], 'row', beside)]  46.8 us
    ppermute x1, waiting for transfers between devices, per_device(): lax.ppermute(held['side', 2], 'row', beside)  37.4 us
    all_to_all x4, waiting for transfers between devices, exchange(): lax.all_to_all(blocks, 'col', split_axis=0, concat_axis=0, tiled=True)  28.7 us
    all_to_all x1, waiting for transfers between devices, per_device(): every = lax.all_to_all(held['owners'], ('row', 'col'), 0, 0, tiled=True)  24.6 us
    pallas_call x3, Pallas kernels, add_blocks(): pl.pallas_call(add_kernel, out_shape=jax.ShapeDtypeStruct(start.shape, jn...  20.5 us
    all_to_all x4, starting transfers between devices, exchange(): lax.all_to_all(blocks, 'col', split_axis=0, concat_axis=0, tiled=True)  18.4 us
  transfers between devices with their start and end apart: 35, of which 17 were waited for; matrix products, arithmetic and copies ran while one was open for 7% of the time, Pallas kernels for 17%

profile of v5, /device:TPU:0, one launch (start us, length us, event | category | flops | bytes accessed | tf_op | source)
XLA Modules:
  0.0 463.0 jit_solution(11406329371844364480)
XLA Ops:
  3.4 3.4 collective-permute-start.2
  6.8 4.4 collective-permute-start
  12.8 6.4 %collective-permute-done.2.refs_1_ = f32[1,1024,256]{2,1,0:T(8,128)S(1)} collective-permute-done((f32[1,1024,256]{2,1,0:T(8,128)S(1)}, f32[1,1024,256]{2,1,0:T(8,128)S(1)}, u32[]{:S(2)}, u32[]{:S(2)}) %collective-permute-start.2) | collective-permute-done | bytes 1048608 | tf_op jit(solution)/shard_map/ppermute | solution.py:341
  19.1 2.8 collective-permute-start.3
  22.1 4.1 dynamic-slice_multiply_fusion
  26.2 4.5 collective-permute-start.5
  32.0 2.3 collective-permute-done.3.refs_2_
  34.3 2.9 collective-permute-start.4
  37.2 2.2 collective-permute-done.1
  46.4 7.6 %collective-permute-done.5.refs_16_.refs_18_.refs_14_ = f32[128,2048]{1,0:T(8,128)} collective-permute-done((f32[128,2048]{1,0:T(8,128)}, f32[128,2048]{1,0:T(8,128)}, u32[]{:S(2)}, u32[]{:S(2)}) %collective-permute-start.5) | collective-permute-done | bytes 1048608 | tf_op jit(solution)/shard_map/ppermute | solution.py:24
  54.1 7.8 %collective-permute-done.6.refs_8_.refs_10_.refs_12_ = f32[128,2048]{1,0:T(8,128)} collective-permute-done((f32[128,2048]{1,0:T(8,128)S(1)}, f32[128,2048]{1,0:T(8,128)}, u32[]{:S(2)}, u32[]{:S(2)}) %collective-permute-start.6) | collective-permute-done | bytes 1048608 | tf_op jit(solution)/shard_map/ppermute | solution.py:29
  61.8 19.8 %collective-permute-done.8 = f32[1024,256]{1,0:T(8,128)} collective-permute-done((f32[1024,256]{1,0:T(8,128)}, f32[1024,256]{1,0:T(8,128)}, u32[]{:S(2)}, u32[]{:S(2)}) %collective-permute-start.8) | collective-permute-done | bytes 1048608 | tf_op jit(solution)/shard_map/ppermute | solution.py:29
  81.6 2.1 select_bitcast_fusion.1
  83.8 1.8 pad_maximum_fusion.1.refs_0_
  87.0 3.5 collective-permute-start.9
  92.9 3.5 all-to-all-start
  96.3 1.7 collective-permute-start.11
  99.3 24.6 %all-to-all-done = s32[32,2,128]{2,1,0:T(2,128)S(1)} async-done(((s32[32,2,128]{2,1,0:T(2,128)}), s32[32,2,128]{2,1,0:T(2,128)S(1)}, u32[]{:S(2)}, u32[]{:S(2)}) %all-to-all-start) | async-done | bytes 32800 | tf_op jit(solution)/shard_map/all_to_all | solution.py:408
  127.9 1.6 collective-permute-start.13
  130.8 1.7 collective-permute-start.20
  138.5 3.2 collective-permute-done.12.refs_10_.refs_12_.refs_14_
  141.7 1.6 collective-permute-start.15
  144.7 19.4 %collective-permute-done.14.refs_11_.refs_13_.refs_15_ = f32[128,2048]{1,0:T(8,128)} collective-permute-done((f32[128,2048]{1,0:T(8,128)}, f32[128,2048]{1,0:T(8,128)}, u32[]{:S(2)}, u32[]{:S(2)}) %collective-permute-start.14) | collective-permute-done | bytes 1048608 | tf_op jit(solution)/shard_map/ppermute | solution.py:29
  168.3 2.1 collective-permute-start.21
  172.5 14.0 %collective-permute-done.16.refs_12_.refs_14_.refs_16_ = f32[128,2048]{1,0:T(8,128)S(1)} collective-permute-done((f32[128,2048]{1,0:T(8,128)}, f32[128,2048]{1,0:T(8,128)S(1)}, u32[]{:S(2)}, u32[]{:S(2)}) %collective-permute-start.16) | collective-permute-done | bytes 1048608 | tf_op jit(solution)/shard_map/ppermute | solution.py:29
  186.6 2.6 collective-permute-start.22
  190.5 18.5 %collective-permute-done.18.refs_13_.refs_15_.refs_17_ = f32[128,2048]{1,0:T(8,128)S(1)} collective-permute-done((f32[128,2048]{1,0:T(8,128)}, f32[128,2048]{1,0:T(8,128)S(1)}, u32[]{:S(2)}, u32[]{:S(2)}) %collective-permute-start.18) | collective-permute-done | bytes 1048608 | tf_op jit(solution)/shard_map/ppermute | solution.py:29
  209.1 2.6 collective-permute-start.24
  213.0 13.7 %products.4 = f32[64,128,128]{2,1,0:T(8,128)} custom-call(s32[64]{0:T(128)S(1)} %slice_bitcast_fusion.13.table, s32[64]{0:T(128)S(1)} %slice_bitcast_fusion.12.full, s32[1]{0:T(128)S(1)} %bitcast.101, s32[4]{0:T(128)S(1)} %fusion.14.which, f32[1,1024,256]{2,1,0:T(8,128)S(1)} %bitcast.100, f32[1,1024,256]{2,1,0:T(8,128)S(1)} %copy-done.7, ...), custom_call_target="tpu_custom_call" | custom-call | flops 12884901888 | bytes 16777216 | tf_op jit(solution)/shard_map/products/pallas_call | solution.py:126
  226.7 4.8 %collective-permute-done.23.refs_18_.refs_22_ = f32[128,2048]{1,0:T(8,128)} collective-permute-done((f32[128,2048]{1,0:T(8,128)}, f32[128,2048]{1,0:T(8,128)}, u32[]{:S(2)}, u32[]{:S(2)}) %collective-permute-start.23) | collective-permute-done | bytes 1048608 | tf_op jit(solution)/shard_map/ppermute | solution.py:29
  231.5 4.5 all-to-all-start.4
  237.6 14.1 %collective-permute-done.25.refs_19_.refs_23_ = f32[128,2048]{1,0:T(8,128)} collective-permute-done((f32[128,2048]{1,0:T(8,128)}, f32[128,2048]{1,0:T(8,128)}, u32[]{:S(2)}, u32[]{:S(2)}) %collective-permute-start.25) | collective-permute-done | bytes 1048608 | tf_op jit(solution)/shard_map/ppermute | solution.py:29
  255.2 9.9 %products.6 = (f32[32,128,128]{2,1,0:T(8,128)}, f32[32,128,128]{2,1,0:T(8,128)}, f32[32,128,128]{2,1,0:T(8,128)}, f32[32,128,128]{2,1,0:T(8,128)}) custom-call(s32[128]{0:T(128)S(1)} %bitcast.104, s32[128]{0:T(128)S(1)} %bitcast.105, s32[1]{0:T(128)} %bitcast.41.used, s32[4]{0:T(128)S(1)} %fusion.16.which, f32[3,1024,256]{2,1,0:T(8,128)} %pad_maximum_fusion.1.refs_0_, ...), custom_call_target="tpu_custom_call" | custom-call | flops 25769803776 | bytes 20971520 | tf_op jit(solution)/shard_map/products/pallas_call | solution.py:126
  265.1 15.0 %products.5 = f32[64,128,128]{2,1,0:T(8,128)} custom-call(s32[64]{0:T(128)S(1)} %slice_bitcast_fusion.11.table, s32[64]{0:T(128)S(1)} %slice_bitcast_fusion.10.full, s32[1]{0:T(128)} %bitcast.37.used, s32[4]{0:T(128)S(1)} %fusion.15.which, f32[3,1024,256]{2,1,0:T(8,128)} %pad_maximum_fusion.1.refs_0_, f32[3,1024,256]{2,1,0:T(8,128)} %collective-permute-done.19.refs_1_, ...), custom_call_target="tpu_custom_call" | custom-call | flops 12884901888 | bytes 16777216 | tf_op jit(solution)/shard_map/products/pallas_call | solution.py:126
  282.2 3.0 all-to-all-done.4.got
  285.2 4.7 %all-to-all-start.3 = ((f32[64,128,128]{2,1,0:T(8,128)}), f32[64,128,128]{2,1,0:T(8,128)}, u32[]{:S(2)}, u32[]{:S(2)}) async-start(f32[64,128,128]{2,1,0:T(8,128)} %products.5), calls=%async_computation.3 | async-start | bytes 8388608 | tf_op jit(solution)/shard_map/all_to_all | solution.py:378
  292.5 15.0 %products.7 = f32[64,128,128]{2,1,0:T(8,128)} custom-call(s32[64]{0:T(128)S(1)} %slice_bitcast_fusion.9.table, s32[64]{0:T(128)S(1)} %slice_bitcast_fusion.8.full, s32[1]{0:T(128)} %bitcast.45.used, s32[4]{0:T(128)S(1)} %fusion.17.which, f32[3,1024,256]{2,1,0:T(8,128)} %pad_maximum_fusion.1.refs_0_, f32[3,1024,256]{2,1,0:T(8,128)} %collective-permute-done.19.refs_1_, ...), custom_call_target="tpu_custom_call" | custom-call | flops 12884901888 | bytes 16777216 | tf_op jit(solution)/shard_map/products/pallas_call | solution.py:126
  307.5 37.4 %collective-permute-done.28 = f32[32,128,128]{2,1,0:T(8,128)} collective-permute-done((f32[32,128,128]{2,1,0:T(8,128)}, f32[32,128,128]{2,1,0:T(8,128)}, u32[]{:S(2)}, u32[]{:S(2)}) %collective-permute-start.28) | collective-permute-done | bytes 2097184 | tf_op jit(solution)/shard_map/ppermute | solution.py:393
  344.9 4.6 all-to-all-start.2
  350.9 1.9 broadcast_select_fusion.1
  352.8 46.8 %collective-permute-done.29 = f32[32,128,128]{2,1,0:T(8,128)S(1)} collective-permute-done((f32[32,128,128]{2,1,0:T(8,128)}, f32[32,128,128]{2,1,0:T(8,128)S(1)}, u32[]{:S(2)}, u32[]{:S(2)}) %collective-permute-start.29) | collective-permute-done | bytes 2097184 | tf_op jit(solution)/shard_map/ppermute | solution.py:420
  399.9 2.4 pad_maximum_fusion
  402.3 4.6 all-to-all-start.1
  407.0 9.7 %first_blocks.1.start = f32[128,128,128]{2,1,0:T(8,128)} custom-call(s32[64]{0:T(128)S(1)} %slice_bitcast_fusion.1.targets, f32[64,128,128]{2,1,0:T(8,128)} %all-to-all-done.4.got, f32[128,128,128]{2,1,0:T(8,128)} %bitcast.106), custom_call_target="tpu_custom_call" | custom-call | flops 1048576 | bytes 20971520 | tf_op jit(solution)/shard_map/first_blocks/pallas_call | solution.py:226
  416.6 6.9 %add_blocks.3.start = f32[128,128,128]{2,1,0:T(8,128)} custom-call(s32[64]{0:T(128)S(1)} %slice_bitcast_fusion.3.targets, s32[64]{0:T(128)S(1)} %slice_bitcast_fusion.2.leader, f32[64,128,128]{2,1,0:T(8,128)} %all-to-all-done.3.got, f32[128,128,128]{2,1,0:T(8,128)} %first_blocks.1.start), custom_call_target="tpu_custom_call", output_to_operand_aliasing={{}: (3, {})} | custom-call | flops 1048576 | bytes 12582912 | tf_op jit(solution)/shard_map/add_blocks/pallas_call | solution.py:191
  423.5 6.8 %add_blocks.4.start = f32[128,128,128]{2,1,0:T(8,128)} custom-call(s32[64]{0:T(128)S(1)} %get-tuple-element.596.targets, s32[64]{0:T(128)S(1)} %get-tuple-element.594.leader, f32[64,128,128]{2,1,0:T(8,128)} %all-to-all-done.2.got, f32[128,128,128]{2,1,0:T(8,128)} %add_blocks.3.start), custom_call_target="tpu_custom_call", output_to_operand_aliasing={{}: (3, {})} | custom-call | flops 1048576 | bytes 12582912 | tf_op jit(solution)/shard_map/add_blocks/pallas_call | solution.py:191
  430.3 25.7 %all-to-all-done.1.got = f32[64,128,128]{2,1,0:T(8,128)} async-done(((f32[64,128,128]{2,1,0:T(8,128)}), f32[64,128,128]{2,1,0:T(8,128)}, u32[]{:S(2)}, u32[]{:S(2)}) %all-to-all-start.1) | async-done | bytes 4194336 | tf_op jit(solution)/shard_map/all_to_all | solution.py:378
  456.0 6.8 %add_blocks.5 = f32[128,128,128]{2,1,0:T(8,128)} custom-call(s32[64]{0:T(128)S(1)} %get-tuple-element.597.targets, s32[64]{0:T(128)S(1)} %get-tuple-element.595.leader, f32[64,128,128]{2,1,0:T(8,128)} %all-to-all-done.1.got, f32[128,128,128]{2,1,0:T(8,128)} %add_blocks.4.start), custom_call_target="tpu_custom_call", output_to_operand_aliasing={{}: (3, {})} | custom-call | flops 1048576 | bytes 12582912 | tf_op jit(solution)/shard_map/add_blocks/pallas_call | solution.py:191
  (166 shorter events, 48.6 us)
Async XLA Ops:
  3.4 22.8 %copy-start.4 = (f32[1024,256]{1,0:T(8,128)}, f32[1024,256]{1,0:T(8,128)S(1)}, u32[]{:S(2)}) copy-start(f32[1024,256]{1,0:T(8,128)S(1)} %bitcast_multiply_fusion) | copy-start | bytes 3145732
  3.4 15.7 %collective-permute-start.2 = (f32[1,1024,256]{2,1,0:T(8,128)S(1)}, f32[1,1024,256]{2,1,0:T(8,128)S(1)}, u32[]{:S(2)}, u32[]{:S(2)}) collective-permute-start(f32[1,1024,256]{2,1,0:T(8,128)S(1)} %bitcast.99), channel_id=1, source_target_pairs={{1,0},{2,1},{3,2},{4,3},{5,4},{6,5},{7,6},{0,7},{9,8},{10,9},{11,1... | collective-permute-start | bytes 3145736 | tf_op jit(solution)/shard_map/ppermute | solution.py:341
  6.8 30.4 %collective-permute-start = (f32[1024,256]{1,0:T(8,128)S(1)}, f32[1024,256]{1,0:T(8,128)}, u32[]{:S(2)}, u32[]{:S(2)}) collective-permute-start(f32[1024,256]{1,0:T(8,128)S(1)} %bitcast_multiply_fusion), channel_id=1, source_target_pairs={{0,8},{8,16},{16,24},{1,9},{9,17},{17,25},{2,10},{10,18},{18,26},{... | collective-permute-start | bytes 3145736 | tf_op jit(solution)/shard_map/ppermute | solution.py:24
  11.3 28.1 %collective-permute-start.1 = (f32[1024,256]{1,0:T(8,128)S(1)}, f32[1024,256]{1,0:T(8,128)}, u32[]{:S(2)}, u32[]{:S(2)}) collective-permute-start(f32[1024,256]{1,0:T(8,128)S(1)} %bitcast_multiply_fusion), channel_id=1, source_target_pairs={{8,0},{16,8},{24,16},{9,1},{17,9},{25,17},{10,2},{18,10},{26,18},{... | collective-permute-start | bytes 3145736 | tf_op jit(solution)/shard_map/ppermute | solution.py:29
  19.1 15.1 %collective-permute-start.3 = (f32[1,1024,256]{2,1,0:T(8,128)S(1)}, f32[1,1024,256]{2,1,0:T(8,128)}, u32[]{:S(2)}, u32[]{:S(2)}) collective-permute-start(f32[1,1024,256]{2,1,0:T(8,128)S(1)} %collective-permute-done.2.refs_1_), channel_id=1, source_target_pairs={{1,0},{2,1},{3,2},{4,3},{5,4},{6,5},{7,6},{0,7},{9,8},{10,9},{11,1... | collective-permute-start | bytes 3145736 | tf_op jit(solution)/shard_map/ppermute | solution.py:341
  22.1 21.8 %copy-start.24 = (s32[4]{0:T(128)S(1)}, s32[4]{0:T(128)}, u32[]{:S(2)}) copy-start(s32[4]{0:T(128)} %constant.173.clone) | copy-start | bytes 52
  22.1 23.1 %copy-start.23 = (s32[4]{0:T(128)S(1)}, s32[4]{0:T(128)}, u32[]{:S(2)}) copy-start(s32[4]{0:T(128)} %constant.171.clone) | copy-start | bytes 52
  26.2 160.3 %copy-start = (f32[128,2048]{1,0:T(8,128)}, f32[128,2048]{1,0:T(8,128)S(1)}, u32[]{:S(2)}) copy-start(f32[128,2048]{1,0:T(8,128)S(1)} %get-tuple-element.544.refs_6_.refs_8_.refs_10_) | copy-start | bytes 3145732
  26.2 27.9 %collective-permute-start.5 = (f32[128,2048]{1,0:T(8,128)}, f32[128,2048]{1,0:T(8,128)}, u32[]{:S(2)}, u32[]{:S(2)}) collective-permute-start(f32[128,2048]{1,0:T(8,128)} %get-tuple-element.543.refs_20_.refs_16_), channel_id=1, source_target_pairs={{0,8},{8,16},{16,24},{1,9},{9,17},{17,25},{2,10},{10,18},{18,26},{... | collective-permute-start | bytes 3145736 | tf_op jit(solution)/shard_map/ppermute | solution.py:24
  30.7 31.2 %collective-permute-start.6 = (f32[128,2048]{1,0:T(8,128)S(1)}, f32[128,2048]{1,0:T(8,128)}, u32[]{:S(2)}, u32[]{:S(2)}) collective-permute-start(f32[128,2048]{1,0:T(8,128)S(1)} %get-tuple-element.544.refs_6_.refs_8_.refs_10_), channel_id=1, source_target_pairs={{8,0},{16,8},{24,16},{9,1},{17,9},{25,17},{10,2},{18,10},{26,18},{... | collective-permute-start | bytes 3145736 | tf_op jit(solution)/shard_map/ppermute | solution.py:29
  34.3 27.6 %collective-permute-start.4 = (f32[1,1024,256]{2,1,0:T(8,128)}, f32[1,1024,256]{2,1,0:T(8,128)S(1)}, u32[]{:S(2)}, u32[]{:S(2)}) collective-permute-start(f32[1,1024,256]{2,1,0:T(8,128)} %collective-permute-done.3.refs_2_), channel_id=1, source_target_pairs={{1,0},{2,1},{3,2},{4,3},{5,4},{6,5},{7,6},{0,7},{9,8},{10,9},{11,1... | collective-permute-start | bytes 3145736 | tf_op jit(solution)/shard_map/ppermute | solution.py:341
  40.0 21.9 %collective-permute-start.7 = (f32[1024,256]{1,0:T(8,128)}, f32[1024,256]{1,0:T(8,128)S(1)}, u32[]{:S(2)}, u32[]{:S(2)}) collective-permute-start(f32[1024,256]{1,0:T(8,128)} %collective-permute-done), channel_id=1, source_target_pairs={{8,16},{16,24},{9,17},{17,25},{10,18},{18,26},{11,19},{19,27},{12,... | collective-permute-start | bytes 3145736 | tf_op jit(solution)/shard_map/ppermute | solution.py:24
  40.7 40.9 %collective-permute-start.8 = (f32[1024,256]{1,0:T(8,128)}, f32[1024,256]{1,0:T(8,128)}, u32[]{:S(2)}, u32[]{:S(2)}) collective-permute-start(f32[1024,256]{1,0:T(8,128)} %collective-permute-done.1), channel_id=1, source_target_pairs={{8,0},{16,8},{9,1},{17,9},{10,2},{18,10},{11,3},{19,11},{12,4},{20... | collective-permute-start | bytes 3145736 | tf_op jit(solution)/shard_map/ppermute | solution.py:29
  61.8 21.9 %copy-start.8 = (f32[1,1024,256]{2,1,0:T(8,128)}, f32[1,1024,256]{2,1,0:T(8,128)S(1)}, u32[]{:S(2)}) copy-start(f32[1,1024,256]{2,1,0:T(8,128)S(1)} %collective-permute-done.4.refs_3_) | copy-start | bytes 3145732
  85.6 45.2 %collective-permute-start.19 = (f32[3,1024,256]{2,1,0:T(8,128)}, f32[3,1024,256]{2,1,0:T(8,128)}, u32[]{:S(2)}, u32[]{:S(2)}) collective-permute-start(f32[3,1024,256]{2,1,0:T(8,128)} %pad_maximum_fusion.1.refs_0_), channel_id=1, source_target_pairs={{1,0},{2,1},{3,2},{4,3},{5,4},{6,5},{7,6},{0,7},{9,8},{10,9},{11,1... | collective-permute-start | bytes 9437192 | tf_op jit(solution)/shard_map/ppermute | solution.py:341
  87.0 36.8 %collective-permute-start.9 = (f32[128,2048]{1,0:T(8,128)}, f32[128,2048]{1,0:T(8,128)}, u32[]{:S(2)}, u32[]{:S(2)}) collective-permute-start(f32[128,2048]{1,0:T(8,128)} %get-tuple-element.545.refs_21_.refs_17_), channel_id=1, source_target_pairs={{0,8},{8,16},{16,24},{1,9},{9,17},{17,25},{2,10},{10,18},{18,26},{... | collective-permute-start | bytes 3145736 | tf_op jit(solution)/shard_map/ppermute | solution.py:24
  90.5 33.3 %collective-permute-start.10 = (f32[128,2048]{1,0:T(8,128)S(1)}, f32[128,2048]{1,0:T(8,128)}, u32[]{:S(2)}, u32[]{:S(2)}) collective-permute-start(f32[128,2048]{1,0:T(8,128)S(1)} %copy-done.14), channel_id=1, source_target_pairs={{8,0},{16,8},{24,16},{9,1},{17,9},{25,17},{10,2},{18,10},{26,18},{... | collective-permute-start | bytes 3145736 | tf_op jit(solution)/shard_map/ppermute | solution.py:29
  92.9 31.0 %all-to-all-start = ((s32[32,2,128]{2,1,0:T(2,128)}), s32[32,2,128]{2,1,0:T(2,128)S(1)}, u32[]{:S(2)}, u32[]{:S(2)}) async-start(s32[32,2,128]{2,1,0:T(2,128)} %broadcast_in_dim.133), calls=%async_computation | async-start | bytes 65536 | tf_op jit(solution)/shard_map/all_to_all | solution.py:408
  96.3 42.1 %collective-permute-start.11 = (f32[128,2048]{1,0:T(8,128)}, f32[128,2048]{1,0:T(8,128)}, u32[]{:S(2)}, u32[]{:S(2)}) collective-permute-start(f32[128,2048]{1,0:T(8,128)} %collective-permute-done.5.refs_16_.refs_18_.refs_14_), channel_id=1, source_target_pairs={{8,16},{16,24},{9,17},{17,25},{10,18},{18,26},{11,19},{19,27},{12,... | collective-permute-start | bytes 3145736 | tf_op jit(solution)/shard_map/ppermute | solution.py:24
  98.0 43.6 %collective-permute-start.12 = (f32[128,2048]{1,0:T(8,128)}, f32[128,2048]{1,0:T(8,128)}, u32[]{:S(2)}, u32[]{:S(2)}) collective-permute-start(f32[128,2048]{1,0:T(8,128)} %collective-permute-done.6.refs_8_.refs_10_.refs_12_), channel_id=1, source_target_pairs={{8,0},{16,8},{9,1},{17,9},{10,2},{18,10},{11,3},{19,11},{12,4},{20... | collective-permute-start | bytes 3145736 | tf_op jit(solution)/shard_map/ppermute | solution.py:29
  127.9 16.8 %collective-permute-start.13 = (f32[128,2048]{1,0:T(8,128)}, f32[128,2048]{1,0:T(8,128)}, u32[]{:S(2)}, u32[]{:S(2)}) collective-permute-start(f32[128,2048]{1,0:T(8,128)} %collective-permute-done.9.refs_17_.refs_19_.refs_15_), channel_id=1, source_target_pairs={{8,16},{16,24},{9,17},{17,25},{10,18},{18,26},{11,19},{19,27},{12,... | collective-permute-start | bytes 3145736 | tf_op jit(solution)/shard_map/ppermute | solution.py:24
  129.5 34.6 %collective-permute-start.14 = (f32[128,2048]{1,0:T(8,128)}, f32[128,2048]{1,0:T(8,128)}, u32[]{:S(2)}, u32[]{:S(2)}) collective-permute-start(f32[128,2048]{1,0:T(8,128)} %collective-permute-done.10.refs_9_.refs_11_.refs_13_), channel_id=1, source_target_pairs={{8,0},{16,8},{9,1},{17,9},{10,2},{18,10},{11,3},{19,11},{12,4},{20... | collective-permute-start | bytes 3145736 | tf_op jit(solution)/shard_map/ppermute | solution.py:29
  130.8 37.4 %collective-permute-start.20 = (f32[3,1024,256]{2,1,0:T(8,128)}, f32[3,1024,256]{2,1,0:T(8,128)}, u32[]{:S(2)}, u32[]{:S(2)}) collective-permute-start(f32[3,1024,256]{2,1,0:T(8,128)} %collective-permute-done.19.refs_1_), channel_id=1, source_target_pairs={{1,0},{2,1},{3,2},{4,3},{5,4},{6,5},{7,6},{0,7},{9,8},{10,9},{11,1... | collective-permute-start | bytes 9437192 | tf_op jit(solution)/shard_map/ppermute | solution.py:341
  141.7 67.2 %copy-start.15 = (f32[128,2048]{1,0:T(8,128)S(1)}, f32[128,2048]{1,0:T(8,128)}, u32[]{:S(2)}) copy-start(f32[128,2048]{1,0:T(8,128)} %get-tuple-element.546.refs_7_.refs_9_.refs_11_) | copy-start | bytes 3145732
  141.7 30.7 %collective-permute-start.15 = (f32[128,2048]{1,0:T(8,128)S(1)}, f32[128,2048]{1,0:T(8,128)S(1)}, u32[]{:S(2)}, u32[]{:S(2)}) collective-permute-start(f32[128,2048]{1,0:T(8,128)S(1)} %broadcast_select_fusion.7), channel_id=1, source_target_pairs={{0,8},{8,16},{16,24},{1,9},{9,17},{17,25},{2,10},{10,18},{18,26},{... | collective-permute-start | bytes 3145736 | tf_op jit(solution)/shard_map/ppermute | solution.py:327
  143.4 43.1 %collective-permute-start.16 = (f32[128,2048]{1,0:T(8,128)}, f32[128,2048]{1,0:T(8,128)S(1)}, u32[]{:S(2)}, u32[]{:S(2)}) collective-permute-start(f32[128,2048]{1,0:T(8,128)} %collective-permute-done.12.refs_10_.refs_12_.refs_14_), channel_id=1, source_target_pairs={{8,0},{9,1},{10,2},{11,3},{12,4},{13,5},{14,6},{15,7}} | collective-permute-start | bytes 3145736 | tf_op jit(solution)/shard_map/ppermute | solution.py:29
  165.4 25.0 %collective-permute-start.17 = (f32[128,2048]{1,0:T(8,128)S(1)}, f32[128,2048]{1,0:T(8,128)S(1)}, u32[]{:S(2)}, u32[]{:S(2)}) collective-permute-start(f32[128,2048]{1,0:T(8,128)S(1)} %broadcast_select_fusion.6), channel_id=1, source_target_pairs={{0,8},{8,16},{16,24},{1,9},{9,17},{17,25},{2,10},{10,18},{18,26},{... | collective-permute-start | bytes 3145736 | tf_op jit(solution)/shard_map/ppermute | solution.py:327
  167.0 42.0 %collective-permute-start.18 = (f32[128,2048]{1,0:T(8,128)}, f32[128,2048]{1,0:T(8,128)S(1)}, u32[]{:S(2)}, u32[]{:S(2)}) collective-permute-start(f32[128,2048]{1,0:T(8,128)} %collective-permute-done.14.refs_11_.refs_13_.refs_15_), channel_id=1, source_target_pairs={{8,0},{9,1},{10,2},{11,3},{12,4},{13,5},{14,6},{15,7}} | collective-permute-start | bytes 3145736 | tf_op jit(solution)/shard_map/ppermute | solution.py:29
  168.3 63.2 %collective-permute-start.21 = (f32[3,1024,256]{2,1,0:T(8,128)}, f32[3,1024,256]{2,1,0:T(8,128)}, u32[]{:S(2)}, u32[]{:S(2)}) collective-permute-start(f32[3,1024,256]{2,1,0:T(8,128)} %collective-permute-done.20.refs_2_), channel_id=1, source_target_pairs={{1,0},{2,1},{3,2},{4,3},{5,4},{6,5},{7,6},{0,7},{9,8},{10,9},{11,1... | collective-permute-start | bytes 9437192 | tf_op jit(solution)/shard_map/ppermute | solution.py:341
  172.5 40.5 %copy-start.5 = (f32[1024,256]{1,0:T(8,128)S(1)}, f32[1024,256]{1,0:T(8,128)}, u32[]{:S(2)}) copy-start(f32[1024,256]{1,0:T(8,128)} %copy-done.4) | copy-start | bytes 3145732
  172.5 40.5 %copy-start.7 = (f32[1,1024,256]{2,1,0:T(8,128)S(1)}, f32[1,1024,256]{2,1,0:T(8,128)}, u32[]{:S(2)}) copy-start(f32[1,1024,256]{2,1,0:T(8,128)} %copy-done.6) | copy-start | bytes 3145732
  172.5 40.5 %copy-start.9 = (f32[1,1024,256]{2,1,0:T(8,128)S(1)}, f32[1,1024,256]{2,1,0:T(8,128)}, u32[]{:S(2)}) copy-start(f32[1,1024,256]{2,1,0:T(8,128)} %copy-done.8) | copy-start | bytes 3145732
  186.5 22.6 %copy-start.21 = (f32[128,2048]{1,0:T(8,128)}, f32[128,2048]{1,0:T(8,128)S(1)}, u32[]{:S(2)}) copy-start(f32[128,2048]{1,0:T(8,128)S(1)} %collective-permute-done.16.refs_12_.refs_14_.refs_16_) | copy-start | bytes 3145732
  186.6 40.1 %collective-permute-start.22 = (f32[128,2048]{1,0:T(8,128)S(1)}, f32[128,2048]{1,0:T(8,128)}, u32[]{:S(2)}, u32[]{:S(2)}) collective-permute-start(f32[128,2048]{1,0:T(8,128)S(1)} %broadcast_select_fusion.5), channel_id=1, source_target_pairs={{0,8},{8,16},{16,24},{1,9},{9,17},{17,25},{2,10},{10,18},{18,26},{... | collective-permute-start | bytes 3145736 | tf_op jit(solution)/shard_map/ppermute | solution.py:327
  189.2 42.3 %collective-permute-start.23 = (f32[128,2048]{1,0:T(8,128)}, f32[128,2048]{1,0:T(8,128)}, u32[]{:S(2)}, u32[]{:S(2)}) collective-permute-start(f32[128,2048]{1,0:T(8,128)} %get-tuple-element.543.refs_20_.refs_16_), channel_id=1, source_target_pairs={{8,0},{16,8},{9,1},{17,9},{10,2},{18,10},{11,3},{19,11},{12,4},{20... | collective-permute-start | bytes 3145736 | tf_op jit(solution)/shard_map/ppermute | solution.py:29
  190.5 22.5 %copy-start.2 = (f32[128,2048]{1,0:T(8,128)}, f32[128,2048]{1,0:T(8,128)S(1)}, u32[]{:S(2)}) copy-start(f32[128,2048]{1,0:T(8,128)S(1)} %collective-permute-done.17.refs_5_.refs_7_.refs_9_) | copy-start | bytes 3145732
  209.1 28.5 %collective-permute-start.24 = (f32[128,2048]{1,0:T(8,128)S(1)}, f32[128,2048]{1,0:T(8,128)}, u32[]{:S(2)}, u32[]{:S(2)}) collective-permute-start(f32[128,2048]{1,0:T(8,128)S(1)} %broadcast_select_fusion.4), channel_id=1, source_target_pairs={{0,8},{8,16},{16,24},{1,9},{9,17},{17,25},{2,10},{10,18},{18,26},{... | collective-permute-start | bytes 3145736 | tf_op jit(solution)/shard_map/ppermute | solution.py:327
  211.6 40.1 %collective-permute-start.25 = (f32[128,2048]{1,0:T(8,128)}, f32[128,2048]{1,0:T(8,128)}, u32[]{:S(2)}, u32[]{:S(2)}) collective-permute-start(f32[128,2048]{1,0:T(8,128)} %get-tuple-element.545.refs_21_.refs_17_), channel_id=1, source_target_pairs={{8,0},{16,8},{9,1},{17,9},{10,2},{18,10},{11,3},{19,11},{12,4},{20... | collective-permute-start | bytes 3145736 | tf_op jit(solution)/shard_map/ppermute | solution.py:29
  231.5 53.7 %all-to-all-start.4 = ((f32[64,128,128]{2,1,0:T(8,128)}), f32[64,128,128]{2,1,0:T(8,128)}, u32[]{:S(2)}, u32[]{:S(2)}) async-start(f32[64,128,128]{2,1,0:T(8,128)} %products.4), calls=%async_computation.4 | async-start | bytes 8388608 | tf_op jit(solution)/shard_map/all_to_all | solution.py:378
  251.7 28.4 %collective-permute-start.26 = (f32[128,2048]{1,0:T(8,128)S(1)}, f32[128,2048]{1,0:T(8,128)S(1)}, u32[]{:S(2)}, u32[]{:S(2)}) collective-permute-start(f32[128,2048]{1,0:T(8,128)S(1)} %broadcast_select_fusion.3), channel_id=1, source_target_pairs={{16,24},{17,25},{18,26},{19,27},{20,28},{21,29},{22,30},{23,31}} | collective-permute-start | bytes 3145736 | tf_op jit(solution)/shard_map/ppermute | solution.py:327
  254.5 26.7 %collective-permute-start.27 = (f32[128,2048]{1,0:T(8,128)S(1)}, f32[128,2048]{1,0:T(8,128)S(1)}, u32[]{:S(2)}, u32[]{:S(2)}) collective-permute-start(f32[128,2048]{1,0:T(8,128)S(1)} %broadcast_select_fusion.2), channel_id=1, source_target_pairs={{16,24},{17,25},{18,26},{19,27},{20,28},{21,29},{22,30},{23,31}} | collective-permute-start | bytes 3145736 | tf_op jit(solution)/shard_map/ppermute | solution.py:327
  285.2 59.7 %all-to-all-start.3 = ((f32[64,128,128]{2,1,0:T(8,128)}), f32[64,128,128]{2,1,0:T(8,128)}, u32[]{:S(2)}, u32[]{:S(2)}) async-start(f32[64,128,128]{2,1,0:T(8,128)} %products.5), calls=%async_computation.3 | async-start | bytes 8388608 | tf_op jit(solution)/shard_map/all_to_all | solution.py:378
  289.9 55.0 %collective-permute-start.28 = (f32[32,128,128]{2,1,0:T(8,128)}, f32[32,128,128]{2,1,0:T(8,128)}, u32[]{:S(2)}, u32[]{:S(2)}) collective-permute-start(f32[32,128,128]{2,1,0:T(8,128)} %get-tuple-element.541), channel_id=1, source_target_pairs={{8,0},{16,24},{9,1},{17,25},{10,2},{18,26},{11,3},{19,27},{12,4},{... | collective-permute-start | bytes 6291464 | tf_op jit(solution)/shard_map/ppermute | solution.py:393
  307.5 43.4 %copy-start.17 = (f32[32,128,128]{2,1,0:T(8,128)S(1)}, f32[32,128,128]{2,1,0:T(8,128)}, u32[]{:S(2)}) copy-start(f32[32,128,128]{2,1,0:T(8,128)} %get-tuple-element.579) | copy-start | bytes 6291460
  344.9 57.4 %all-to-all-start.2 = ((f32[64,128,128]{2,1,0:T(8,128)}), f32[64,128,128]{2,1,0:T(8,128)}, u32[]{:S(2)}, u32[]{:S(2)}) async-start(f32[64,128,128]{2,1,0:T(8,128)} %products.7), calls=%async_computation.2 | async-start | bytes 8388608 | tf_op jit(solution)/shard_map/all_to_all | solution.py:378
  349.5 50.1 %copy-start.16 = (f32[32,128,128]{2,1,0:T(8,128)S(1)}, f32[32,128,128]{2,1,0:T(8,128)}, u32[]{:S(2)}) copy-start(f32[32,128,128]{2,1,0:T(8,128)} %get-tuple-element.581) | copy-start | bytes 6291460
  349.5 50.1 %collective-permute-start.29 = (f32[32,128,128]{2,1,0:T(8,128)}, f32[32,128,128]{2,1,0:T(8,128)S(1)}, u32[]{:S(2)}, u32[]{:S(2)}) collective-permute-start(f32[32,128,128]{2,1,0:T(8,128)} %get-tuple-element.580), channel_id=1, source_target_pairs={{8,0},{16,24},{9,1},{17,25},{10,2},{18,26},{11,3},{19,27},{12,4},{... | collective-permute-start | bytes 6291464 | tf_op jit(solution)/shard_map/ppermute | solution.py:420
  402.3 53.7 %all-to-all-start.1 = ((f32[64,128,128]{2,1,0:T(8,128)}), f32[64,128,128]{2,1,0:T(8,128)}, u32[]{:S(2)}, u32[]{:S(2)}) async-start(f32[64,128,128]{2,1,0:T(8,128)} %pad_maximum_fusion), calls=%async_computation.1 | async-start | bytes 8388608 | tf_op jit(solution)/shard_map/all_to_all | solution.py:378
  (13 other events, 126.3 us)

commit v6 on v5

--- a/solution.py
+++ b/solution.py
@@ -403,7 +403,7 @@
             flying[3].update(hops("own", held["A", 0, 0][None]))
         if number == ends["A", 0, 1 - reach] + 2:
             panels = jnp.stack([chosen(step) for step in range(1, n_row)])
-            flying.setdefault(number + 6, {}).update(hops("rest", panels))
+            flying.setdefault(number + 7, {}).update(hops("rest", panels))
         if number == 2:
             every = lax.all_to_all(held["owners"], ("row", "col"), 0, 0, tiled=True)
             flying[5]["every"] = every

time: 467 us -> 460 us (0.985)
    ppermute x10, waiting for transfers between devices: 104 us -> 83.2 us  [down_step(): return lax.ppermute(value, 'row', pairs) if pairs else None]
    ppermute x6, waiting for transfers between devices: 0.02 us -> 10.1 us  [relay(): return lax.ppermute(jnp.where(row == reach - 1, later, lower), 'row', pairs)]
    all_to_all x1, waiting for transfers between devices: 24.6 us -> 30.7 us  [per_device(): every = lax.all_to_all(held['owners'], ('row', 'col'), 0, 0, tiled=True)]
    ppermute x1, waiting for transfers between devices: 37.4 us -> 32.2 us  [per_device(): lax.ppermute(held['side', 2], 'row', beside)]
    all_to_all x4, waiting for transfers between devices: 28.7 us -> 33.6 us  [exchange(): lax.all_to_all(blocks, 'col', split_axis=0, concat_axis=0, tiled=True)]
  transfers between devices with their start and end apart: 35 -> 35, of which waited for: 17 -> 19; matrix products, arithmetic and copies ran while one was open for 7% -> 8% of each run, Pallas kernels for 17% -> 16%
where the time goes in v6:
time: 460 us; the launch traced here: 456 us
  waiting for transfers between devices  253 us (55%)
  Pallas kernels  81.5 us (18%)
  starting transfers between devices  77 us (17%)
  other arithmetic  28.2 us (6%)
  local copies, waits for them, and re-layouts  12.6 us (3%)
    ppermute x10, waiting for transfers between devices, down_step(): return lax.ppermute(value, 'row', pairs) if pairs else None  83.2 us
    pallas_call x4, Pallas kernels, products(): pl.pallas_call(functools.partial(product_kernel, place, choices, pieces),...  51 us
    ppermute x1, waiting for transfers between devices, per_device(): far = [held['half'], lax.ppermute(held['side', 3], 'row', beside)]  46.8 us
    all_to_all x4, waiting for transfers between devices, exchange(): lax.all_to_all(blocks, 'col', split_axis=0, concat_axis=0, tiled=True)  33.6 us
    ppermute x1, waiting for transfers between devices, per_device(): lax.ppermute(held['side', 2], 'row', beside)  32.2 us
    all_to_all x1, waiting for transfers between devices, per_device(): every = lax.all_to_all(held['owners'], ('row', 'col'), 0, 0, tiled=True)  30.7 us
    pallas_call x3, Pallas kernels, add_blocks(): pl.pallas_call(add_kernel, out_shape=jax.ShapeDtypeStruct(start.shape, jn...  20.7 us
    all_to_all x4, starting transfers between devices, exchange(): lax.all_to_all(blocks, 'col', split_axis=0, concat_axis=0, tiled=True)  18.4 us
  transfers between devices with their start and end apart: 35, of which 19 were waited for; matrix products, arithmetic and copies ran while one was open for 8% of the time, Pallas kernels for 16%

profile of v6, /device:TPU:0, one launch (start us, length us, event | category | flops | bytes accessed | tf_op | source)
XLA Modules:
  0.0 455.7 jit_solution(3891120701824352999)
XLA Ops:
  3.4 3.4 collective-permute-start.2
  6.8 4.5 collective-permute-start
  12.8 6.4 %collective-permute-done.2.refs_1_ = f32[1,1024,256]{2,1,0:T(8,128)S(1)} collective-permute-done((f32[1,1024,256]{2,1,0:T(8,128)S(1)}, f32[1,1024,256]{2,1,0:T(8,128)S(1)}, u32[]{:S(2)}, u32[]{:S(2)}) %collective-permute-start.2) | collective-permute-done | bytes 1048608 | tf_op jit(solution)/shard_map/ppermute | solution.py:341
  19.1 2.8 collective-permute-start.3
  22.2 4.1 dynamic-slice_multiply_fusion
  26.2 4.5 collective-permute-start.5
  32.0 2.3 collective-permute-done.3.refs_2_
  34.3 2.9 collective-permute-start.4
  37.2 2.2 collective-permute-done.1
  46.8 7.3 %collective-permute-done.5.refs_16_.refs_18_.refs_14_ = f32[128,2048]{1,0:T(8,128)} collective-permute-done((f32[128,2048]{1,0:T(8,128)}, f32[128,2048]{1,0:T(8,128)}, u32[]{:S(2)}, u32[]{:S(2)}) %collective-permute-start.5) | collective-permute-done | bytes 1048608 | tf_op jit(solution)/shard_map/ppermute | solution.py:24
  54.1 7.8 %collective-permute-done.6.refs_8_.refs_10_.refs_12_ = f32[128,2048]{1,0:T(8,128)} collective-permute-done((f32[128,2048]{1,0:T(8,128)S(1)}, f32[128,2048]{1,0:T(8,128)}, u32[]{:S(2)}, u32[]{:S(2)}) %collective-permute-start.6) | collective-permute-done | bytes 1048608 | tf_op jit(solution)/shard_map/ppermute | solution.py:29
  61.9 3.5 collective-permute-start.9
  66.6 17.7 %collective-permute-done.8 = f32[1024,256]{1,0:T(8,128)} collective-permute-done((f32[1024,256]{1,0:T(8,128)}, f32[1024,256]{1,0:T(8,128)}, u32[]{:S(2)}, u32[]{:S(2)}) %collective-permute-start.8) | collective-permute-done | bytes 1048608 | tf_op jit(solution)/shard_map/ppermute | solution.py:29
  84.3 2.1 select_bitcast_fusion.1
  86.5 1.9 pad_maximum_fusion.1.refs_0_
  89.3 2.6 all-to-all-start
  93.9 30.7 %all-to-all-done = s32[32,2,128]{2,1,0:T(2,128)S(1)} async-done(((s32[32,2,128]{2,1,0:T(2,128)}), s32[32,2,128]{2,1,0:T(2,128)S(1)}, u32[]{:S(2)}, u32[]{:S(2)}) %all-to-all-start) | async-done | bytes 32800 | tf_op jit(solution)/shard_map/all_to_all | solution.py:408
  128.7 1.7 collective-permute-start.13
  132.5 2.2 collective-permute-start.22
  140.6 4.5 collective-permute-start.15
  146.4 12.2 %collective-permute-done.14.refs_11_.refs_13_.refs_15_ = f32[128,2048]{1,0:T(8,128)} collective-permute-done((f32[128,2048]{1,0:T(8,128)}, f32[128,2048]{1,0:T(8,128)}, u32[]{:S(2)}, u32[]{:S(2)}) %collective-permute-start.14) | collective-permute-done | bytes 1048608 | tf_op jit(solution)/shard_map/ppermute | solution.py:29
  160.0 2.0 collective-permute-start.17
  165.4 3.2 collective-permute-done.15.refs_4_.refs_6_.refs_8_
  168.6 12.4 %collective-permute-done.16.refs_12_.refs_14_.refs_16_ = f32[128,2048]{1,0:T(8,128)S(1)} collective-permute-done((f32[128,2048]{1,0:T(8,128)}, f32[128,2048]{1,0:T(8,128)S(1)}, u32[]{:S(2)}, u32[]{:S(2)}) %collective-permute-start.16) | collective-permute-done | bytes 1048608 | tf_op jit(solution)/shard_map/ppermute | solution.py:29
  184.5 6.6 %collective-permute-done.17.refs_5_.refs_7_.refs_9_ = f32[128,2048]{1,0:T(8,128)S(1)} collective-permute-done((f32[128,2048]{1,0:T(8,128)S(1)}, f32[128,2048]{1,0:T(8,128)S(1)}, u32[]{:S(2)}, u32[]{:S(2)}) %collective-permute-start.17) | collective-permute-done | bytes 1048608 | tf_op jit(solution)/shard_map/ppermute | solution.py:327
  191.1 12.4 %collective-permute-done.18.refs_13_.refs_15_.refs_17_ = f32[128,2048]{1,0:T(8,128)S(1)} collective-permute-done((f32[128,2048]{1,0:T(8,128)}, f32[128,2048]{1,0:T(8,128)S(1)}, u32[]{:S(2)}, u32[]{:S(2)}) %collective-permute-start.18) | collective-permute-done | bytes 1048608 | tf_op jit(solution)/shard_map/ppermute | solution.py:29
  204.7 2.5 collective-permute-start.24
  208.6 12.4 %products.4 = f32[64,128,128]{2,1,0:T(8,128)} custom-call(s32[64]{0:T(128)S(1)} %slice_bitcast_fusion.13.table, s32[64]{0:T(128)S(1)} %slice_bitcast_fusion.12.full, s32[1]{0:T(128)S(1)} %bitcast.101, s32[4]{0:T(128)S(1)} %fusion.14.which, f32[1,1024,256]{2,1,0:T(8,128)S(1)} %bitcast.100, f32[1,1024,256]{2,1,0:T(8,128)S(1)} %copy-done.10, ...), custom_call_target="tpu_custom_call" | custom-call | flops 12884901888 | bytes 16777216 | tf_op jit(solution)/shard_map/products/pallas_call | solution.py:126
  221.0 5.0 %collective-permute-done.20.refs_18_.refs_22_ = f32[128,2048]{1,0:T(8,128)} collective-permute-done((f32[128,2048]{1,0:T(8,128)}, f32[128,2048]{1,0:T(8,128)}, u32[]{:S(2)}, u32[]{:S(2)}) %collective-permute-start.20) | collective-permute-done | bytes 1048608 | tf_op jit(solution)/shard_map/ppermute | solution.py:29
  227.2 1.8 collective-permute-start.26
  229.0 4.5 all-to-all-start.4
  233.7 13.6 %collective-permute-done.25.refs_19_.refs_23_ = f32[128,2048]{1,0:T(8,128)} collective-permute-done((f32[128,2048]{1,0:T(8,128)}, f32[128,2048]{1,0:T(8,128)}, u32[]{:S(2)}, u32[]{:S(2)}) %collective-permute-start.25) | collective-permute-done | bytes 1048608 | tf_op jit(solution)/shard_map/ppermute | solution.py:29
  250.0 9.9 %products.6 = (f32[32,128,128]{2,1,0:T(8,128)}, f32[32,128,128]{2,1,0:T(8,128)}, f32[32,128,128]{2,1,0:T(8,128)}, f32[32,128,128]{2,1,0:T(8,128)}) custom-call(s32[128]{0:T(128)S(1)} %bitcast.104, s32[128]{0:T(128)S(1)} %bitcast.105, s32[1]{0:T(128)} %bitcast.41.used, s32[4]{0:T(128)S(1)} %fusion.16.which, f32[3,1024,256]{2,1,0:T(8,128)} %pad_maximum_fusion.1.refs_0_, ...), custom_call_target="tpu_custom_call" | custom-call | flops 25769803776 | bytes 20971520 | tf_op jit(solution)/shard_map/products/pallas_call | solution.py:126
  259.9 13.6 %products.5 = f32[64,128,128]{2,1,0:T(8,128)} custom-call(s32[64]{0:T(128)S(1)} %slice_bitcast_fusion.11.table, s32[64]{0:T(128)S(1)} %slice_bitcast_fusion.10.full, s32[1]{0:T(128)} %bitcast.37.used, s32[4]{0:T(128)S(1)} %fusion.15.which, f32[3,1024,256]{2,1,0:T(8,128)} %pad_maximum_fusion.1.refs_0_, f32[3,1024,256]{2,1,0:T(8,128)} %collective-permute-done.21.refs_1_, ...), custom_call_target="tpu_custom_call" | custom-call | flops 12884901888 | bytes 16777216 | tf_op jit(solution)/shard_map/products/pallas_call | solution.py:126
  274.6 8.1 %all-to-all-done.4.got = f32[64,128,128]{2,1,0:T(8,128)} async-done(((f32[64,128,128]{2,1,0:T(8,128)}), f32[64,128,128]{2,1,0:T(8,128)}, u32[]{:S(2)}, u32[]{:S(2)}) %all-to-all-start.4) | async-done | bytes 4194336 | tf_op jit(solution)/shard_map/all_to_all | solution.py:378
  282.6 4.7 %all-to-all-start.3 = ((f32[64,128,128]{2,1,0:T(8,128)}), f32[64,128,128]{2,1,0:T(8,128)}, u32[]{:S(2)}, u32[]{:S(2)}) async-start(f32[64,128,128]{2,1,0:T(8,128)} %products.5), calls=%async_computation.3 | async-start | bytes 8388608 | tf_op jit(solution)/shard_map/all_to_all | solution.py:378
  290.0 15.2 %products.7 = f32[64,128,128]{2,1,0:T(8,128)} custom-call(s32[64]{0:T(128)S(1)} %slice_bitcast_fusion.9.table, s32[64]{0:T(128)S(1)} %slice_bitcast_fusion.8.full, s32[1]{0:T(128)} %bitcast.45.used, s32[4]{0:T(128)S(1)} %fusion.17.which, f32[3,1024,256]{2,1,0:T(8,128)} %pad_maximum_fusion.1.refs_0_, f32[3,1024,256]{2,1,0:T(8,128)} %collective-permute-done.21.refs_1_, ...), custom_call_target="tpu_custom_call" | custom-call | flops 12884901888 | bytes 16777216 | tf_op jit(solution)/shard_map/products/pallas_call | solution.py:126
  305.2 32.2 %collective-permute-done.28 = f32[32,128,128]{2,1,0:T(8,128)} collective-permute-done((f32[32,128,128]{2,1,0:T(8,128)}, f32[32,128,128]{2,1,0:T(8,128)}, u32[]{:S(2)}, u32[]{:S(2)}) %collective-permute-start.28) | collective-permute-done | bytes 2097184 | tf_op jit(solution)/shard_map/ppermute | solution.py:393
  337.4 4.6 %all-to-all-start.2 = ((f32[64,128,128]{2,1,0:T(8,128)}), f32[64,128,128]{2,1,0:T(8,128)}, u32[]{:S(2)}, u32[]{:S(2)}) async-start(f32[64,128,128]{2,1,0:T(8,128)} %products.7), calls=%async_computation.2 | async-start | bytes 8388608 | tf_op jit(solution)/shard_map/all_to_all | solution.py:378
  343.5 1.9 broadcast_select_fusion.1
  345.4 46.8 %collective-permute-done.29 = f32[32,128,128]{2,1,0:T(8,128)S(1)} collective-permute-done((f32[32,128,128]{2,1,0:T(8,128)}, f32[32,128,128]{2,1,0:T(8,128)S(1)}, u32[]{:S(2)}, u32[]{:S(2)}) %collective-permute-start.29) | collective-permute-done | bytes 2097184 | tf_op jit(solution)/shard_map/ppermute | solution.py:420
  392.4 2.4 pad_maximum_fusion
  394.9 4.6 %all-to-all-start.1 = ((f32[64,128,128]{2,1,0:T(8,128)}), f32[64,128,128]{2,1,0:T(8,128)}, u32[]{:S(2)}, u32[]{:S(2)}) async-start(f32[64,128,128]{2,1,0:T(8,128)} %pad_maximum_fusion), calls=%async_computation.1 | async-start | bytes 8388608 | tf_op jit(solution)/shard_map/all_to_all | solution.py:378
  399.5 9.8 %first_blocks.1.start = f32[128,128,128]{2,1,0:T(8,128)} custom-call(s32[64]{0:T(128)S(1)} %slice_bitcast_fusion.1.targets, f32[64,128,128]{2,1,0:T(8,128)} %all-to-all-done.4.got, f32[128,128,128]{2,1,0:T(8,128)} %bitcast.106), custom_call_target="tpu_custom_call" | custom-call | flops 1048576 | bytes 20971520 | tf_op jit(solution)/shard_map/first_blocks/pallas_call | solution.py:226
  409.3 6.9 %add_blocks.3.start = f32[128,128,128]{2,1,0:T(8,128)} custom-call(s32[64]{0:T(128)S(1)} %slice_bitcast_fusion.3.targets, s32[64]{0:T(128)S(1)} %slice_bitcast_fusion.2.leader, f32[64,128,128]{2,1,0:T(8,128)} %all-to-all-done.3.got, f32[128,128,128]{2,1,0:T(8,128)} %first_blocks.1.start), custom_call_target="tpu_custom_call", output_to_operand_aliasing={{}: (3, {})} | custom-call | flops 1048576 | bytes 12582912 | tf_op jit(solution)/shard_map/add_blocks/pallas_call | solution.py:191
  416.2 6.9 %add_blocks.4.start = f32[128,128,128]{2,1,0:T(8,128)} custom-call(s32[64]{0:T(128)S(1)} %get-tuple-element.588.targets, s32[64]{0:T(128)S(1)} %get-tuple-element.586.leader, f32[64,128,128]{2,1,0:T(8,128)} %all-to-all-done.2.got, f32[128,128,128]{2,1,0:T(8,128)} %add_blocks.3.start), custom_call_target="tpu_custom_call", output_to_operand_aliasing={{}: (3, {})} | custom-call | flops 1048576 | bytes 12582912 | tf_op jit(solution)/shard_map/add_blocks/pallas_call | solution.py:191
  423.1 25.5 %all-to-all-done.1.got = f32[64,128,128]{2,1,0:T(8,128)} async-done(((f32[64,128,128]{2,1,0:T(8,128)}), f32[64,128,128]{2,1,0:T(8,128)}, u32[]{:S(2)}, u32[]{:S(2)}) %all-to-all-start.1) | async-done | bytes 4194336 | tf_op jit(solution)/shard_map/all_to_all | solution.py:378
  448.6 6.9 %add_blocks.5 = f32[128,128,128]{2,1,0:T(8,128)} custom-call(s32[64]{0:T(128)S(1)} %get-tuple-element.589.targets, s32[64]{0:T(128)S(1)} %get-tuple-element.587.leader, f32[64,128,128]{2,1,0:T(8,128)} %all-to-all-done.1.got, f32[128,128,128]{2,1,0:T(8,128)} %add_blocks.4.start), custom_call_target="tpu_custom_call", output_to_operand_aliasing={{}: (3, {})} | custom-call | flops 1048576 | bytes 12582912 | tf_op jit(solution)/shard_map/add_blocks/pallas_call | solution.py:191
  (168 shorter events, 48.5 us)
Async XLA Ops:
  0.0 22.0 %copy-start.19 = (s32[4,16]{1,0:T(4,128)S(1)}, s32[4,16]{1,0:T(4,128)}, u32[]{:S(2)}) copy-start(s32[4,16]{1,0:T(4,128)} %param.18) | copy-start | bytes 772
  3.4 22.8 %copy-start.4 = (f32[1024,256]{1,0:T(8,128)}, f32[1024,256]{1,0:T(8,128)S(1)}, u32[]{:S(2)}) copy-start(f32[1024,256]{1,0:T(8,128)S(1)} %bitcast_multiply_fusion) | copy-start | bytes 3145732
  3.4 15.7 %collective-permute-start.2 = (f32[1,1024,256]{2,1,0:T(8,128)S(1)}, f32[1,1024,256]{2,1,0:T(8,128)S(1)}, u32[]{:S(2)}, u32[]{:S(2)}) collective-permute-start(f32[1,1024,256]{2,1,0:T(8,128)S(1)} %bitcast.99), channel_id=1, source_target_pairs={{1,0},{2,1},{3,2},{4,3},{5,4},{6,5},{7,6},{0,7},{9,8},{10,9},{11,1... | collective-permute-start | bytes 3145736 | tf_op jit(solution)/shard_map/ppermute | solution.py:341
  6.8 30.4 %collective-permute-start = (f32[1024,256]{1,0:T(8,128)S(1)}, f32[1024,256]{1,0:T(8,128)}, u32[]{:S(2)}, u32[]{:S(2)}) collective-permute-start(f32[1024,256]{1,0:T(8,128)S(1)} %bitcast_multiply_fusion), channel_id=1, source_target_pairs={{0,8},{8,16},{16,24},{1,9},{9,17},{17,25},{2,10},{10,18},{18,26},{... | collective-permute-start | bytes 3145736 | tf_op jit(solution)/shard_map/ppermute | solution.py:24
  11.3 28.1 %collective-permute-start.1 = (f32[1024,256]{1,0:T(8,128)S(1)}, f32[1024,256]{1,0:T(8,128)}, u32[]{:S(2)}, u32[]{:S(2)}) collective-permute-start(f32[1024,256]{1,0:T(8,128)S(1)} %bitcast_multiply_fusion), channel_id=1, source_target_pairs={{8,0},{16,8},{24,16},{9,1},{17,9},{25,17},{10,2},{18,10},{26,18},{... | collective-permute-start | bytes 3145736 | tf_op jit(solution)/shard_map/ppermute | solution.py:29
  19.1 15.1 %collective-permute-start.3 = (f32[1,1024,256]{2,1,0:T(8,128)S(1)}, f32[1,1024,256]{2,1,0:T(8,128)}, u32[]{:S(2)}, u32[]{:S(2)}) collective-permute-start(f32[1,1024,256]{2,1,0:T(8,128)S(1)} %collective-permute-done.2.refs_1_), channel_id=1, source_target_pairs={{1,0},{2,1},{3,2},{4,3},{5,4},{6,5},{7,6},{0,7},{9,8},{10,9},{11,1... | collective-permute-start | bytes 3145736 | tf_op jit(solution)/shard_map/ppermute | solution.py:341
  22.1 21.8 %copy-start.25 = (s32[4]{0:T(128)S(1)}, s32[4]{0:T(128)}, u32[]{:S(2)}) copy-start(s32[4]{0:T(128)} %constant.173.clone) | copy-start | bytes 52
  22.2 23.2 %copy-start.24 = (s32[4]{0:T(128)S(1)}, s32[4]{0:T(128)}, u32[]{:S(2)}) copy-start(s32[4]{0:T(128)} %constant.171.clone) | copy-start | bytes 52
  26.2 155.2 %copy-start = (f32[128,2048]{1,0:T(8,128)}, f32[128,2048]{1,0:T(8,128)S(1)}, u32[]{:S(2)}) copy-start(f32[128,2048]{1,0:T(8,128)S(1)} %get-tuple-element.536.refs_6_.refs_8_.refs_10_) | copy-start | bytes 3145732
  26.2 27.8 %collective-permute-start.5 = (f32[128,2048]{1,0:T(8,128)}, f32[128,2048]{1,0:T(8,128)}, u32[]{:S(2)}, u32[]{:S(2)}) collective-permute-start(f32[128,2048]{1,0:T(8,128)} %get-tuple-element.535.refs_20_.refs_16_), channel_id=1, source_target_pairs={{0,8},{8,16},{16,24},{1,9},{9,17},{17,25},{2,10},{10,18},{18,26},{... | collective-permute-start | bytes 3145736 | tf_op jit(solution)/shard_map/ppermute | solution.py:24
  30.7 31.1 %collective-permute-start.6 = (f32[128,2048]{1,0:T(8,128)S(1)}, f32[128,2048]{1,0:T(8,128)}, u32[]{:S(2)}, u32[]{:S(2)}) collective-permute-start(f32[128,2048]{1,0:T(8,128)S(1)} %get-tuple-element.536.refs_6_.refs_8_.refs_10_), channel_id=1, source_target_pairs={{8,0},{16,8},{24,16},{9,1},{17,9},{25,17},{10,2},{18,10},{26,18},{... | collective-permute-start | bytes 3145736 | tf_op jit(solution)/shard_map/ppermute | solution.py:29
  34.3 27.6 %collective-permute-start.4 = (f32[1,1024,256]{2,1,0:T(8,128)}, f32[1,1024,256]{2,1,0:T(8,128)S(1)}, u32[]{:S(2)}, u32[]{:S(2)}) collective-permute-start(f32[1,1024,256]{2,1,0:T(8,128)} %collective-permute-done.3.refs_2_), channel_id=1, source_target_pairs={{1,0},{2,1},{3,2},{4,3},{5,4},{6,5},{7,6},{0,7},{9,8},{10,9},{11,1... | collective-permute-start | bytes 3145736 | tf_op jit(solution)/shard_map/ppermute | solution.py:341
  40.0 26.6 %collective-permute-start.7 = (f32[1024,256]{1,0:T(8,128)}, f32[1024,256]{1,0:T(8,128)S(1)}, u32[]{:S(2)}, u32[]{:S(2)}) collective-permute-start(f32[1024,256]{1,0:T(8,128)} %collective-permute-done), channel_id=1, source_target_pairs={{8,16},{16,24},{9,17},{17,25},{10,18},{18,26},{11,19},{19,27},{12,... | collective-permute-start | bytes 3145736 | tf_op jit(solution)/shard_map/ppermute | solution.py:24
  40.7 43.6 %collective-permute-start.8 = (f32[1024,256]{1,0:T(8,128)}, f32[1024,256]{1,0:T(8,128)}, u32[]{:S(2)}, u32[]{:S(2)}) collective-permute-start(f32[1024,256]{1,0:T(8,128)} %collective-permute-done.1), channel_id=1, source_target_pairs={{8,0},{16,8},{9,1},{17,9},{10,2},{18,10},{11,3},{19,11},{12,4},{20... | collective-permute-start | bytes 3145736 | tf_op jit(solution)/shard_map/ppermute | solution.py:29
  61.9 24.6 %copy-start.11 = (f32[1,1024,256]{2,1,0:T(8,128)}, f32[1,1024,256]{2,1,0:T(8,128)S(1)}, u32[]{:S(2)}) copy-start(f32[1,1024,256]{2,1,0:T(8,128)S(1)} %collective-permute-done.4.refs_3_) | copy-start | bytes 3145732
  61.9 62.8 %collective-permute-start.9 = (f32[128,2048]{1,0:T(8,128)}, f32[128,2048]{1,0:T(8,128)}, u32[]{:S(2)}, u32[]{:S(2)}) collective-permute-start(f32[128,2048]{1,0:T(8,128)} %get-tuple-element.537.refs_21_.refs_17_), channel_id=1, source_target_pairs={{0,8},{8,16},{16,24},{1,9},{9,17},{17,25},{2,10},{10,18},{18,26},{... | collective-permute-start | bytes 3145736 | tf_op jit(solution)/shard_map/ppermute | solution.py:24
  65.3 59.3 %collective-permute-start.10 = (f32[128,2048]{1,0:T(8,128)}, f32[128,2048]{1,0:T(8,128)}, u32[]{:S(2)}, u32[]{:S(2)}) collective-permute-start(f32[128,2048]{1,0:T(8,128)} %get-tuple-element.538.refs_7_.refs_9_.refs_11_), channel_id=1, source_target_pairs={{8,0},{16,8},{24,16},{9,1},{17,9},{25,17},{10,2},{18,10},{26,18},{... | collective-permute-start | bytes 3145736 | tf_op jit(solution)/shard_map/ppermute | solution.py:29
  88.3 44.2 %collective-permute-start.21 = (f32[3,1024,256]{2,1,0:T(8,128)}, f32[3,1024,256]{2,1,0:T(8,128)}, u32[]{:S(2)}, u32[]{:S(2)}) collective-permute-start(f32[3,1024,256]{2,1,0:T(8,128)} %pad_maximum_fusion.1.refs_0_), channel_id=1, source_target_pairs={{1,0},{2,1},{3,2},{4,3},{5,4},{6,5},{7,6},{0,7},{9,8},{10,9},{11,1... | collective-permute-start | bytes 9437192 | tf_op jit(solution)/shard_map/ppermute | solution.py:341
  89.3 35.4 %all-to-all-start = ((s32[32,2,128]{2,1,0:T(2,128)}), s32[32,2,128]{2,1,0:T(2,128)S(1)}, u32[]{:S(2)}, u32[]{:S(2)}) async-start(s32[32,2,128]{2,1,0:T(2,128)} %broadcast_in_dim.133), calls=%async_computation | async-start | bytes 65536 | tf_op jit(solution)/shard_map/all_to_all | solution.py:408
  91.9 47.6 %collective-permute-start.11 = (f32[128,2048]{1,0:T(8,128)}, f32[128,2048]{1,0:T(8,128)S(1)}, u32[]{:S(2)}, u32[]{:S(2)}) collective-permute-start(f32[128,2048]{1,0:T(8,128)} %collective-permute-done.5.refs_16_.refs_18_.refs_14_), channel_id=1, source_target_pairs={{8,16},{16,24},{9,17},{17,25},{10,18},{18,26},{11,19},{19,27},{12,... | collective-permute-start | bytes 3145736 | tf_op jit(solution)/shard_map/ppermute | solution.py:24
  92.6 46.9 %collective-permute-start.12 = (f32[128,2048]{1,0:T(8,128)}, f32[128,2048]{1,0:T(8,128)}, u32[]{:S(2)}, u32[]{:S(2)}) collective-permute-start(f32[128,2048]{1,0:T(8,128)} %collective-permute-done.6.refs_8_.refs_10_.refs_12_), channel_id=1, source_target_pairs={{8,0},{16,8},{9,1},{17,9},{10,2},{18,10},{11,3},{19,11},{12,4},{20... | collective-permute-start | bytes 3145736 | tf_op jit(solution)/shard_map/ppermute | solution.py:29
  128.7 17.7 %collective-permute-start.13 = (f32[128,2048]{1,0:T(8,128)}, f32[128,2048]{1,0:T(8,128)}, u32[]{:S(2)}, u32[]{:S(2)}) collective-permute-start(f32[128,2048]{1,0:T(8,128)} %collective-permute-done.9.refs_17_.refs_19_.refs_15_), channel_id=1, source_target_pairs={{8,16},{16,24},{9,17},{17,25},{10,18},{18,26},{11,19},{19,27},{12,... | collective-permute-start | bytes 3145736 | tf_op jit(solution)/shard_map/ppermute | solution.py:24
  130.4 28.3 %collective-permute-start.14 = (f32[128,2048]{1,0:T(8,128)}, f32[128,2048]{1,0:T(8,128)}, u32[]{:S(2)}, u32[]{:S(2)}) collective-permute-start(f32[128,2048]{1,0:T(8,128)} %collective-permute-done.10.refs_9_.refs_11_.refs_13_), channel_id=1, source_target_pairs={{8,0},{16,8},{9,1},{17,9},{10,2},{18,10},{11,3},{19,11},{12,4},{20... | collective-permute-start | bytes 3145736 | tf_op jit(solution)/shard_map/ppermute | solution.py:29
  132.5 48.5 %collective-permute-start.22 = (f32[3,1024,256]{2,1,0:T(8,128)}, f32[3,1024,256]{2,1,0:T(8,128)}, u32[]{:S(2)}, u32[]{:S(2)}) collective-permute-start(f32[3,1024,256]{2,1,0:T(8,128)} %collective-permute-done.21.refs_1_), channel_id=1, source_target_pairs={{1,0},{2,1},{3,2},{4,3},{5,4},{6,5},{7,6},{0,7},{9,8},{10,9},{11,1... | collective-permute-start | bytes 9437192 | tf_op jit(solution)/shard_map/ppermute | solution.py:341
  140.6 62.9 %copy-start.15 = (f32[128,2048]{1,0:T(8,128)S(1)}, f32[128,2048]{1,0:T(8,128)}, u32[]{:S(2)}) copy-start(f32[128,2048]{1,0:T(8,128)} %get-tuple-element.538.refs_7_.refs_9_.refs_11_) | copy-start | bytes 3145732
  140.6 28.0 %collective-permute-start.15 = (f32[128,2048]{1,0:T(8,128)S(1)}, f32[128,2048]{1,0:T(8,128)S(1)}, u32[]{:S(2)}, u32[]{:S(2)}) collective-permute-start(f32[128,2048]{1,0:T(8,128)S(1)} %broadcast_select_fusion.7), channel_id=1, source_target_pairs={{0,8},{8,16},{16,24},{1,9},{9,17},{17,25},{2,10},{10,18},{18,26},{... | collective-permute-start | bytes 3145736 | tf_op jit(solution)/shard_map/ppermute | solution.py:327
  145.1 35.9 %collective-permute-start.16 = (f32[128,2048]{1,0:T(8,128)}, f32[128,2048]{1,0:T(8,128)S(1)}, u32[]{:S(2)}, u32[]{:S(2)}) collective-permute-start(f32[128,2048]{1,0:T(8,128)} %collective-permute-done.12.refs_10_.refs_12_.refs_14_), channel_id=1, source_target_pairs={{8,0},{9,1},{10,2},{11,3},{12,4},{13,5},{14,6},{15,7}} | collective-permute-start | bytes 3145736 | tf_op jit(solution)/shard_map/ppermute | solution.py:29
  160.0 31.1 %collective-permute-start.17 = (f32[128,2048]{1,0:T(8,128)S(1)}, f32[128,2048]{1,0:T(8,128)S(1)}, u32[]{:S(2)}, u32[]{:S(2)}) collective-permute-start(f32[128,2048]{1,0:T(8,128)S(1)} %broadcast_select_fusion.6), channel_id=1, source_target_pairs={{0,8},{8,16},{16,24},{1,9},{9,17},{17,25},{2,10},{10,18},{18,26},{... | collective-permute-start | bytes 3145736 | tf_op jit(solution)/shard_map/ppermute | solution.py:327
  162.0 41.5 %collective-permute-start.18 = (f32[128,2048]{1,0:T(8,128)}, f32[128,2048]{1,0:T(8,128)S(1)}, u32[]{:S(2)}, u32[]{:S(2)}) collective-permute-start(f32[128,2048]{1,0:T(8,128)} %collective-permute-done.14.refs_11_.refs_13_.refs_15_), channel_id=1, source_target_pairs={{8,0},{9,1},{10,2},{11,3},{12,4},{13,5},{14,6},{15,7}} | collective-permute-start | bytes 3145736 | tf_op jit(solution)/shard_map/ppermute | solution.py:29
  165.4 43.2 %copy-start.5 = (f32[1024,256]{1,0:T(8,128)S(1)}, f32[1024,256]{1,0:T(8,128)}, u32[]{:S(2)}) copy-start(f32[1024,256]{1,0:T(8,128)} %copy-done.4) | copy-start | bytes 3145732
  165.4 43.2 %copy-start.10 = (f32[1,1024,256]{2,1,0:T(8,128)S(1)}, f32[1,1024,256]{2,1,0:T(8,128)}, u32[]{:S(2)}) copy-start(f32[1,1024,256]{2,1,0:T(8,128)} %copy-done.9) | copy-start | bytes 3145732
  165.4 43.2 %copy-start.12 = (f32[1,1024,256]{2,1,0:T(8,128)S(1)}, f32[1,1024,256]{2,1,0:T(8,128)}, u32[]{:S(2)}) copy-start(f32[1,1024,256]{2,1,0:T(8,128)} %copy-done.11) | copy-start | bytes 3145732
  181.0 23.7 %copy-start.22 = (f32[128,2048]{1,0:T(8,128)}, f32[128,2048]{1,0:T(8,128)S(1)}, u32[]{:S(2)}) copy-start(f32[128,2048]{1,0:T(8,128)S(1)} %collective-permute-done.16.refs_12_.refs_14_.refs_16_) | copy-start | bytes 3145732
  181.0 66.3 %collective-permute-start.23 = (f32[3,1024,256]{2,1,0:T(8,128)}, f32[3,1024,256]{2,1,0:T(8,128)}, u32[]{:S(2)}, u32[]{:S(2)}) collective-permute-start(f32[3,1024,256]{2,1,0:T(8,128)} %collective-permute-done.22.refs_2_), channel_id=1, source_target_pairs={{1,0},{2,1},{3,2},{4,3},{5,4},{6,5},{7,6},{0,7},{9,8},{10,9},{11,1... | collective-permute-start | bytes 9437192 | tf_op jit(solution)/shard_map/ppermute | solution.py:341
  181.6 39.4 %collective-permute-start.19 = (f32[128,2048]{1,0:T(8,128)S(1)}, f32[128,2048]{1,0:T(8,128)S(1)}, u32[]{:S(2)}, u32[]{:S(2)}) collective-permute-start(f32[128,2048]{1,0:T(8,128)S(1)} %broadcast_select_fusion.5), channel_id=1, source_target_pairs={{0,8},{8,16},{16,24},{1,9},{9,17},{17,25},{2,10},{10,18},{18,26},{... | collective-permute-start | bytes 3145736 | tf_op jit(solution)/shard_map/ppermute | solution.py:327
  183.2 42.8 %collective-permute-start.20 = (f32[128,2048]{1,0:T(8,128)}, f32[128,2048]{1,0:T(8,128)}, u32[]{:S(2)}, u32[]{:S(2)}) collective-permute-start(f32[128,2048]{1,0:T(8,128)} %get-tuple-element.535.refs_20_.refs_16_), channel_id=1, source_target_pairs={{8,0},{16,8},{9,1},{17,9},{10,2},{18,10},{11,3},{19,11},{12,4},{20... | collective-permute-start | bytes 3145736 | tf_op jit(solution)/shard_map/ppermute | solution.py:29
  204.7 29.0 %collective-permute-start.24 = (f32[128,2048]{1,0:T(8,128)}, f32[128,2048]{1,0:T(8,128)}, u32[]{:S(2)}, u32[]{:S(2)}) collective-permute-start(f32[128,2048]{1,0:T(8,128)} %broadcast_select_fusion.4), channel_id=1, source_target_pairs={{0,8},{8,16},{16,24},{1,9},{9,17},{17,25},{2,10},{10,18},{18,26},{... | collective-permute-start | bytes 3145736 | tf_op jit(solution)/shard_map/ppermute | solution.py:327
  207.3 40.0 %collective-permute-start.25 = (f32[128,2048]{1,0:T(8,128)}, f32[128,2048]{1,0:T(8,128)}, u32[]{:S(2)}, u32[]{:S(2)}) collective-permute-start(f32[128,2048]{1,0:T(8,128)} %get-tuple-element.537.refs_21_.refs_17_), channel_id=1, source_target_pairs={{8,0},{16,8},{9,1},{17,9},{10,2},{18,10},{11,3},{19,11},{12,4},{20... | collective-permute-start | bytes 3145736 | tf_op jit(solution)/shard_map/ppermute | solution.py:29
  227.2 46.3 %collective-permute-start.26 = (f32[128,2048]{1,0:T(8,128)S(1)}, f32[128,2048]{1,0:T(8,128)}, u32[]{:S(2)}, u32[]{:S(2)}) collective-permute-start(f32[128,2048]{1,0:T(8,128)S(1)} %broadcast_select_fusion.3), channel_id=1, source_target_pairs={{16,24},{17,25},{18,26},{19,27},{20,28},{21,29},{22,30},{23,31}} | collective-permute-start | bytes 3145736 | tf_op jit(solution)/shard_map/ppermute | solution.py:327
  229.0 53.7 %all-to-all-start.4 = ((f32[64,128,128]{2,1,0:T(8,128)}), f32[64,128,128]{2,1,0:T(8,128)}, u32[]{:S(2)}, u32[]{:S(2)}) async-start(f32[64,128,128]{2,1,0:T(8,128)} %products.4), calls=%async_computation.4 | async-start | bytes 8388608 | tf_op jit(solution)/shard_map/all_to_all | solution.py:378
  249.3 24.3 %collective-permute-start.27 = (f32[128,2048]{1,0:T(8,128)S(1)}, f32[128,2048]{1,0:T(8,128)S(1)}, u32[]{:S(2)}, u32[]{:S(2)}) collective-permute-start(f32[128,2048]{1,0:T(8,128)S(1)} %broadcast_select_fusion.2), channel_id=1, source_target_pairs={{16,24},{17,25},{18,26},{19,27},{20,28},{21,29},{22,30},{23,31}} | collective-permute-start | bytes 3145736 | tf_op jit(solution)/shard_map/ppermute | solution.py:327
  282.6 54.8 %all-to-all-start.3 = ((f32[64,128,128]{2,1,0:T(8,128)}), f32[64,128,128]{2,1,0:T(8,128)}, u32[]{:S(2)}, u32[]{:S(2)}) async-start(f32[64,128,128]{2,1,0:T(8,128)} %products.5), calls=%async_computation.3 | async-start | bytes 8388608 | tf_op jit(solution)/shard_map/all_to_all | solution.py:378
  287.3 50.1 %collective-permute-start.28 = (f32[32,128,128]{2,1,0:T(8,128)}, f32[32,128,128]{2,1,0:T(8,128)}, u32[]{:S(2)}, u32[]{:S(2)}) collective-permute-start(f32[32,128,128]{2,1,0:T(8,128)} %get-tuple-element.533), channel_id=1, source_target_pairs={{8,0},{16,24},{9,1},{17,25},{10,2},{18,26},{11,3},{19,27},{12,4},{... | collective-permute-start | bytes 6291464 | tf_op jit(solution)/shard_map/ppermute | solution.py:393
  305.2 38.3 %copy-start.17 = (f32[32,128,128]{2,1,0:T(8,128)S(1)}, f32[32,128,128]{2,1,0:T(8,128)}, u32[]{:S(2)}) copy-start(f32[32,128,128]{2,1,0:T(8,128)} %get-tuple-element.571) | copy-start | bytes 6291460
  337.4 57.5 %all-to-all-start.2 = ((f32[64,128,128]{2,1,0:T(8,128)}), f32[64,128,128]{2,1,0:T(8,128)}, u32[]{:S(2)}, u32[]{:S(2)}) async-start(f32[64,128,128]{2,1,0:T(8,128)} %products.7), calls=%async_computation.2 | async-start | bytes 8388608 | tf_op jit(solution)/shard_map/all_to_all | solution.py:378
  342.0 50.1 %copy-start.16 = (f32[32,128,128]{2,1,0:T(8,128)S(1)}, f32[32,128,128]{2,1,0:T(8,128)}, u32[]{:S(2)}) copy-start(f32[32,128,128]{2,1,0:T(8,128)} %get-tuple-element.573) | copy-start | bytes 6291460
  342.1 50.1 %collective-permute-start.29 = (f32[32,128,128]{2,1,0:T(8,128)}, f32[32,128,128]{2,1,0:T(8,128)S(1)}, u32[]{:S(2)}, u32[]{:S(2)}) collective-permute-start(f32[32,128,128]{2,1,0:T(8,128)} %get-tuple-element.572), channel_id=1, source_target_pairs={{8,0},{16,24},{9,1},{17,25},{10,2},{18,26},{11,3},{19,27},{12,4},{... | collective-permute-start | bytes 6291464 | tf_op jit(solution)/shard_map/ppermute | solution.py:420
  394.9 53.7 %all-to-all-start.1 = ((f32[64,128,128]{2,1,0:T(8,128)}), f32[64,128,128]{2,1,0:T(8,128)}, u32[]{:S(2)}, u32[]{:S(2)}) async-start(f32[64,128,128]{2,1,0:T(8,128)} %pad_maximum_fusion), calls=%async_computation.1 | async-start | bytes 8388608 | tf_op jit(solution)/shard_map/all_to_all | solution.py:378
  (14 other events, 159.6 us)

commit v7 on v6

--- a/solution.py
+++ b/solution.py
@@ -160,28 +160,43 @@
     def out_copy(slot):
         return pltpu.make_async_copy(total.at[slot], out.at[targets[slot]], out_sem.at[slot])
 
-    def every(leads, work):
+    def every(work):
         @pl.loop(0, slots)
         def _(slot):
-            there = targets[slot] >= 0
-            if leads:
-                there = jnp.logical_and(there, leader[slot] == slot)
-
-            @pl.when(there)
+            @pl.when(targets[slot] >= 0)
             def _():
-                work(slot)
-
-    every(True, lambda slot: start_copy(slot).start())
-    every(False, lambda slot: got_copy(slot).start())
-    every(True, lambda slot: start_copy(slot).wait())
-
-    def add(slot):
+                work(slot, leader[slot])
+
+    def fetch(slot, lead):
+        got_copy(slot).start()
+
+        @pl.when(lead == slot)
+        def _():
+            start_copy(slot).start()
+
+    def add(slot, lead):
         got_copy(slot).wait()
-        total[leader[slot]] = total[leader[slot]] + got_in[slot]
-
-    every(False, add)
-    every(True, lambda slot: out_copy(slot).start())
-    every(True, lambda slot: out_copy(slot).wait())
+
+        @pl.when(lead == slot)
+        def _():
+            start_copy(slot).wait()
+
+        total[lead] = total[lead] + got_in[slot]
+
+    def store(slot, lead):
+        @pl.when(lead == slot)
+        def _():
+            out_copy(slot).start()
+
+    def stored(slot, lead):
+        @pl.when(lead == slot)
+        def _():
+            out_copy(slot).wait()
+
+    every(fetch)
+    every(add)
+    every(store)
+    every(stored)
 
 
 def add_blocks(targets, leader, got, start):

time: 460 us -> 461 us (level)
  no operation moved by 1% of the time
where the time goes in v7:
time: 461 us; the launch traced here: 455 us
  waiting for transfers between devices  255 us (55%)
  Pallas kernels  78.9 us (17%)
  starting transfers between devices  77 us (17%)
  other arithmetic  28.2 us (6%)
  local copies, waits for them, and re-layouts  12.6 us (3%)
    ppermute x10, waiting for transfers between devices, down_step(): return lax.ppermute(value, 'row', pairs) if pairs else None  83.3 us
    pallas_call x4, Pallas kernels, products(): pl.pallas_call(functools.partial(product_kernel, place, choices, pieces),...  49.7 us
    ppermute x1, waiting for transfers between devices, per_device(): far = [held['half'], lax.ppermute(held['side', 3], 'row', beside)]  46.8 us
    all_to_all x4, waiting for transfers between devices, exchange(): lax.all_to_all(blocks, 'col', split_axis=0, concat_axis=0, tiled=True)  34.5 us
    ppermute x1, waiting for transfers between devices, per_device(): lax.ppermute(held['side', 2], 'row', beside)  33.6 us
    all_to_all x1, waiting for transfers between devices, per_device(): every = lax.all_to_all(held['owners'], ('row', 'col'), 0, 0, tiled=True)  30.7 us
    pallas_call x3, Pallas kernels, add_blocks(): pl.pallas_call(add_kernel, out_shape=jax.ShapeDtypeStruct(start.shape, jn...  19.6 us
    all_to_all x4, starting transfers between devices, exchange(): lax.all_to_all(blocks, 'col', split_axis=0, concat_axis=0, tiled=True)  18.4 us
  transfers between devices with their start and end apart: 35, of which 19 were waited for; matrix products, arithmetic and copies ran while one was open for 8% of the time, Pallas kernels for 16%

profile of v7, /device:TPU:0, one launch (start us, length us, event | category | flops | bytes accessed | tf_op | source)
XLA Modules:
  0.0 455.3 jit_solution(12125815946642874442)
XLA Ops:
  3.4 3.4 collective-permute-start.2
  6.8 4.5 collective-permute-start
  12.8 6.4 %collective-permute-done.2.refs_1_ = f32[1,1024,256]{2,1,0:T(8,128)S(1)} collective-permute-done((f32[1,1024,256]{2,1,0:T(8,128)S(1)}, f32[1,1024,256]{2,1,0:T(8,128)S(1)}, u32[]{:S(2)}, u32[]{:S(2)}) %collective-permute-start.2) | collective-permute-done | bytes 1048608 | tf_op jit(solution)/shard_map/ppermute | solution.py:356
  19.1 2.8 collective-permute-start.3
  22.2 4.1 dynamic-slice_multiply_fusion
  26.2 4.5 collective-permute-start.5
  32.0 2.3 collective-permute-done.3.refs_2_
  34.3 2.9 collective-permute-start.4
  37.2 2.2 collective-permute-done.1
  46.8 7.3 %collective-permute-done.5.refs_16_.refs_18_.refs_14_ = f32[128,2048]{1,0:T(8,128)} collective-permute-done((f32[128,2048]{1,0:T(8,128)}, f32[128,2048]{1,0:T(8,128)}, u32[]{:S(2)}, u32[]{:S(2)}) %collective-permute-start.5) | collective-permute-done | bytes 1048608 | tf_op jit(solution)/shard_map/ppermute | solution.py:24
  54.1 7.8 %collective-permute-done.6.refs_8_.refs_10_.refs_12_ = f32[128,2048]{1,0:T(8,128)} collective-permute-done((f32[128,2048]{1,0:T(8,128)S(1)}, f32[128,2048]{1,0:T(8,128)}, u32[]{:S(2)}, u32[]{:S(2)}) %collective-permute-start.6) | collective-permute-done | bytes 1048608 | tf_op jit(solution)/shard_map/ppermute | solution.py:29
  61.9 3.5 collective-permute-start.9
  66.6 17.7 %collective-permute-done.8 = f32[1024,256]{1,0:T(8,128)} collective-permute-done((f32[1024,256]{1,0:T(8,128)}, f32[1024,256]{1,0:T(8,128)}, u32[]{:S(2)}, u32[]{:S(2)}) %collective-permute-start.8) | collective-permute-done | bytes 1048608 | tf_op jit(solution)/shard_map/ppermute | solution.py:29
  84.3 2.1 select_bitcast_fusion.1
  86.5 1.9 pad_maximum_fusion.1.refs_0_
  89.3 2.6 all-to-all-start
  93.9 30.7 %all-to-all-done = s32[32,2,128]{2,1,0:T(2,128)S(1)} async-done(((s32[32,2,128]{2,1,0:T(2,128)}), s32[32,2,128]{2,1,0:T(2,128)S(1)}, u32[]{:S(2)}, u32[]{:S(2)}) %all-to-all-start) | async-done | bytes 32800 | tf_op jit(solution)/shard_map/all_to_all | solution.py:423
  128.7 1.7 collective-permute-start.13
  132.5 2.2 collective-permute-start.22
  140.6 4.5 collective-permute-start.15
  146.4 12.2 %collective-permute-done.14.refs_11_.refs_13_.refs_15_ = f32[128,2048]{1,0:T(8,128)} collective-permute-done((f32[128,2048]{1,0:T(8,128)}, f32[128,2048]{1,0:T(8,128)}, u32[]{:S(2)}, u32[]{:S(2)}) %collective-permute-start.14) | collective-permute-done | bytes 1048608 | tf_op jit(solution)/shard_map/ppermute | solution.py:29
  160.0 2.0 collective-permute-start.17
  165.4 3.2 collective-permute-done.15.refs_4_.refs_6_.refs_8_
  168.6 12.4 %collective-permute-done.16.refs_12_.refs_14_.refs_16_ = f32[128,2048]{1,0:T(8,128)S(1)} collective-permute-done((f32[128,2048]{1,0:T(8,128)}, f32[128,2048]{1,0:T(8,128)S(1)}, u32[]{:S(2)}, u32[]{:S(2)}) %collective-permute-start.16) | collective-permute-done | bytes 1048608 | tf_op jit(solution)/shard_map/ppermute | solution.py:29
  184.5 6.6 %collective-permute-done.17.refs_5_.refs_7_.refs_9_ = f32[128,2048]{1,0:T(8,128)S(1)} collective-permute-done((f32[128,2048]{1,0:T(8,128)S(1)}, f32[128,2048]{1,0:T(8,128)S(1)}, u32[]{:S(2)}, u32[]{:S(2)}) %collective-permute-start.17) | collective-permute-done | bytes 1048608 | tf_op jit(solution)/shard_map/ppermute | solution.py:342
  191.1 12.4 %collective-permute-done.18.refs_13_.refs_15_.refs_17_ = f32[128,2048]{1,0:T(8,128)S(1)} collective-permute-done((f32[128,2048]{1,0:T(8,128)}, f32[128,2048]{1,0:T(8,128)S(1)}, u32[]{:S(2)}, u32[]{:S(2)}) %collective-permute-start.18) | collective-permute-done | bytes 1048608 | tf_op jit(solution)/shard_map/ppermute | solution.py:29
  204.7 2.5 collective-permute-start.24
  208.6 12.3 %products.4 = f32[64,128,128]{2,1,0:T(8,128)} custom-call(s32[64]{0:T(128)S(1)} %slice_bitcast_fusion.13.table, s32[64]{0:T(128)S(1)} %slice_bitcast_fusion.12.full, s32[1]{0:T(128)S(1)} %bitcast.101, s32[4]{0:T(128)S(1)} %fusion.14.which, f32[1,1024,256]{2,1,0:T(8,128)S(1)} %bitcast.100, f32[1,1024,256]{2,1,0:T(8,128)S(1)} %copy-done.10, ...), custom_call_target="tpu_custom_call" | custom-call | flops 12884901888 | bytes 16777216 | tf_op jit(solution)/shard_map/products/pallas_call | solution.py:126
  221.0 5.1 %collective-permute-done.20.refs_18_.refs_22_ = f32[128,2048]{1,0:T(8,128)} collective-permute-done((f32[128,2048]{1,0:T(8,128)}, f32[128,2048]{1,0:T(8,128)}, u32[]{:S(2)}, u32[]{:S(2)}) %collective-permute-start.20) | collective-permute-done | bytes 1048608 | tf_op jit(solution)/shard_map/ppermute | solution.py:29
  227.2 1.8 collective-permute-start.26
  229.0 4.5 all-to-all-start.4
  233.7 13.6 %collective-permute-done.25.refs_19_.refs_23_ = f32[128,2048]{1,0:T(8,128)} collective-permute-done((f32[128,2048]{1,0:T(8,128)}, f32[128,2048]{1,0:T(8,128)}, u32[]{:S(2)}, u32[]{:S(2)}) %collective-permute-start.25) | collective-permute-done | bytes 1048608 | tf_op jit(solution)/shard_map/ppermute | solution.py:29
  250.0 9.9 %products.6 = (f32[32,128,128]{2,1,0:T(8,128)}, f32[32,128,128]{2,1,0:T(8,128)}, f32[32,128,128]{2,1,0:T(8,128)}, f32[32,128,128]{2,1,0:T(8,128)}) custom-call(s32[128]{0:T(128)S(1)} %bitcast.104, s32[128]{0:T(128)S(1)} %bitcast.105, s32[1]{0:T(128)} %bitcast.41.used, s32[4]{0:T(128)S(1)} %fusion.16.which, f32[3,1024,256]{2,1,0:T(8,128)} %pad_maximum_fusion.1.refs_0_, ...), custom_call_target="tpu_custom_call" | custom-call | flops 25769803776 | bytes 20971520 | tf_op jit(solution)/shard_map/products/pallas_call | solution.py:126
  259.9 13.6 %products.5 = f32[64,128,128]{2,1,0:T(8,128)} custom-call(s32[64]{0:T(128)S(1)} %slice_bitcast_fusion.11.table, s32[64]{0:T(128)S(1)} %slice_bitcast_fusion.10.full, s32[1]{0:T(128)} %bitcast.37.used, s32[4]{0:T(128)S(1)} %fusion.15.which, f32[3,1024,256]{2,1,0:T(8,128)} %pad_maximum_fusion.1.refs_0_, f32[3,1024,256]{2,1,0:T(8,128)} %collective-permute-done.21.refs_1_, ...), custom_call_target="tpu_custom_call" | custom-call | flops 12884901888 | bytes 16777216 | tf_op jit(solution)/shard_map/products/pallas_call | solution.py:126
  274.5 8.1 %all-to-all-done.4.got = f32[64,128,128]{2,1,0:T(8,128)} async-done(((f32[64,128,128]{2,1,0:T(8,128)}), f32[64,128,128]{2,1,0:T(8,128)}, u32[]{:S(2)}, u32[]{:S(2)}) %all-to-all-start.4) | async-done | bytes 4194336 | tf_op jit(solution)/shard_map/all_to_all | solution.py:393
  282.6 4.7 %all-to-all-start.3 = ((f32[64,128,128]{2,1,0:T(8,128)}), f32[64,128,128]{2,1,0:T(8,128)}, u32[]{:S(2)}, u32[]{:S(2)}) async-start(f32[64,128,128]{2,1,0:T(8,128)} %products.5), calls=%async_computation.3 | async-start | bytes 8388608 | tf_op jit(solution)/shard_map/all_to_all | solution.py:393
  290.0 13.8 %products.7 = f32[64,128,128]{2,1,0:T(8,128)} custom-call(s32[64]{0:T(128)S(1)} %slice_bitcast_fusion.9.table, s32[64]{0:T(128)S(1)} %slice_bitcast_fusion.8.full, s32[1]{0:T(128)} %bitcast.45.used, s32[4]{0:T(128)S(1)} %fusion.17.which, f32[3,1024,256]{2,1,0:T(8,128)} %pad_maximum_fusion.1.refs_0_, f32[3,1024,256]{2,1,0:T(8,128)} %collective-permute-done.21.refs_1_, ...), custom_call_target="tpu_custom_call" | custom-call | flops 12884901888 | bytes 16777216 | tf_op jit(solution)/shard_map/products/pallas_call | solution.py:126
  303.8 33.6 %collective-permute-done.28 = f32[32,128,128]{2,1,0:T(8,128)} collective-permute-done((f32[32,128,128]{2,1,0:T(8,128)}, f32[32,128,128]{2,1,0:T(8,128)}, u32[]{:S(2)}, u32[]{:S(2)}) %collective-permute-start.28) | collective-permute-done | bytes 2097184 | tf_op jit(solution)/shard_map/ppermute | solution.py:408
  337.4 4.6 %all-to-all-start.2 = ((f32[64,128,128]{2,1,0:T(8,128)}), f32[64,128,128]{2,1,0:T(8,128)}, u32[]{:S(2)}, u32[]{:S(2)}) async-start(f32[64,128,128]{2,1,0:T(8,128)} %products.7), calls=%async_computation.2 | async-start | bytes 8388608 | tf_op jit(solution)/shard_map/all_to_all | solution.py:393
  343.5 1.9 broadcast_select_fusion.1
  345.4 46.8 %collective-permute-done.29 = f32[32,128,128]{2,1,0:T(8,128)S(1)} collective-permute-done((f32[32,128,128]{2,1,0:T(8,128)}, f32[32,128,128]{2,1,0:T(8,128)S(1)}, u32[]{:S(2)}, u32[]{:S(2)}) %collective-permute-start.29) | collective-permute-done | bytes 2097184 | tf_op jit(solution)/shard_map/ppermute | solution.py:435
  392.4 2.4 pad_maximum_fusion
  394.9 4.6 %all-to-all-start.1 = ((f32[64,128,128]{2,1,0:T(8,128)}), f32[64,128,128]{2,1,0:T(8,128)}, u32[]{:S(2)}, u32[]{:S(2)}) async-start(f32[64,128,128]{2,1,0:T(8,128)} %pad_maximum_fusion), calls=%async_computation.1 | async-start | bytes 8388608 | tf_op jit(solution)/shard_map/all_to_all | solution.py:393
  399.5 9.6 %first_blocks.1.start = f32[128,128,128]{2,1,0:T(8,128)} custom-call(s32[64]{0:T(128)S(1)} %slice_bitcast_fusion.1.targets, f32[64,128,128]{2,1,0:T(8,128)} %all-to-all-done.4.got, f32[128,128,128]{2,1,0:T(8,128)} %bitcast.106), custom_call_target="tpu_custom_call" | custom-call | flops 1048576 | bytes 20971520 | tf_op jit(solution)/shard_map/first_blocks/pallas_call | solution.py:241
  409.2 6.5 %add_blocks.3.start = f32[128,128,128]{2,1,0:T(8,128)} custom-call(s32[64]{0:T(128)S(1)} %slice_bitcast_fusion.3.targets, s32[64]{0:T(128)S(1)} %slice_bitcast_fusion.2.leader, f32[64,128,128]{2,1,0:T(8,128)} %all-to-all-done.3.got, f32[128,128,128]{2,1,0:T(8,128)} %first_blocks.1.start), custom_call_target="tpu_custom_call", output_to_operand_aliasing={{}: (3, {})} | custom-call | flops 1048576 | bytes 12582912 | tf_op jit(solution)/shard_map/add_blocks/pallas_call | solution.py:206
  415.7 6.5 %add_blocks.4.start = f32[128,128,128]{2,1,0:T(8,128)} custom-call(s32[64]{0:T(128)S(1)} %get-tuple-element.588.targets, s32[64]{0:T(128)S(1)} %get-tuple-element.586.leader, f32[64,128,128]{2,1,0:T(8,128)} %all-to-all-done.2.got, f32[128,128,128]{2,1,0:T(8,128)} %add_blocks.3.start), custom_call_target="tpu_custom_call", output_to_operand_aliasing={{}: (3, {})} | custom-call | flops 1048576 | bytes 12582912 | tf_op jit(solution)/shard_map/add_blocks/pallas_call | solution.py:206
  422.2 26.4 %all-to-all-done.1.got = f32[64,128,128]{2,1,0:T(8,128)} async-done(((f32[64,128,128]{2,1,0:T(8,128)}), f32[64,128,128]{2,1,0:T(8,128)}, u32[]{:S(2)}, u32[]{:S(2)}) %all-to-all-start.1) | async-done | bytes 4194336 | tf_op jit(solution)/shard_map/all_to_all | solution.py:393
  448.6 6.5 %add_blocks.5 = f32[128,128,128]{2,1,0:T(8,128)} custom-call(s32[64]{0:T(128)S(1)} %get-tuple-element.589.targets, s32[64]{0:T(128)S(1)} %get-tuple-element.587.leader, f32[64,128,128]{2,1,0:T(8,128)} %all-to-all-done.1.got, f32[128,128,128]{2,1,0:T(8,128)} %add_blocks.4.start), custom_call_target="tpu_custom_call", output_to_operand_aliasing={{}: (3, {})} | custom-call | flops 1048576 | bytes 12582912 | tf_op jit(solution)/shard_map/add_blocks/pallas_call | solution.py:206
  (168 shorter events, 48.5 us)
Async XLA Ops:
  0.0 22.0 %copy-start.19 = (s32[4,16]{1,0:T(4,128)S(1)}, s32[4,16]{1,0:T(4,128)}, u32[]{:S(2)}) copy-start(s32[4,16]{1,0:T(4,128)} %param.18) | copy-start | bytes 772
  3.4 22.8 %copy-start.4 = (f32[1024,256]{1,0:T(8,128)}, f32[1024,256]{1,0:T(8,128)S(1)}, u32[]{:S(2)}) copy-start(f32[1024,256]{1,0:T(8,128)S(1)} %bitcast_multiply_fusion) | copy-start | bytes 3145732
  3.4 15.7 %collective-permute-start.2 = (f32[1,1024,256]{2,1,0:T(8,128)S(1)}, f32[1,1024,256]{2,1,0:T(8,128)S(1)}, u32[]{:S(2)}, u32[]{:S(2)}) collective-permute-start(f32[1,1024,256]{2,1,0:T(8,128)S(1)} %bitcast.99), channel_id=1, source_target_pairs={{1,0},{2,1},{3,2},{4,3},{5,4},{6,5},{7,6},{0,7},{9,8},{10,9},{11,1... | collective-permute-start | bytes 3145736 | tf_op jit(solution)/shard_map/ppermute | solution.py:356
  6.8 30.4 %collective-permute-start = (f32[1024,256]{1,0:T(8,128)S(1)}, f32[1024,256]{1,0:T(8,128)}, u32[]{:S(2)}, u32[]{:S(2)}) collective-permute-start(f32[1024,256]{1,0:T(8,128)S(1)} %bitcast_multiply_fusion), channel_id=1, source_target_pairs={{0,8},{8,16},{16,24},{1,9},{9,17},{17,25},{2,10},{10,18},{18,26},{... | collective-permute-start | bytes 3145736 | tf_op jit(solution)/shard_map/ppermute | solution.py:24
  11.3 28.1 %collective-permute-start.1 = (f32[1024,256]{1,0:T(8,128)S(1)}, f32[1024,256]{1,0:T(8,128)}, u32[]{:S(2)}, u32[]{:S(2)}) collective-permute-start(f32[1024,256]{1,0:T(8,128)S(1)} %bitcast_multiply_fusion), channel_id=1, source_target_pairs={{8,0},{16,8},{24,16},{9,1},{17,9},{25,17},{10,2},{18,10},{26,18},{... | collective-permute-start | bytes 3145736 | tf_op jit(solution)/shard_map/ppermute | solution.py:29
  19.1 15.1 %collective-permute-start.3 = (f32[1,1024,256]{2,1,0:T(8,128)S(1)}, f32[1,1024,256]{2,1,0:T(8,128)}, u32[]{:S(2)}, u32[]{:S(2)}) collective-permute-start(f32[1,1024,256]{2,1,0:T(8,128)S(1)} %collective-permute-done.2.refs_1_), channel_id=1, source_target_pairs={{1,0},{2,1},{3,2},{4,3},{5,4},{6,5},{7,6},{0,7},{9,8},{10,9},{11,1... | collective-permute-start | bytes 3145736 | tf_op jit(solution)/shard_map/ppermute | solution.py:356
  22.1 21.8 %copy-start.25 = (s32[4]{0:T(128)S(1)}, s32[4]{0:T(128)}, u32[]{:S(2)}) copy-start(s32[4]{0:T(128)} %constant.173.clone) | copy-start | bytes 52
  22.2 23.2 %copy-start.24 = (s32[4]{0:T(128)S(1)}, s32[4]{0:T(128)}, u32[]{:S(2)}) copy-start(s32[4]{0:T(128)} %constant.171.clone) | copy-start | bytes 52
  26.2 155.2 %copy-start = (f32[128,2048]{1,0:T(8,128)}, f32[128,2048]{1,0:T(8,128)S(1)}, u32[]{:S(2)}) copy-start(f32[128,2048]{1,0:T(8,128)S(1)} %get-tuple-element.536.refs_6_.refs_8_.refs_10_) | copy-start | bytes 3145732
  26.2 27.8 %collective-permute-start.5 = (f32[128,2048]{1,0:T(8,128)}, f32[128,2048]{1,0:T(8,128)}, u32[]{:S(2)}, u32[]{:S(2)}) collective-permute-start(f32[128,2048]{1,0:T(8,128)} %get-tuple-element.535.refs_20_.refs_16_), channel_id=1, source_target_pairs={{0,8},{8,16},{16,24},{1,9},{9,17},{17,25},{2,10},{10,18},{18,26},{... | collective-permute-start | bytes 3145736 | tf_op jit(solution)/shard_map/ppermute | solution.py:24
  30.7 31.1 %collective-permute-start.6 = (f32[128,2048]{1,0:T(8,128)S(1)}, f32[128,2048]{1,0:T(8,128)}, u32[]{:S(2)}, u32[]{:S(2)}) collective-permute-start(f32[128,2048]{1,0:T(8,128)S(1)} %get-tuple-element.536.refs_6_.refs_8_.refs_10_), channel_id=1, source_target_pairs={{8,0},{16,8},{24,16},{9,1},{17,9},{25,17},{10,2},{18,10},{26,18},{... | collective-permute-start | bytes 3145736 | tf_op jit(solution)/shard_map/ppermute | solution.py:29
  34.3 27.6 %collective-permute-start.4 = (f32[1,1024,256]{2,1,0:T(8,128)}, f32[1,1024,256]{2,1,0:T(8,128)S(1)}, u32[]{:S(2)}, u32[]{:S(2)}) collective-permute-start(f32[1,1024,256]{2,1,0:T(8,128)} %collective-permute-done.3.refs_2_), channel_id=1, source_target_pairs={{1,0},{2,1},{3,2},{4,3},{5,4},{6,5},{7,6},{0,7},{9,8},{10,9},{11,1... | collective-permute-start | bytes 3145736 | tf_op jit(solution)/shard_map/ppermute | solution.py:356
  40.0 26.6 %collective-permute-start.7 = (f32[1024,256]{1,0:T(8,128)}, f32[1024,256]{1,0:T(8,128)S(1)}, u32[]{:S(2)}, u32[]{:S(2)}) collective-permute-start(f32[1024,256]{1,0:T(8,128)} %collective-permute-done), channel_id=1, source_target_pairs={{8,16},{16,24},{9,17},{17,25},{10,18},{18,26},{11,19},{19,27},{12,... | collective-permute-start | bytes 3145736 | tf_op jit(solution)/shard_map/ppermute | solution.py:24
  40.7 43.6 %collective-permute-start.8 = (f32[1024,256]{1,0:T(8,128)}, f32[1024,256]{1,0:T(8,128)}, u32[]{:S(2)}, u32[]{:S(2)}) collective-permute-start(f32[1024,256]{1,0:T(8,128)} %collective-permute-done.1), channel_id=1, source_target_pairs={{8,0},{16,8},{9,1},{17,9},{10,2},{18,10},{11,3},{19,11},{12,4},{20... | collective-permute-start | bytes 3145736 | tf_op jit(solution)/shard_map/ppermute | solution.py:29
  61.9 24.6 %copy-start.11 = (f32[1,1024,256]{2,1,0:T(8,128)}, f32[1,1024,256]{2,1,0:T(8,128)S(1)}, u32[]{:S(2)}) copy-start(f32[1,1024,256]{2,1,0:T(8,128)S(1)} %collective-permute-done.4.refs_3_) | copy-start | bytes 3145732
  61.9 62.8 %collective-permute-start.9 = (f32[128,2048]{1,0:T(8,128)}, f32[128,2048]{1,0:T(8,128)}, u32[]{:S(2)}, u32[]{:S(2)}) collective-permute-start(f32[128,2048]{1,0:T(8,128)} %get-tuple-element.537.refs_21_.refs_17_), channel_id=1, source_target_pairs={{0,8},{8,16},{16,24},{1,9},{9,17},{17,25},{2,10},{10,18},{18,26},{... | collective-permute-start | bytes 3145736 | tf_op jit(solution)/shard_map/ppermute | solution.py:24
  65.3 59.3 %collective-permute-start.10 = (f32[128,2048]{1,0:T(8,128)}, f32[128,2048]{1,0:T(8,128)}, u32[]{:S(2)}, u32[]{:S(2)}) collective-permute-start(f32[128,2048]{1,0:T(8,128)} %get-tuple-element.538.refs_7_.refs_9_.refs_11_), channel_id=1, source_target_pairs={{8,0},{16,8},{24,16},{9,1},{17,9},{25,17},{10,2},{18,10},{26,18},{... | collective-permute-start | bytes 3145736 | tf_op jit(solution)/shard_map/ppermute | solution.py:29
  88.3 44.2 %collective-permute-start.21 = (f32[3,1024,256]{2,1,0:T(8,128)}, f32[3,1024,256]{2,1,0:T(8,128)}, u32[]{:S(2)}, u32[]{:S(2)}) collective-permute-start(f32[3,1024,256]{2,1,0:T(8,128)} %pad_maximum_fusion.1.refs_0_), channel_id=1, source_target_pairs={{1,0},{2,1},{3,2},{4,3},{5,4},{6,5},{7,6},{0,7},{9,8},{10,9},{11,1... | collective-permute-start | bytes 9437192 | tf_op jit(solution)/shard_map/ppermute | solution.py:356
  89.3 35.4 %all-to-all-start = ((s32[32,2,128]{2,1,0:T(2,128)}), s32[32,2,128]{2,1,0:T(2,128)S(1)}, u32[]{:S(2)}, u32[]{:S(2)}) async-start(s32[32,2,128]{2,1,0:T(2,128)} %broadcast_in_dim.133), calls=%async_computation | async-start | bytes 65536 | tf_op jit(solution)/shard_map/all_to_all | solution.py:423
  91.9 47.6 %collective-permute-start.11 = (f32[128,2048]{1,0:T(8,128)}, f32[128,2048]{1,0:T(8,128)S(1)}, u32[]{:S(2)}, u32[]{:S(2)}) collective-permute-start(f32[128,2048]{1,0:T(8,128)} %collective-permute-done.5.refs_16_.refs_18_.refs_14_), channel_id=1, source_target_pairs={{8,16},{16,24},{9,17},{17,25},{10,18},{18,26},{11,19},{19,27},{12,... | collective-permute-start | bytes 3145736 | tf_op jit(solution)/shard_map/ppermute | solution.py:24
  92.6 46.9 %collective-permute-start.12 = (f32[128,2048]{1,0:T(8,128)}, f32[128,2048]{1,0:T(8,128)}, u32[]{:S(2)}, u32[]{:S(2)}) collective-permute-start(f32[128,2048]{1,0:T(8,128)} %collective-permute-done.6.refs_8_.refs_10_.refs_12_), channel_id=1, source_target_pairs={{8,0},{16,8},{9,1},{17,9},{10,2},{18,10},{11,3},{19,11},{12,4},{20... | collective-permute-start | bytes 3145736 | tf_op jit(solution)/shard_map/ppermute | solution.py:29
  128.7 17.7 %collective-permute-start.13 = (f32[128,2048]{1,0:T(8,128)}, f32[128,2048]{1,0:T(8,128)}, u32[]{:S(2)}, u32[]{:S(2)}) collective-permute-start(f32[128,2048]{1,0:T(8,128)} %collective-permute-done.9.refs_17_.refs_19_.refs_15_), channel_id=1, source_target_pairs={{8,16},{16,24},{9,17},{17,25},{10,18},{18,26},{11,19},{19,27},{12,... | collective-permute-start | bytes 3145736 | tf_op jit(solution)/shard_map/ppermute | solution.py:24
  130.4 28.3 %collective-permute-start.14 = (f32[128,2048]{1,0:T(8,128)}, f32[128,2048]{1,0:T(8,128)}, u32[]{:S(2)}, u32[]{:S(2)}) collective-permute-start(f32[128,2048]{1,0:T(8,128)} %collective-permute-done.10.refs_9_.refs_11_.refs_13_), channel_id=1, source_target_pairs={{8,0},{16,8},{9,1},{17,9},{10,2},{18,10},{11,3},{19,11},{12,4},{20... | collective-permute-start | bytes 3145736 | tf_op jit(solution)/shard_map/ppermute | solution.py:29
  132.5 48.5 %collective-permute-start.22 = (f32[3,1024,256]{2,1,0:T(8,128)}, f32[3,1024,256]{2,1,0:T(8,128)}, u32[]{:S(2)}, u32[]{:S(2)}) collective-permute-start(f32[3,1024,256]{2,1,0:T(8,128)} %collective-permute-done.21.refs_1_), channel_id=1, source_target_pairs={{1,0},{2,1},{3,2},{4,3},{5,4},{6,5},{7,6},{0,7},{9,8},{10,9},{11,1... | collective-permute-start | bytes 9437192 | tf_op jit(solution)/shard_map/ppermute | solution.py:356
  140.6 62.9 %copy-start.15 = (f32[128,2048]{1,0:T(8,128)S(1)}, f32[128,2048]{1,0:T(8,128)}, u32[]{:S(2)}) copy-start(f32[128,2048]{1,0:T(8,128)} %get-tuple-element.538.refs_7_.refs_9_.refs_11_) | copy-start | bytes 3145732
  140.6 28.0 %collective-permute-start.15 = (f32[128,2048]{1,0:T(8,128)S(1)}, f32[128,2048]{1,0:T(8,128)S(1)}, u32[]{:S(2)}, u32[]{:S(2)}) collective-permute-start(f32[128,2048]{1,0:T(8,128)S(1)} %broadcast_select_fusion.7), channel_id=1, source_target_pairs={{0,8},{8,16},{16,24},{1,9},{9,17},{17,25},{2,10},{10,18},{18,26},{... | collective-permute-start | bytes 3145736 | tf_op jit(solution)/shard_map/ppermute | solution.py:342
  145.1 35.9 %collective-permute-start.16 = (f32[128,2048]{1,0:T(8,128)}, f32[128,2048]{1,0:T(8,128)S(1)}, u32[]{:S(2)}, u32[]{:S(2)}) collective-permute-start(f32[128,2048]{1,0:T(8,128)} %collective-permute-done.12.refs_10_.refs_12_.refs_14_), channel_id=1, source_target_pairs={{8,0},{9,1},{10,2},{11,3},{12,4},{13,5},{14,6},{15,7}} | collective-permute-start | bytes 3145736 | tf_op jit(solution)/shard_map/ppermute | solution.py:29
  160.0 31.1 %collective-permute-start.17 = (f32[128,2048]{1,0:T(8,128)S(1)}, f32[128,2048]{1,0:T(8,128)S(1)}, u32[]{:S(2)}, u32[]{:S(2)}) collective-permute-start(f32[128,2048]{1,0:T(8,128)S(1)} %broadcast_select_fusion.6), channel_id=1, source_target_pairs={{0,8},{8,16},{16,24},{1,9},{9,17},{17,25},{2,10},{10,18},{18,26},{... | collective-permute-start | bytes 3145736 | tf_op jit(solution)/shard_map/ppermute | solution.py:342
  162.0 41.5 %collective-permute-start.18 = (f32[128,2048]{1,0:T(8,128)}, f32[128,2048]{1,0:T(8,128)S(1)}, u32[]{:S(2)}, u32[]{:S(2)}) collective-permute-start(f32[128,2048]{1,0:T(8,128)} %collective-permute-done.14.refs_11_.refs_13_.refs_15_), channel_id=1, source_target_pairs={{8,0},{9,1},{10,2},{11,3},{12,4},{13,5},{14,6},{15,7}} | collective-permute-start | bytes 3145736 | tf_op jit(solution)/shard_map/ppermute | solution.py:29
  165.4 43.2 %copy-start.5 = (f32[1024,256]{1,0:T(8,128)S(1)}, f32[1024,256]{1,0:T(8,128)}, u32[]{:S(2)}) copy-start(f32[1024,256]{1,0:T(8,128)} %copy-done.4) | copy-start | bytes 3145732
  165.4 43.2 %copy-start.10 = (f32[1,1024,256]{2,1,0:T(8,128)S(1)}, f32[1,1024,256]{2,1,0:T(8,128)}, u32[]{:S(2)}) copy-start(f32[1,1024,256]{2,1,0:T(8,128)} %copy-done.9) | copy-start | bytes 3145732
  165.4 43.2 %copy-start.12 = (f32[1,1024,256]{2,1,0:T(8,128)S(1)}, f32[1,1024,256]{2,1,0:T(8,128)}, u32[]{:S(2)}) copy-start(f32[1,1024,256]{2,1,0:T(8,128)} %copy-done.11) | copy-start | bytes 3145732
  181.0 23.7 %copy-start.22 = (f32[128,2048]{1,0:T(8,128)}, f32[128,2048]{1,0:T(8,128)S(1)}, u32[]{:S(2)}) copy-start(f32[128,2048]{1,0:T(8,128)S(1)} %collective-permute-done.16.refs_12_.refs_14_.refs_16_) | copy-start | bytes 3145732
  181.0 66.3 %collective-permute-start.23 = (f32[3,1024,256]{2,1,0:T(8,128)}, f32[3,1024,256]{2,1,0:T(8,128)}, u32[]{:S(2)}, u32[]{:S(2)}) collective-permute-start(f32[3,1024,256]{2,1,0:T(8,128)} %collective-permute-done.22.refs_2_), channel_id=1, source_target_pairs={{1,0},{2,1},{3,2},{4,3},{5,4},{6,5},{7,6},{0,7},{9,8},{10,9},{11,1... | collective-permute-start | bytes 9437192 | tf_op jit(solution)/shard_map/ppermute | solution.py:356
  181.6 39.4 %collective-permute-start.19 = (f32[128,2048]{1,0:T(8,128)S(1)}, f32[128,2048]{1,0:T(8,128)S(1)}, u32[]{:S(2)}, u32[]{:S(2)}) collective-permute-start(f32[128,2048]{1,0:T(8,128)S(1)} %broadcast_select_fusion.5), channel_id=1, source_target_pairs={{0,8},{8,16},{16,24},{1,9},{9,17},{17,25},{2,10},{10,18},{18,26},{... | collective-permute-start | bytes 3145736 | tf_op jit(solution)/shard_map/ppermute | solution.py:342
  183.2 42.8 %collective-permute-start.20 = (f32[128,2048]{1,0:T(8,128)}, f32[128,2048]{1,0:T(8,128)}, u32[]{:S(2)}, u32[]{:S(2)}) collective-permute-start(f32[128,2048]{1,0:T(8,128)} %get-tuple-element.535.refs_20_.refs_16_), channel_id=1, source_target_pairs={{8,0},{16,8},{9,1},{17,9},{10,2},{18,10},{11,3},{19,11},{12,4},{20... | collective-permute-start | bytes 3145736 | tf_op jit(solution)/shard_map/ppermute | solution.py:29
  204.7 29.0 %collective-permute-start.24 = (f32[128,2048]{1,0:T(8,128)}, f32[128,2048]{1,0:T(8,128)}, u32[]{:S(2)}, u32[]{:S(2)}) collective-permute-start(f32[128,2048]{1,0:T(8,128)} %broadcast_select_fusion.4), channel_id=1, source_target_pairs={{0,8},{8,16},{16,24},{1,9},{9,17},{17,25},{2,10},{10,18},{18,26},{... | collective-permute-start | bytes 3145736 | tf_op jit(solution)/shard_map/ppermute | solution.py:342
  207.3 40.0 %collective-permute-start.25 = (f32[128,2048]{1,0:T(8,128)}, f32[128,2048]{1,0:T(8,128)}, u32[]{:S(2)}, u32[]{:S(2)}) collective-permute-start(f32[128,2048]{1,0:T(8,128)} %get-tuple-element.537.refs_21_.refs_17_), channel_id=1, source_target_pairs={{8,0},{16,8},{9,1},{17,9},{10,2},{18,10},{11,3},{19,11},{12,4},{20... | collective-permute-start | bytes 3145736 | tf_op jit(solution)/shard_map/ppermute | solution.py:29
  227.2 46.3 %collective-permute-start.26 = (f32[128,2048]{1,0:T(8,128)S(1)}, f32[128,2048]{1,0:T(8,128)}, u32[]{:S(2)}, u32[]{:S(2)}) collective-permute-start(f32[128,2048]{1,0:T(8,128)S(1)} %broadcast_select_fusion.3), channel_id=1, source_target_pairs={{16,24},{17,25},{18,26},{19,27},{20,28},{21,29},{22,30},{23,31}} | collective-permute-start | bytes 3145736 | tf_op jit(solution)/shard_map/ppermute | solution.py:342
  229.0 53.7 %all-to-all-start.4 = ((f32[64,128,128]{2,1,0:T(8,128)}), f32[64,128,128]{2,1,0:T(8,128)}, u32[]{:S(2)}, u32[]{:S(2)}) async-start(f32[64,128,128]{2,1,0:T(8,128)} %products.4), calls=%async_computation.4 | async-start | bytes 8388608 | tf_op jit(solution)/shard_map/all_to_all | solution.py:393
  249.3 24.3 %collective-permute-start.27 = (f32[128,2048]{1,0:T(8,128)S(1)}, f32[128,2048]{1,0:T(8,128)S(1)}, u32[]{:S(2)}, u32[]{:S(2)}) collective-permute-start(f32[128,2048]{1,0:T(8,128)S(1)} %broadcast_select_fusion.2), channel_id=1, source_target_pairs={{16,24},{17,25},{18,26},{19,27},{20,28},{21,29},{22,30},{23,31}} | collective-permute-start | bytes 3145736 | tf_op jit(solution)/shard_map/ppermute | solution.py:342
  282.6 54.8 %all-to-all-start.3 = ((f32[64,128,128]{2,1,0:T(8,128)}), f32[64,128,128]{2,1,0:T(8,128)}, u32[]{:S(2)}, u32[]{:S(2)}) async-start(f32[64,128,128]{2,1,0:T(8,128)} %products.5), calls=%async_computation.3 | async-start | bytes 8388608 | tf_op jit(solution)/shard_map/all_to_all | solution.py:393
  287.3 50.1 %collective-permute-start.28 = (f32[32,128,128]{2,1,0:T(8,128)}, f32[32,128,128]{2,1,0:T(8,128)}, u32[]{:S(2)}, u32[]{:S(2)}) collective-permute-start(f32[32,128,128]{2,1,0:T(8,128)} %get-tuple-element.533), channel_id=1, source_target_pairs={{8,0},{16,24},{9,1},{17,25},{10,2},{18,26},{11,3},{19,27},{12,4},{... | collective-permute-start | bytes 6291464 | tf_op jit(solution)/shard_map/ppermute | solution.py:408
  303.8 39.7 %copy-start.17 = (f32[32,128,128]{2,1,0:T(8,128)S(1)}, f32[32,128,128]{2,1,0:T(8,128)}, u32[]{:S(2)}) copy-start(f32[32,128,128]{2,1,0:T(8,128)} %get-tuple-element.571) | copy-start | bytes 6291460
  337.4 57.5 %all-to-all-start.2 = ((f32[64,128,128]{2,1,0:T(8,128)}), f32[64,128,128]{2,1,0:T(8,128)}, u32[]{:S(2)}, u32[]{:S(2)}) async-start(f32[64,128,128]{2,1,0:T(8,128)} %products.7), calls=%async_computation.2 | async-start | bytes 8388608 | tf_op jit(solution)/shard_map/all_to_all | solution.py:393
  342.0 50.1 %copy-start.16 = (f32[32,128,128]{2,1,0:T(8,128)S(1)}, f32[32,128,128]{2,1,0:T(8,128)}, u32[]{:S(2)}) copy-start(f32[32,128,128]{2,1,0:T(8,128)} %get-tuple-element.573) | copy-start | bytes 6291460
  342.1 50.1 %collective-permute-start.29 = (f32[32,128,128]{2,1,0:T(8,128)}, f32[32,128,128]{2,1,0:T(8,128)S(1)}, u32[]{:S(2)}, u32[]{:S(2)}) collective-permute-start(f32[32,128,128]{2,1,0:T(8,128)} %get-tuple-element.572), channel_id=1, source_target_pairs={{8,0},{16,24},{9,1},{17,25},{10,2},{18,26},{11,3},{19,27},{12,4},{... | collective-permute-start | bytes 6291464 | tf_op jit(solution)/shard_map/ppermute | solution.py:435
  394.9 53.7 %all-to-all-start.1 = ((f32[64,128,128]{2,1,0:T(8,128)}), f32[64,128,128]{2,1,0:T(8,128)}, u32[]{:S(2)}, u32[]{:S(2)}) async-start(f32[64,128,128]{2,1,0:T(8,128)} %pad_maximum_fusion), calls=%async_computation.1 | async-start | bytes 8388608 | tf_op jit(solution)/shard_map/all_to_all | solution.py:393
  (14 other events, 159.6 us)
